TPU v7x, 32 devices: a whole 2x2x4 slice. The times are simulated.
32 devices in a mesh: grp: 16 (over z, y, x), rep: 2 (over core).
Axes of the slice: x: 2, y: 2, z: 4, core: 2. Of those that a mesh axis runs over, the one named last changes fastest.
Arguments:
- layer_input: bfloat16 [2, 2, 1024, 2048], P('rep', None, 'grp'), may hold values from -6 to 6
- out_grad: bfloat16 [2, 2, 1024, 2048], P('rep', None, 'grp'), may hold values from -6 to 6
- routes: int32 [2, 2, 1024, 8], P('rep', None, 'grp'), may hold values from 0 to 15, all different within a row; in each aligned block of 64 rows (0 to 63, 64 to 127, ..., all dimensions but the last counted through in order) at most 36 rows name the same one
- norm_in: bfloat16 [2048], P('grp'), may hold values from 0.5 to 1.5
- query_weight: bfloat16 [2048, 4096], P('grp'), may hold values from -0.125 to 0.125
- key_weight: bfloat16 [2048, 512], P('grp'), may hold values from -0.125 to 0.125
- value_weight: bfloat16 [2048, 512], P('grp'), may hold values from -0.125 to 0.125
- query_gain: bfloat16 [128], P('grp'), may hold values from 0.5 to 1.5
- key_gain: bfloat16 [128], P('grp'), may hold values from 0.5 to 1.5
- out_weight: bfloat16 [4096, 2048], P('grp'), may hold values from -0.75 to 0.75
- norm_mid: bfloat16 [2048], P('grp'), may hold values from 0.5 to 1.5
- router: bfloat16 [2048, 16], P('grp'), may hold values from -0.25 to 0.25
- expert_gate: bfloat16 [16, 2048, 768], P('grp'), may hold values from -0.125 to 0.125
- expert_up: bfloat16 [16, 2048, 768], P('grp'), may hold values from -0.125 to 0.125
- expert_down: bfloat16 [16, 768, 2048], P('grp'), may hold values from -0.21875 to 0.21875
Outputs:
- layer_out: bfloat16 [2, 2, 1024, 2048], P('rep', None, 'grp')
- input_grad: float32 [2, 2, 1024, 2048], P('rep', None, 'grp')
- norm_in_grad: float32 [2048], P('grp')
- query_weight_grad: float32 [2048, 4096], P('grp')
- key_weight_grad: float32 [2048, 512], P('grp')
- value_weight_grad: float32 [2048, 512], P('grp')
- query_gain_grad: float32 [128], P('grp')
- key_gain_grad: float32 [128], P('grp')
- out_weight_grad: float32 [4096, 2048], P('grp')
- norm_mid_grad: float32 [2048], P('grp')
- router_grad: float32 [2048, 16], P('grp')
- expert_gate_grad: float32 [16, 2048, 768], P('grp')
- expert_up_grad: float32 [16, 2048, 768], P('grp')
- expert_down_grad: float32 [16, 768, 2048], P('grp')
Inputs may be any that keep to these rules, and one draw needn't show every extreme that they name: `routes`: each row names 8 different experts; in each aligned block of 64 rows (the rows of one device in one micro-batch) no expert is named more than 36 times.
All inputs are finite; a program needn't handle non-finite values.
Results may differ from a plain program's by a relative error of at most 0.022.
Values may be sent and summed in bfloat16 or wider, within the bound.
No kernel may reach another device: no remote copies, remote signals or barrier semaphores. Data moves between devices by JAX's collectives and lax.ppermute only.
A program may use at most 384 MiB of HBM per device.

v0:
```python
import math

import jax
import jax.numpy as jnp
from jax import lax
from jax.sharding import PartitionSpec as P

SEQ_MIN = 1024
BLOCK = 256


EPS = 1e-06
THETA = 1000000.0
NEGATIVE = -1e30


def row_scale(values):
    return lax.rsqrt(jnp.mean(values * values, axis=-1, keepdims=True) + EPS)


def norm_back(grad, values, factor, gain):
    inner = grad * gain
    back = factor * inner - values * factor**3 * jnp.mean(inner * values, axis=-1, keepdims=True)
    return (back, grad * values * factor)


def rotate(values, cosine, sine):
    half_size = values.shape[-1] // 2
    first = values[..., :half_size]
    second = values[..., half_size:]
    return jnp.concatenate(
        [first * cosine - second * sine, second * cosine + first * sine], axis=-1
    )


def unrotate(grad, cosine, sine):
    half_size = grad.shape[-1] // 2
    first = grad[..., :half_size]
    second = grad[..., half_size:]
    return jnp.concatenate(
        [first * cosine + second * sine, second * cosine - first * sine], axis=-1
    )


def contract_out(left, right):
    return lax.dot_general(
        left, right, (((1,), (1,)), ((), ())), preferred_element_type=jnp.float32
    )


def contract_rows(left, right):
    return lax.dot_general(
        left, right, (((0,), (0,)), ((), ())), preferred_element_type=jnp.float32
    )


def per_device(
    layer_input,
    out_grad,
    routes,
    norm_in,
    query_weight,
    key_weight,
    value_weight,
    query_gain,
    key_gain,
    out_weight,
    norm_mid,
    router,
    expert_gate,
    expert_up,
    expert_down,
):
    groups = lax.axis_size("grp")
    my_index = lax.axis_index("grp")
    batches = layer_input.shape[1]
    tokens = layer_input.shape[2]
    model_width = layer_input.shape[3]
    top_count = routes.shape[3]
    local_count = expert_gate.shape[0]
    experts = groups * local_count
    capacity = min(tokens, 9 * tokens * top_count // (8 * experts))
    head_size = query_gain.shape[0] * groups
    key_width = key_weight.shape[1]
    query_width = query_weight.shape[1]
    kv_heads = key_width // head_size
    per_kv = query_width // key_width
    factor = 1.0 / math.sqrt(head_size)
    seq_length = max(SEQ_MIN, tokens * groups)
    row_ids = my_index * tokens + jnp.arange(tokens, dtype=jnp.int32)
    query_seq = row_ids // seq_length
    query_pos = row_ids % seq_length
    query_blk = query_pos // BLOCK
    key_ids = jnp.arange(tokens * groups, dtype=jnp.int32)
    visible = ((key_ids // seq_length)[None, :] == query_seq[:, None]) & (
        (key_ids % seq_length // BLOCK)[None, :] <= query_blk[:, None]
    )
    half_size = head_size // 2
    inverse = THETA ** (-(jnp.arange(half_size, dtype=jnp.float32) * 2.0 / head_size))
    angle = query_pos.astype(jnp.float32)[:, None] * inverse[None, :]
    cosine = jnp.cos(angle)
    sine = jnp.sin(angle)
    cos_query = cosine[:, None, None, :]
    sin_query = sine[:, None, None, :]
    cos_key = cosine[:, None, :]
    sin_key = sine[:, None, :]
    expert_ids = jnp.arange(experts, dtype=jnp.int32)
    held = None
    held = (
        lax.all_gather(norm_in, "grp", axis=0, tiled=True),
        lax.all_gather(query_weight, "grp", axis=0, tiled=True),
        lax.all_gather(key_weight, "grp", axis=0, tiled=True),
        lax.all_gather(value_weight, "grp", axis=0, tiled=True),
        lax.all_gather(query_gain, "grp", axis=0, tiled=True),
        lax.all_gather(key_gain, "grp", axis=0, tiled=True),
        lax.all_gather(out_weight, "grp", axis=0, tiled=True),
        lax.all_gather(norm_mid, "grp", axis=0, tiled=True),
        lax.all_gather(router, "grp", axis=0, tiled=True),
    )
    shard_total = None
    full_total = None
    gate_total = jnp.zeros(expert_gate.shape, jnp.float32)
    up_total = jnp.zeros(expert_up.shape, jnp.float32)
    down_total = jnp.zeros(expert_down.shape, jnp.float32)
    out_list = []
    grad_list = []
    for batch_index in range(batches):
        weights_now = held
        gain_in = weights_now[0].astype(jnp.float32)
        query_g = weights_now[4].astype(jnp.float32)
        key_g = weights_now[5].astype(jnp.float32)
        gain_mid = weights_now[7].astype(jnp.float32)
        inputs = layer_input[0, batch_index].astype(jnp.float32)
        scale_in = row_scale(inputs)
        low_in = (inputs * scale_in * gain_in).astype(jnp.bfloat16)
        query_pre = jnp.dot(low_in, weights_now[1], preferred_element_type=jnp.float32).reshape(
            tokens, kv_heads, per_kv, head_size
        )
        key_pre = jnp.dot(low_in, weights_now[2], preferred_element_type=jnp.float32).reshape(
            tokens, kv_heads, head_size
        )
        value_low = jnp.dot(low_in, weights_now[3], preferred_element_type=jnp.float32).astype(
            jnp.bfloat16
        )
        query_scale = row_scale(query_pre)
        key_scale = row_scale(key_pre)
        query_rot = rotate(query_pre * query_scale * query_g, cos_query, sin_query).astype(
            jnp.bfloat16
        )
        key_rot = rotate(key_pre * key_scale * key_g, cos_key, sin_key).astype(jnp.bfloat16)
        own_keys = key_rot.reshape(tokens, key_width)
        gathered = (
            lax.all_gather(own_keys, "grp", axis=0, tiled=True),
            lax.all_gather(value_low, "grp", axis=0, tiled=True),
        )
        keys_all = gathered[0].reshape(-1, kv_heads, head_size)
        values_all = gathered[1].reshape(-1, kv_heads, head_size)
        scores = (
            jnp.einsum("qkgd,nkd->kgqn", query_rot, keys_all, preferred_element_type=jnp.float32)
            * factor
        )
        scores = jnp.where(visible, scores, NEGATIVE)
        peak = jnp.max(scores, axis=-1, keepdims=True)
        expo = jnp.exp(scores - peak)
        total = jnp.sum(expo, axis=-1, keepdims=True)
        log_total = peak + jnp.log(total)
        probs_low = (expo / total).astype(jnp.bfloat16)
        att_low = (
            jnp.einsum("kgqn,nkd->qkgd", probs_low, values_all, preferred_element_type=jnp.float32)
            .reshape(tokens, query_width)
            .astype(jnp.bfloat16)
        )
        mid = inputs + jnp.dot(att_low, weights_now[6], preferred_element_type=jnp.float32)
        scale_mid = row_scale(mid)
        low_mid = (mid * scale_mid * gain_mid).astype(jnp.bfloat16)
        logits = jnp.dot(low_mid, weights_now[8], preferred_element_type=jnp.float32)
        chosen = routes[0, batch_index]
        picks = (chosen[:, :, None] == expert_ids[None, None, :]).astype(jnp.float32)
        gates = jax.nn.softmax(jnp.sum(picks * logits[:, None, :], axis=-1), axis=-1)
        flat_routes = chosen.reshape(-1)
        marks = (flat_routes[:, None] == expert_ids[None, :]).astype(jnp.int32)
        slots = jnp.sum((jnp.cumsum(marks, axis=0) - marks) * marks, axis=1)
        target = flat_routes * capacity + slots
        entries = tokens * top_count
        source = (
            jnp.full((experts * capacity,), entries, jnp.int32)
            .at[target]
            .set(jnp.arange(entries, dtype=jnp.int32))
        )
        padded_in = jnp.concatenate([low_mid, jnp.zeros((1, model_width), jnp.bfloat16)], axis=0)
        sent = padded_in[source // top_count].reshape(groups, local_count * capacity, model_width)
        arrived = lax.all_to_all(sent, "grp", split_axis=0, concat_axis=0, tiled=True).reshape(
            groups, local_count, capacity, model_width
        )
        gate_pre = jnp.einsum(
            "sjcd,jdf->sjcf", arrived, expert_gate, preferred_element_type=jnp.float32
        )
        up_pre = jnp.einsum(
            "sjcd,jdf->sjcf", arrived, expert_up, preferred_element_type=jnp.float32
        )
        sigmoid_gate = jax.nn.sigmoid(gate_pre)
        silu_gate = gate_pre * sigmoid_gate
        hidden = (silu_gate * up_pre).astype(jnp.bfloat16)
        produced = jnp.einsum(
            "sjcf,jfd->sjcd", hidden, expert_down, preferred_element_type=jnp.float32
        ).astype(jnp.bfloat16)
        returned = lax.all_to_all(
            produced.reshape(groups, local_count * capacity, model_width),
            "grp",
            split_axis=0,
            concat_axis=0,
            tiled=True,
        ).reshape(experts * capacity, model_width)
        slot_out = returned[target].reshape(tokens, top_count, model_width).astype(jnp.float32)
        out_list.append((mid + jnp.sum(gates[:, :, None] * slot_out, axis=1)).astype(jnp.bfloat16))
        weights_now = held
        grad_out = out_grad[0, batch_index].astype(jnp.float32)
        gate_grad = jnp.sum(slot_out * grad_out[:, None, :], axis=-1)
        slot_grad = (
            (gates[:, :, None] * grad_out[:, None, :])
            .astype(jnp.bfloat16)
            .reshape(entries, model_width)
        )
        padded_grad = jnp.concatenate(
            [slot_grad, jnp.zeros((1, model_width), jnp.bfloat16)], axis=0
        )
        grad_sent = padded_grad[source].reshape(groups, local_count * capacity, model_width)
        grad_arrived = lax.all_to_all(
            grad_sent, "grp", split_axis=0, concat_axis=0, tiled=True
        ).reshape(groups, local_count, capacity, model_width)
        down_total = down_total + jnp.einsum(
            "sjcf,sjcd->jfd", hidden, grad_arrived, preferred_element_type=jnp.float32
        )
        hidden_grad = jnp.einsum(
            "sjcd,jfd->sjcf", grad_arrived, expert_down, preferred_element_type=jnp.float32
        )
        gate_low = (
            hidden_grad * up_pre * sigmoid_gate * (1.0 + gate_pre * (1.0 - sigmoid_gate))
        ).astype(jnp.bfloat16)
        up_low = (hidden_grad * silu_gate).astype(jnp.bfloat16)
        gate_total = gate_total + jnp.einsum(
            "sjcd,sjcf->jdf", arrived, gate_low, preferred_element_type=jnp.float32
        )
        up_total = up_total + jnp.einsum(
            "sjcd,sjcf->jdf", arrived, up_low, preferred_element_type=jnp.float32
        )
        back_rows = jnp.einsum(
            "sjcf,jdf->sjcd", gate_low, expert_gate, preferred_element_type=jnp.float32
        ) + jnp.einsum("sjcf,jdf->sjcd", up_low, expert_up, preferred_element_type=jnp.float32)
        came_back = lax.all_to_all(
            back_rows.astype(jnp.bfloat16).reshape(groups, local_count * capacity, model_width),
            "grp",
            split_axis=0,
            concat_axis=0,
            tiled=True,
        ).reshape(experts * capacity, model_width)
        expert_part = jnp.sum(
            came_back[target].reshape(tokens, top_count, model_width).astype(jnp.float32), axis=1
        )
        pick_grad = gates * (gate_grad - jnp.sum(gates * gate_grad, axis=-1, keepdims=True))
        logit_low = jnp.sum(picks * pick_grad[:, :, None], axis=1).astype(jnp.bfloat16)
        router_grad = contract_rows(low_mid, logit_low)
        normed_mid_grad = expert_part + contract_out(logit_low, weights_now[8])
        mid_back, mid_gain_part = norm_back(normed_mid_grad, mid, scale_mid, gain_mid)
        mid_grad = mid_back + grad_out
        branch_low = mid_grad.astype(jnp.bfloat16)
        out_w_grad = contract_rows(att_low, branch_low)
        att_grad = (
            contract_out(branch_low, weights_now[6])
            .astype(jnp.bfloat16)
            .reshape(tokens, kv_heads, per_kv, head_size)
        )
        scores = (
            jnp.einsum("qkgd,nkd->kgqn", query_rot, keys_all, preferred_element_type=jnp.float32)
            * factor
        )
        probs = jnp.where(visible, jnp.exp(scores - log_total), 0.0)
        prob_grad = jnp.einsum(
            "qkgd,nkd->kgqn", att_grad, values_all, preferred_element_type=jnp.float32
        )
        score_low = (
            probs * (prob_grad - jnp.sum(probs * prob_grad, axis=-1, keepdims=True))
        ).astype(jnp.bfloat16)
        query_grad = (
            jnp.einsum("kgqn,nkd->qkgd", score_low, keys_all, preferred_element_type=jnp.float32)
            * factor
        )
        key_flat = (
            jnp.einsum("kgqn,qkgd->nkd", score_low, query_rot, preferred_element_type=jnp.float32)
            * factor
        ).reshape(-1, key_width)
        value_flat = jnp.einsum(
            "kgqn,qkgd->nkd", probs_low, att_grad, preferred_element_type=jnp.float32
        ).reshape(-1, key_width)
        owned = (
            lax.psum_scatter(
                key_flat.astype(jnp.bfloat16), "grp", scatter_dimension=0, tiled=True
            ).astype(jnp.float32),
            lax.psum_scatter(
                value_flat.astype(jnp.bfloat16), "grp", scatter_dimension=0, tiled=True
            ).astype(jnp.float32),
        )
        key_sum = owned[0]
        value_sum = owned[1]
        key_back, key_gain_part = norm_back(
            unrotate(key_sum.reshape(tokens, kv_heads, head_size), cos_key, sin_key),
            key_pre,
            key_scale,
            key_g,
        )
        query_back, query_gain_part = norm_back(
            unrotate(query_grad, cos_query, sin_query), query_pre, query_scale, query_g
        )
        query_low = query_back.reshape(tokens, query_width).astype(jnp.bfloat16)
        key_low = key_back.reshape(tokens, key_width).astype(jnp.bfloat16)
        value_grad_low = value_sum.astype(jnp.bfloat16)
        normed_grad = (
            contract_out(query_low, weights_now[1])
            + contract_out(key_low, weights_now[2])
            + contract_out(value_grad_low, weights_now[3])
        )
        in_back, in_gain_part = norm_back(normed_grad, inputs, scale_in, gain_in)
        grad_list.append(mid_grad + in_back)
        batch_grads = (
            jnp.sum(in_gain_part, axis=0),
            contract_rows(low_in, query_low),
            contract_rows(low_in, key_low),
            contract_rows(low_in, value_grad_low),
            jnp.sum(query_gain_part, axis=(0, 1, 2)),
            jnp.sum(key_gain_part, axis=(0, 1)),
            out_w_grad,
            jnp.sum(mid_gain_part, axis=0),
            router_grad,
        )
        full_total = (
            batch_grads if full_total is None else jax.tree.map(jnp.add, full_total, batch_grads)
        )
    shard_total = (
        lax.psum_scatter(full_total[0], "grp", scatter_dimension=0, tiled=True),
        lax.psum_scatter(full_total[1], "grp", scatter_dimension=0, tiled=True),
        lax.psum_scatter(full_total[2], "grp", scatter_dimension=0, tiled=True),
        lax.psum_scatter(full_total[3], "grp", scatter_dimension=0, tiled=True),
        lax.psum_scatter(full_total[4], "grp", scatter_dimension=0, tiled=True),
        lax.psum_scatter(full_total[5], "grp", scatter_dimension=0, tiled=True),
        lax.psum_scatter(full_total[6], "grp", scatter_dimension=0, tiled=True),
        lax.psum_scatter(full_total[7], "grp", scatter_dimension=0, tiled=True),
        lax.psum_scatter(full_total[8], "grp", scatter_dimension=0, tiled=True),
    )
    summed = lax.psum(
        (
            shard_total[0],
            shard_total[1],
            shard_total[2],
            shard_total[3],
            shard_total[4],
            shard_total[5],
            shard_total[6],
            shard_total[7],
            shard_total[8],
            gate_total,
            up_total,
            down_total,
        ),
        "rep",
    )
    layer_out = jnp.stack(out_list, axis=0)[None]
    input_grad = jnp.stack(grad_list, axis=0)[None]
    return (
        layer_out,
        input_grad,
        summed[0],
        summed[1],
        summed[2],
        summed[3],
        summed[4],
        summed[5],
        summed[6],
        summed[7],
        summed[8],
        summed[9],
        summed[10],
        summed[11],
    )


def solution(mesh):
    placed = (
        P("rep", None, "grp", None),
        P("rep", None, "grp", None),
        P("rep", None, "grp", None),
        P("grp"),
        P("grp", None),
        P("grp", None),
        P("grp", None),
        P("grp"),
        P("grp"),
        P("grp", None),
        P("grp"),
        P("grp", None),
        P("grp", None, None),
        P("grp", None, None),
        P("grp", None, None),
    )
    return jax.shard_map(
        per_device,
        mesh=mesh,
        in_specs=placed,
        out_specs=(
            P("rep", None, "grp", None),
            P("rep", None, "grp", None),
            P("grp"),
            P("grp", None),
            P("grp", None),
            P("grp", None),
            P("grp"),
            P("grp"),
            P("grp", None),
            P("grp"),
            P("grp", None),
            P("grp", None, None),
            P("grp", None, None),
            P("grp", None, None),
        ),
        check_vma=False,
    )
```

profile of v0, /device:TPU:0, one launch (start us, length us, event | category | flops | bytes accessed | tf_op | source)
XLA Modules:
  0.0 3465.8 jit_solution(2635313314376230809)
XLA Ops:
  8.7 42.4 %all-gather = bf16[16,1,128]{2,1,0:T(2,128)(2,1)S(1)} all-gather(bf16[1,1,128]{2,1,0:T(2,128)(2,1)} %bitcast.706), channel_id=1, replica_groups=mesh['grp'=16,'rep'=2] {'grp'}, dimensions={0}, use_global_device_ids=true | all-gather | bytes 4352 | tf_op jit(solution)/shard_map/all_gather | solution.py:110
  54.9 37.0 %all-reduce.13 = (bf16[128]{0:T(256)(128)(2,1)S(1)}, bf16[128]{0:T(256)(128)(2,1)S(1)}) all-reduce(bf16[128]{0:T(256)(128)(2,1)S(1)} %dynamic-update-slice, bf16[128]{0:T(256)(128)(2,1)S(1)} %dynamic-update-slice.1), channel_id=1, replica_groups=mesh['grp'=16,'rep'=2] {'grp'}, use_global_device_ids=true, to_apply=%add.4 | all-reduce | flops 256 | bytes 1024
  106.4 30.5 all-gather.11.cloned.1.call-done
  141.9 38.1 %all-gather.1 = bf16[16,1,128]{2,1,0:T(2,128)(2,1)S(1)} all-gather(bf16[1,1,128]{2,1,0:T(2,128)(2,1)S(1)} %bitcast.707), channel_id=1, replica_groups=mesh['grp'=16,'rep'=2] {'grp'}, dimensions={0}, use_global_device_ids=true | all-gather | bytes 4352 | tf_op jit(solution)/shard_map/all_gather | solution.py:117
  196.5 55.0 %all-gather.13.cloned.1.call-done = bf16[1024,512]{1,0:T(8,128)(2,1)} async-done(((bf16[64,512]{1,0:T(8,128)(2,1)}), bf16[1024,512]{1,0:T(8,128)(2,1)}) %all-gather.13.cloned.1.call-update) | async-done | bytes 1048592 | tf_op jit(solution)/shard_map/all_gather | solution.py:154
  253.7 190.9 %all-gather.19.cloned.1.call-done = bf16[2048,4096]{1,0:T(8,128)(2,1)} async-done(((bf16[128,4096]{1,0:T(8,128)(2,1)}), bf16[2048,4096]{1,0:T(8,128)(2,1)}) %all-gather.19.cloned.1.call-update) | async-done | bytes 16777232 | tf_op jit(solution)/shard_map/all_gather | solution.py:111
  444.6 22.5 copy.172
  507.8 129.2 %all-gather.21.cloned.1.call-done = bf16[4096,2048]{1,0:T(8,128)(2,1)} async-done(((bf16[256,2048]{1,0:T(8,128)(2,1)}), bf16[4096,2048]{1,0:T(8,128)(2,1)}) %all-gather.21.cloned.1.call-update) | async-done | bytes 16777232 | tf_op jit(solution)/shard_map/all_gather | solution.py:116
  660.6 77.3 %all_gather.49 = bf16[2048,16]{0,1:T(8,128)(2,1)S(1)} all-gather(bf16[128,16]{0,1:T(8,128)(2,1)S(1)} %copy-done.136), channel_id=1, replica_groups=mesh['grp'=16,'rep'=2] {'grp'}, dimensions={0}, use_global_device_ids=true | all-gather | bytes 69632 | tf_op jit(solution)/shard_map/all_gather | solution.py:118
  772.8 40.7 %all-to-all-done.4 = bf16[16,36,2048]{2,1,0:T(8,128)(2,1)} async-done(((bf16[16,36,2048]{2,1,0:T(8,128)(2,1)}), bf16[16,36,2048]{2,1,0:T(8,128)(2,1)}, u32[]{:S(2)}, u32[]{:S(2)}) %all-to-all-start.4) | async-done | bytes 2359328 | tf_op jit(solution)/shard_map/all_to_all | solution.py:228
  848.2 47.7 %all-to-all-done.5 = bf16[16,36,2048]{2,1,0:T(8,128)(2,1)} async-done(((bf16[16,36,2048]{2,1,0:T(8,128)(2,1)}), bf16[16,36,2048]{2,1,0:T(8,128)(2,1)}, u32[]{:S(2)}, u32[]{:S(2)}) %all-to-all-start.5) | async-done | bytes 2359328 | tf_op jit(solution)/shard_map/all_to_all | solution.py:250
  895.9 13.1 all-to-all-start.1
  931.6 65.9 %all-gather.23.cloned.1.call-done = bf16[1024,512]{1,0:T(8,128)(2,1)} async-done(((bf16[64,512]{1,0:T(8,128)(2,1)}), bf16[1024,512]{1,0:T(8,128)(2,1)}) %all-gather.23.cloned.1.call-update) | async-done | bytes 1048592 | tf_op jit(solution)/shard_map/all_gather | solution.py:154
  1107.5 42.3 %all-to-all-done.6 = bf16[16,36,2048]{2,1,0:T(8,128)(2,1)} async-done(((bf16[16,36,2048]{2,1,0:T(8,128)(2,1)}), bf16[16,36,2048]{2,1,0:T(8,128)(2,1)}, u32[]{:S(2)}, u32[]{:S(2)}) %all-to-all-start.6) | async-done | bytes 2359328 | tf_op jit(solution)/shard_map/all_to_all | solution.py:228
  1149.7 12.4 all-to-all-start.2
  1168.3 45.2 %all-to-all-done.2 = bf16[16,36,2048]{2,1,0:T(8,128)(2,1)} async-done(((bf16[16,36,2048]{2,1,0:T(8,128)(2,1)}), bf16[16,36,2048]{2,1,0:T(8,128)(2,1)}, u32[]{:S(2)}, u32[]{:S(2)}) %all-to-all-start.2) | async-done | bytes 2359328 | tf_op jit(solution)/shard_map/all_to_all | solution.py:192
  1248.4 45.6 %all-to-all-done.7 = bf16[16,36,2048]{2,1,0:T(8,128)(2,1)S(1)} async-done(((bf16[16,36,2048]{2,1,0:T(8,128)(2,1)}), bf16[16,36,2048]{2,1,0:T(8,128)(2,1)S(1)}, u32[]{:S(2)}, u32[]{:S(2)}) %all-to-all-start.7) | async-done | bytes 2359328 | tf_op jit(solution)/shard_map/all_to_all | solution.py:250
  1316.0 41.5 %all-to-all-done.3 = bf16[16,36,2048]{2,1,0:T(8,128)(2,1)} async-done(((bf16[16,36,2048]{2,1,0:T(8,128)(2,1)}), bf16[16,36,2048]{2,1,0:T(8,128)(2,1)}, u32[]{:S(2)}, u32[]{:S(2)}) %all-to-all-start.3) | async-done | bytes 2359328 | tf_op jit(solution)/shard_map/all_to_all | solution.py:207
  1381.2 13.3 fusion.5
  1423.1 59.1 %reduce-scatter.14.cloned.1.call-done = bf16[64,512]{1,0:T(8,128)(2,1)} async-done(((bf16[1024,512]{1,0:T(8,128)(2,1)}), bf16[64,512]{1,0:T(8,128)(2,1)}) %reduce-scatter.14.cloned.1.call-update) | async-done | bytes 65552 | tf_op jit(solution)/shard_map/reduce_scatter | solution.py:296
  1483.1 75.3 %reduce-scatter.16.cloned.1.call-done = bf16[64,512]{1,0:T(8,128)(2,1)} async-done(((bf16[1024,512]{1,0:T(8,128)(2,1)}), bf16[64,512]{1,0:T(8,128)(2,1)}) %reduce-scatter.16.cloned.1.call-update) | async-done | bytes 65552 | tf_op jit(solution)/shard_map/reduce_scatter | solution.py:296
  1564.6 70.2 %reduce-scatter.28.cloned.1.call-done = bf16[64,512]{1,0:T(8,128)(2,1)} async-done(((bf16[1024,512]{1,0:T(8,128)(2,1)}), bf16[64,512]{1,0:T(8,128)(2,1)}) %reduce-scatter.28.cloned.1.call-update) | async-done | bytes 65552
  1638.4 72.9 %reduce-scatter.30.cloned.1.call-done = bf16[64,512]{1,0:T(8,128)(2,1)} async-done(((bf16[1024,512]{1,0:T(8,128)(2,1)}), bf16[64,512]{1,0:T(8,128)(2,1)}) %reduce-scatter.30.cloned.1.call-update) | async-done | bytes 65552
  1729.7 13.5 fusion.129
  1743.2 25.0 convolution_add_fusion
  1769.4 13.3 fusion.135
  1782.8 24.9 convolution_add_fusion.1
  1849.5 52.5 %reduce-scatter.22.cloned.1.call-done = f32[128,512]{1,0:T(8,128)} async-done(((f32[2048,512]{1,0:T(8,128)}), f32[128,512]{1,0:T(8,128)}) %reduce-scatter.22.cloned.1.call-update) | async-done | bytes 262160 | tf_op jit(solution)/shard_map/reduce_scatter | solution.py:342
  1902.0 685.3 %reduce-scatter.18.cloned.1.call-done = f32[128,4096]{1,0:T(8,128)} async-done(((f32[2048,4096]{1,0:T(8,128)}), f32[128,4096]{1,0:T(8,128)}) %reduce-scatter.18.cloned.1.call-update) | async-done | bytes 2097168 | tf_op jit(solution)/shard_map/reduce_scatter | solution.py:340
  2587.3 691.3 %reduce-scatter.24.cloned.1.call-done = f32[256,2048]{1,0:T(8,128)} async-done(((f32[4096,2048]{1,0:T(8,128)}), f32[256,2048]{1,0:T(8,128)}) %reduce-scatter.24.cloned.1.call-update) | async-done | bytes 2097168 | tf_op jit(solution)/shard_map/reduce_scatter | solution.py:345
  3309.1 79.3 %all-reduce.10 = (f32[2048]{0:T(1024)S(1)}, f32[128]{0:T(128)S(1)}, f32[128]{0:T(128)S(1)}, f32[2048]{0:T(1024)S(1)}) all-reduce(f32[2048]{0:T(1024)S(1)} %add.464, f32[128]{0:T(128)S(1)} %add.468, f32[128]{0:T(128)S(1)} %add.469, f32[2048]{0:T(1024)S(1)} %add.471), channel_id=6, replica_groups=mesh['grp'=16,'rep'=2] {'grp'}, use_global_device_ids=true, to_apply=%region_52.53.clone | all-reduce | flops 4352 | bytes 34816
  3396.2 44.1 %all-reduce.16.cloned.1.call-done = (f32[128,4096]{1,0:T(8,128)}, f32[128,512]{1,0:T(8,128)}, f32[128,512]{1,0:T(8,128)}, f32[256,2048]{1,0:T(8,128)}, f32[1,204...) async-done(((f32[128,4096]{1,0:T(8,128)}, f32[128,512]{1,0:T(8,128)}, f32[128,512]{1,0:T(8,128)}, f32[256,2048]{1,0:T(8,128)}, ...) | async-done | bytes 23592976 | tf_op jit(solution)/shard_map/psum | solution.py:349
  (619 shorter events, 549.5 us)
Async XLA Ops:
  7.2 811.4 %copy-start = (bf16[1,2048,768]{2,1,0:T(8,128)(2,1)S(1)}, bf16[1,2048,768]{2,1,0:T(8,128)(2,1)}, u32[]{:S(2)}) copy-start(bf16[1,2048,768]{2,1,0:T(8,128)(2,1)} %param.27) | copy-start | bytes 9437188
  7.2 86.8 %all-gather.15.cloned.1.call-start = ((), (), s32[]{:S(2)}) async-start(), calls=%async_computation.19 | async-start | bytes 2228224 | tf_op jit(solution)/shard_map/all_gather | solution.py:112
  7.9 129.0 %all-gather.11.cloned.1.call-start = ((), (), s32[]{:S(2)}) async-start(), calls=%async_computation.17 | async-start | bytes 2228224 | tf_op jit(solution)/shard_map/all_gather | solution.py:113
  8.7 185.6 %all-gather.17.cloned.1.call-start = ((), (), s32[]{:S(2)}) async-start(), calls=%async_computation.20 | async-start | bytes 1114112 | tf_op jit(solution)/shard_map/all_gather | solution.py:153
  51.1 858.4 %copy-start.48 = (f32[16,1,128]{2,1,0:T(1,128)}, f32[16,1,128]{2,1,0:T(1,128)S(1)}, u32[]{:S(2)}) copy-start(f32[16,1,128]{2,1,0:T(1,128)S(1)} %convert_element_type.432) | copy-start | bytes 24580
  93.7 373.4 %copy-start.97 = (f32[64]{0:T(128)}, f32[64]{0:T(128)S(1)}, u32[]{:S(2)}) copy-start(f32[64]{0:T(128)S(1)} %get-tuple-element.161) | copy-start | bytes 772
  93.8 386.1 %copy-start.93 = (f32[64]{0:T(128)}, f32[64]{0:T(128)S(1)}, u32[]{:S(2)}) copy-start(f32[64]{0:T(128)S(1)} %get-tuple-element.126) | copy-start | bytes 772
  94.0 400.5 %copy-start.66 = (f32[64,64]{1,0:T(8,128)}, f32[64,64]{1,0:T(8,128)S(1)}, u32[]{:S(2)}) copy-start(f32[64,64]{1,0:T(8,128)S(1)} %get-tuple-element.119) | copy-start | bytes 49156
  94.0 400.5 %copy-start.68 = (f32[64,64]{1,0:T(8,128)}, f32[64,64]{1,0:T(8,128)S(1)}, u32[]{:S(2)}) copy-start(f32[64,64]{1,0:T(8,128)S(1)} %get-tuple-element.120) | copy-start | bytes 49156
  106.4 145.2 %all-gather.13.cloned.1.call-start = ((), (), s32[]{:S(2)}) async-start(), calls=%async_computation.18 | async-start | bytes 1114112 | tf_op jit(solution)/shard_map/all_gather | solution.py:154
  139.8 304.8 %all-gather.19.cloned.1.call-start = ((), (), s32[]{:S(2)}) async-start(), calls=%async_computation.21 | async-start | bytes 17825792 | tf_op jit(solution)/shard_map/all_gather | solution.py:111
  140.4 496.7 %all-gather.21.cloned.1.call-start = ((), (), s32[]{:S(2)}) async-start(), calls=%async_computation.22 | async-start | bytes 17825792 | tf_op jit(solution)/shard_map/all_gather | solution.py:116
  656.0 100.2 %all-to-all-start = ((bf16[16,36,2048]{2,1,0:T(8,128)(2,1)}), bf16[16,36,2048]{2,1,0:T(8,128)(2,1)}, u32[]{:S(2)}, u32[]{:S(2)}) async-start(bf16[16,36,2048]{2,1,0:T(8,128)(2,1)} %reshape.1021), calls=%async_computation | async-start | bytes 5242880 | tf_op jit(solution)/shard_map/all_to_all | solution.py:192
  756.1 57.3 %all-to-all-start.4 = ((bf16[16,36,2048]{2,1,0:T(8,128)(2,1)}), bf16[16,36,2048]{2,1,0:T(8,128)(2,1)}, u32[]{:S(2)}, u32[]{:S(2)}) async-start(bf16[16,36,2048]{2,1,0:T(8,128)(2,1)} %reshape.1033), calls=%async_computation.4 | async-start | bytes 5242880 | tf_op jit(solution)/shard_map/all_to_all | solution.py:228
  830.6 65.3 %all-to-all-start.5 = ((bf16[16,36,2048]{2,1,0:T(8,128)(2,1)}), bf16[16,36,2048]{2,1,0:T(8,128)(2,1)}, u32[]{:S(2)}, u32[]{:S(2)}) async-start(bf16[16,36,2048]{2,1,0:T(8,128)(2,1)} %add_convert_fusion.1), calls=%async_computation.5 | async-start | bytes 5242880 | tf_op jit(solution)/shard_map/all_to_all | solution.py:250
  841.5 87.8 %all-gather.25.cloned.1.call-start = ((), (), s32[]{:S(2)}) async-start(), calls=%async_computation.24 | async-start | bytes 1114112 | tf_op jit(solution)/shard_map/all_gather | solution.py:153
  895.9 124.9 %all-to-all-start.1 = ((bf16[16,36,2048]{2,1,0:T(8,128)(2,1)}), bf16[16,36,2048]{2,1,0:T(8,128)(2,1)}, u32[]{:S(2)}, u32[]{:S(2)}) async-start(bf16[16,36,2048]{2,1,0:T(8,128)(2,1)} %convolution_convert_fusion.3), calls=%async_computation.1 | async-start | bytes 5242880 | tf_op jit(solution)/shard_map/all_to_all | solution.py:207
  909.0 88.5 %all-gather.23.cloned.1.call-start = ((), (), s32[]{:S(2)}) async-start(), calls=%async_computation.23 | async-start | bytes 1114112 | tf_op jit(solution)/shard_map/all_gather | solution.py:154
  1093.8 55.9 %all-to-all-start.6 = ((bf16[16,36,2048]{2,1,0:T(8,128)(2,1)}), bf16[16,36,2048]{2,1,0:T(8,128)(2,1)}, u32[]{:S(2)}, u32[]{:S(2)}) async-start(bf16[16,36,2048]{2,1,0:T(8,128)(2,1)} %reshape.1040), calls=%async_computation.7 | async-start | bytes 5242880 | tf_op jit(solution)/shard_map/all_to_all | solution.py:228
  1149.7 63.7 %all-to-all-start.2 = ((bf16[16,36,2048]{2,1,0:T(8,128)(2,1)}), bf16[16,36,2048]{2,1,0:T(8,128)(2,1)}, u32[]{:S(2)}, u32[]{:S(2)}) async-start(bf16[16,36,2048]{2,1,0:T(8,128)(2,1)} %reshape.1030), calls=%async_computation.2 | async-start | bytes 5242880 | tf_op jit(solution)/shard_map/all_to_all | solution.py:192
  1230.5 63.5 %all-to-all-start.7 = ((bf16[16,36,2048]{2,1,0:T(8,128)(2,1)}), bf16[16,36,2048]{2,1,0:T(8,128)(2,1)S(1)}, u32[]{:S(2)}, u32[]{:S(2)}) async-start(bf16[16,36,2048]{2,1,0:T(8,128)(2,1)} %add_convert_fusion), calls=%async_computation.8 | async-start | bytes 5242880 | tf_op jit(solution)/shard_map/all_to_all | solution.py:250
  1294.0 63.5 %all-to-all-start.3 = ((bf16[16,36,2048]{2,1,0:T(8,128)(2,1)}), bf16[16,36,2048]{2,1,0:T(8,128)(2,1)}, u32[]{:S(2)}, u32[]{:S(2)}) async-start(bf16[16,36,2048]{2,1,0:T(8,128)(2,1)} %convolution_convert_fusion.2), calls=%async_computation.3 | async-start | bytes 5242880 | tf_op jit(solution)/shard_map/all_to_all | solution.py:207
  1306.0 176.1 %reduce-scatter.14.cloned.1.call-start = ((), (), s32[]{:S(2)}) async-start(), calls=%async_computation.25 | async-start | bytes 1114112 | tf_op jit(solution)/shard_map/reduce_scatter | solution.py:296
  1397.9 160.6 %reduce-scatter.16.cloned.1.call-start = ((), (), s32[]{:S(2)}) async-start(), calls=%async_computation.26 | async-start | bytes 1114112 | tf_op jit(solution)/shard_map/reduce_scatter | solution.py:296
  1410.0 224.8 %reduce-scatter.28.cloned.1.call-start = ((), (), s32[]{:S(2)}) async-start(), calls=%async_computation.32 | async-start | bytes 1114112
  1416.3 295.1 %reduce-scatter.30.cloned.1.call-start = ((), (), s32[]{:S(2)}) async-start(), calls=%async_computation.33 | async-start | bytes 1114112
  1422.6 426.9 %reduce-scatter.20.cloned.1.call-start = ((), (), s32[]{:S(2)}) async-start(), calls=%async_computation.28 | async-start | bytes 4456448 | tf_op jit(solution)/shard_map/reduce_scatter | solution.py:341
  1564.5 337.5 %reduce-scatter.22.cloned.1.call-start = ((), (), s32[]{:S(2)}) async-start(), calls=%async_computation.29 | async-start | bytes 4456448 | tf_op jit(solution)/shard_map/reduce_scatter | solution.py:342
  1716.4 870.9 %reduce-scatter.18.cloned.1.call-start = ((), (), s32[]{:S(2)}) async-start(), calls=%async_computation.27 | async-start | bytes 35651584 | tf_op jit(solution)/shard_map/reduce_scatter | solution.py:340
  1768.3 1510.4 %reduce-scatter.24.cloned.1.call-start = ((), (), s32[]{:S(2)}) async-start(), calls=%async_computation.30 | async-start | bytes 35651584 | tf_op jit(solution)/shard_map/reduce_scatter | solution.py:345
  1807.7 1580.9 %reduce-scatter.26.cloned.1.call-start = ((), (), s32[]{:S(2)}) async-start(), calls=%async_computation.31 | async-start | bytes 139264 | tf_op jit(solution)/shard_map/reduce_scatter | solution.py:347
  1839.9 1600.3 %all-reduce.16.cloned.1.call-start = ((), (), s32[]{:S(2)}) async-start(), calls=%async_computation.34 | async-start | bytes 47185920 | tf_op jit(solution)/shard_map/psum | solution.py:349
  (162 other events, 3582.9 us)
Sparse Core Ops, SparseCore 0:
  10.8 63.6 all-gather.14
  77.3 59.5 all-gather.10
  140.3 53.9 all-gather.16
  197.4 54.0 all-gather.12
  254.2 190.4 all-gather.18
  447.2 189.7 all-gather.20
  845.7 83.5 all-gather.24
  932.6 64.8 all-gather.22
  1398.0 84.0 reduce-scatter.13
  1484.3 74.0 reduce-scatter.15
  1560.7 74.0 reduce-scatter.27
  1637.0 74.2 reduce-scatter.29
  1713.6 91.5 reduce-scatter.19
  1807.3 94.6 reduce-scatter.21
  1904.2 683.0 reduce-scatter.17
  2589.5 689.0 reduce-scatter.23
  3281.3 81.5 reduce-scatter.25
  3366.9 73.3 all-reduce.15
where the time goes:
time: 3470 us
  waiting for transfers between devices  2510 us (72%)
  matrix products  339 us (10%)
  blocking collectives  279 us (8%)
  local copies, waits for them, and re-layouts  169 us (5%)
  starting transfers between devices  82.1 us (2%)
  other arithmetic  70.1 us (2%)
    reduce_scatter x1, waiting for transfers between devices, per_device(): lax.psum_scatter(full_total[6], 'grp', scatter_dimension=0, tiled=True)  691 us
    reduce_scatter x1, waiting for transfers between devices, per_device(): lax.psum_scatter(full_total[1], 'grp', scatter_dimension=0, tiled=True)  685 us
    all_gather x1, waiting for transfers between devices, per_device(): lax.all_gather(query_weight, 'grp', axis=0, tiled=True)  191 us
    unnamed x20, waiting for transfers between devices  146 us
    reduce_scatter x2, waiting for transfers between devices, per_device(): lax.psum_scatter(key_flat.astype(jnp.bfloat16), 'grp', scatter_dimension=...  134 us
    all_gather x1, waiting for transfers between devices, per_device(): lax.all_gather(out_weight, 'grp', axis=0, tiled=True)  129 us
    all_gather x2, waiting for transfers between devices, per_device(): lax.all_gather(value_low, 'grp', axis=0, tiled=True)  121 us
    unnamed x2, blocking collectives  116 us
  transfers between devices with their start and end apart: 26, of which 21 were waited for; matrix products, arithmetic and copies ran while one was open for 11% of the time, Pallas kernels for 0%

commit v1 on v0

v1 whole, which is shorter than its diff:
```python
import math

import jax
import jax.numpy as jnp
from jax import lax
from jax.sharding import PartitionSpec as P

BLOCK = 256
SEQ = 1024
EPS = 1e-06
THETA = 1000000.0
NEGATIVE = -1e30
AXES = ("grp", "rep")
LINES = 4
F32 = jnp.float32
BF16 = jnp.bfloat16


def row_scale(values):
    return lax.rsqrt(jnp.mean(values * values, axis=-1, keepdims=True) + EPS)


def norm_back(grad, values, factor, gain):
    inner = grad * gain
    back = factor * inner - values * factor**3 * jnp.mean(inner * values, axis=-1, keepdims=True)
    return (back, grad * values * factor)


def rotate(values, cosine, sine):
    half = values.shape[-1] // 2
    first, second = values[..., :half], values[..., half:]
    return jnp.concatenate([first * cosine - second * sine, second * cosine + first * sine], axis=-1)


def dot(left, right):
    return lax.dot_general(left, right, (((1,), (0,)), ((), ())), preferred_element_type=F32)


def dot_out(left, right):
    return lax.dot_general(left, right, (((1,), (1,)), ((), ())), preferred_element_type=F32)


def dot_rows(left, right):
    return lax.dot_general(left, right, (((0,), (0,)), ((), ())), preferred_element_type=F32)


def flip_bit(values, axis, bit):
    count = values.shape[axis]
    pieces = [lax.slice_in_dim(values, i, i + bit, axis=axis) for i in range(0, count, bit)]
    order = [i ^ 1 for i in range(len(pieces))]
    return jnp.concatenate([pieces[i] for i in order], axis=axis)


def xor_order(values, axis, mine):
    bit = 1
    while bit < values.shape[axis]:
        values = jnp.where((mine & bit) != 0, flip_bit(values, axis, bit), values)
        bit *= 2
    return values


def build(groups, reps):
    columns = groups // LINES
    sequences = max(1, groups // 16)

    class Moves:
        pass

    def index(g, r):
        return g * reps + r

    def pairs(target):
        return [
            (index(g, r), index(*target(g, r))) for g in range(groups) for r in range(reps)
        ]

    def line(k):
        table = pairs(lambda g, r: (((g // columns) ^ k) * columns + g % columns, r))
        return lambda v: lax.ppermute(v, AXES, table)

    def plane(k):
        table = pairs(lambda g, r: (g ^ k, r))
        return lambda v: lax.ppermute(v, AXES, table)

    def replica(k):
        table = pairs(lambda g, r: (g, r ^ k))
        return lambda v: lax.ppermute(v, AXES, table)

    def home(k):
        def target(g, r):
            sequence, block = g // 16, g % 16
            batch = k ^ (g & 1)
            column = (sequence * 2 + r % 2) * 2 + batch
            return ((block // 4) * columns + column, (r // 2) * 2 + (block // 2) % 2)

        table = pairs(target)
        back = [(b, a) for a, b in table]
        return (
            lambda v: lax.ppermute(v, AXES, table),
            lambda v: lax.ppermute(v, AXES, back),
        )

    moves = Moves()
    moves.columns = columns
    moves.line = [None] + [line(k) for k in range(1, LINES)]
    moves.plane = [None] + [plane(k) for k in range(1, columns)]
    moves.core = replica(1)
    moves.replicas = [replica(2 * k) for k in range(1, reps // 2)]
    moves.home = [home(0), home(1)]
    del sequences
    return moves


def per_device(
    layer_input,
    out_grad,
    routes,
    norm_in,
    query_weight,
    key_weight,
    value_weight,
    query_gain,
    key_gain,
    out_weight,
    norm_mid,
    router,
    expert_gate,
    expert_up,
    expert_down,
):
    groups, reps = lax.axis_size("grp"), lax.axis_size("rep")
    mv = build(groups, reps)
    columns = mv.columns
    g, r = lax.axis_index("grp"), lax.axis_index("rep")
    tz, gc, core = g // columns, g % columns, r % 2
    odd = (g & 1) != 0
    batches, tokens, width = layer_input.shape[1:]
    experts = groups
    piece = width // groups
    head = query_gain.shape[0] * groups
    heads = query_weight.shape[1] // head
    kv_heads = key_weight.shape[1] // head
    local_heads = heads // (2 * kv_heads)
    scale = 1.0 / math.sqrt(head)
    hidden_half = expert_gate.shape[2] // 2
    rows = batches * tokens
    total = 8 * rows

    def bring(values):
        values = jnp.where(odd, values[::-1], values)
        first, second = (mv.home[k][0](values[k]) for k in range(2))
        got = jnp.stack([first, second])
        return jnp.where(odd, got[::-1], got).reshape((rows,) + values.shape[2:])

    def take_back(values):
        values = values.reshape((2, tokens) + values.shape[1:])
        values = jnp.where(odd, values[::-1], values)
        got = jnp.stack([mv.home[k][1](values[k]) for k in range(2)])
        return jnp.where(odd, got[::-1], got)

    def gather_tokens(values):
        parts = [values] + [mv.line[k](values) for k in range(1, LINES)]
        others = [mv.core(part) for part in parts]
        return jnp.concatenate(parts + others, axis=0)

    def scatter_tokens(partial):
        half = total // 2
        both = partial[:half].astype(F32) + mv.core(partial[half:]).astype(F32)
        blocks = both.reshape((LINES, rows) + both.shape[1:])
        low = blocks.astype(BF16)
        result = blocks[0]
        for k in range(1, LINES):
            result = result + mv.line[k](low[k]).astype(F32)
        return result

    def gather_plane(values, last_bit):
        bits = [b for b in (1, 2, 4, 8) if b < columns]
        if last_bit == 1:
            bits = bits[::-1]
        held = {0: values}
        for b in bits:
            for s in list(held):
                held[s | b] = mv.plane[b](held[s])
        return [held[s] for s in range(columns)]

    def scatter_plane(parts, last_bit):
        bits = [b for b in (1, 2, 4, 8) if b < columns]
        if last_bit == 1:
            bits = bits[::-1]
        held = dict(enumerate(parts))
        for b in bits:
            for s in [s for s in held if s & b]:
                got = mv.plane[b](held.pop(s).astype(BF16))
                held[s ^ b] = held[s ^ b].astype(F32) + got.astype(F32)
        result = held[0]
        if mv.replicas:
            low = result.astype(BF16)
            for move in mv.replicas:
                result = result + move(low).astype(F32)
        return result

    gains = jnp.concatenate([query_gain, key_gain])
    packed = jnp.concatenate(
        [
            norm_in[None],
            norm_mid[None],
            router.T,
            jnp.pad(gains, (0, piece - gains.shape[0]))[None],
        ]
    )
    packed = jnp.stack([packed] + [mv.plane[s](packed) for s in range(1, columns)])
    packed = jnp.stack([packed] + [mv.line[k](packed) for k in range(1, LINES)])
    packed = xor_order(xor_order(packed, 0, tz), 1, gc).reshape(groups, experts + 3, piece)
    small = packed[:, : experts + 2].transpose(1, 0, 2).reshape(experts + 2, width)
    gain_in, gain_mid = small[0].astype(F32), small[1].astype(F32)
    router_t = small[2:]
    part = head // groups
    gain_q = packed[:, experts + 2, :part].reshape(head).astype(F32)
    gain_k = packed[:, experts + 2, part : 2 * part].reshape(head).astype(F32)

    inputs_low = bring(layer_input[0])
    grad_low = bring(out_grad[0])
    named = (routes[0][..., None] == jnp.arange(experts, dtype=jnp.int32)).any(axis=2)
    named = bring(named.astype(BF16))
    inputs = inputs_low.astype(F32)
    grad_out = grad_low.astype(F32)

    per_q = query_weight.reshape(piece, kv_heads, local_heads, 2, head)
    own_q = jnp.where(core == 0, per_q[:, :, :, 0], per_q[:, :, :, 1]).reshape(
        piece, kv_heads, local_heads * head
    )
    qkv = jnp.concatenate(
        [
            own_q,
            key_weight.reshape(piece, kv_heads, head),
            value_weight.reshape(piece, kv_heads, head),
        ],
        axis=2,
    ).transpose(1, 0, 2)
    rel = xor_order(qkv, 0, tz)
    rel = jnp.stack([rel[0]] + [mv.line[k](rel[k]) for k in range(1, LINES)])
    qkv = xor_order(rel, 0, tz)
    w_qkv = jnp.stack(gather_plane(qkv, 2), axis=1).reshape(width, -1)

    out_heads = out_weight.shape[0] // head
    if out_heads == 2:
        own_out = jnp.where(core == 0, out_weight[:head], out_weight[head:])
        w_out = jnp.stack(gather_plane(own_out, 2))
        w_out = xor_order(w_out, 0, gc).reshape(local_heads * head, width)
    else:
        w_out = xor_order(jnp.stack(gather_plane(out_weight, 2)), 0, gc)
        w_out = w_out.reshape(local_heads, 2, head, width)
        w_out = jnp.where(core == 0, w_out[:, 0], w_out[:, 1]).reshape(local_heads * head, width)

    def half_of(values, axis):
        low = lax.slice_in_dim(values, 0, hidden_half, axis=axis)
        high = lax.slice_in_dim(values, hidden_half, 2 * hidden_half, axis=axis)
        return jnp.where(core == 0, low, high)

    w_gate = gather_plane(half_of(expert_gate[0], 1), 1)
    w_up = gather_plane(half_of(expert_up[0], 1), 2)
    w_down = gather_plane(half_of(expert_down[0], 0), 1)

    which = jnp.arange(total, dtype=jnp.int32)
    side, block, inner = which // (LINES * rows), which // rows % LINES, which % rows
    block = block ^ tz
    position = (block * 2 + (side ^ core)) * rows + inner
    block = position // BLOCK
    visible = block[None, :] <= block[:, None]
    inverse = THETA ** (-(jnp.arange(head // 2, dtype=F32) * 2.0 / head))
    angle = position.astype(F32)[:, None] * inverse[None, :]
    cosine, sine = jnp.cos(angle), jnp.sin(angle)

    def swap_columns(values):
        pieces = values.reshape(values.shape[0], LINES, columns, piece)
        return xor_order(pieces, 2, gc).reshape(values.shape)

    scale_in = row_scale(inputs)
    low_in = (inputs * scale_in * gain_in).astype(BF16)
    a1 = gather_tokens(swap_columns(low_in))
    pre = dot(a1, w_qkv)
    q_width = local_heads * head
    query_pre = [pre[:, i * head : (i + 1) * head] for i in range(local_heads)]
    key_pre = pre[:, q_width : q_width + head]
    value_low = pre[:, q_width + head :].astype(BF16)
    query_scale = [row_scale(v) for v in query_pre]
    key_scale = row_scale(key_pre)
    query_rot = [
        rotate(v * s * gain_q, cosine, sine).astype(BF16) for v, s in zip(query_pre, query_scale)
    ]
    key_rot = rotate(key_pre * key_scale * gain_k, cosine, sine).astype(BF16)
    attended, probs_low, log_totals = [], [], []
    for i in range(local_heads):
        scores = jnp.where(visible, dot_out(query_rot[i], key_rot) * scale, NEGATIVE)
        peak = jnp.max(scores, axis=-1, keepdims=True)
        expo = jnp.exp(scores - peak)
        mass = jnp.sum(expo, axis=-1, keepdims=True)
        log_totals.append(peak + jnp.log(mass))
        low = (expo / mass).astype(BF16)
        probs_low.append(low)
        attended.append(dot(low, value_low).astype(BF16))
    attended = jnp.concatenate(attended, axis=1)
    mid = inputs + scatter_tokens(dot(attended, w_out).astype(BF16))
    scale_mid = row_scale(mid)
    low_mid = (mid * scale_mid * gain_mid).astype(BF16)

    a2 = gather_tokens(low_mid)
    dy = gather_tokens(grad_low)
    named_all = gather_tokens(named)

    def gates_of(rows_low, mask):
        logits = jnp.where(mask > 0, dot_out(rows_low, router_t), NEGATIVE)
        return jax.nn.softmax(logits, axis=-1)

    gates_own = gates_of(low_mid, named)
    gates_all = gates_of(a2, named_all).reshape(total, LINES, columns)
    gates_all = xor_order(gates_all, 2, gc)
    gates_line = jnp.sum(
        jnp.where(jnp.arange(LINES)[None, :, None] == tz, gates_all, 0.0), axis=1
    )
    gate_grads, mixed, gate_lows, up_lows = [], [], [], []
    for s in range(columns):
        weight = gates_line[:, s : s + 1]
        gate_pre = dot(a2, w_gate[s])
        up_pre = dot(a2, w_up[s])
        back = dot_out(dy, w_down[s])
        sigmoid = jax.nn.sigmoid(gate_pre)
        silu = gate_pre * sigmoid
        hidden = silu * up_pre
        gate_grads.append(jnp.sum(hidden * back, axis=1))
        mixed.append((hidden * weight).astype(BF16))
        hidden_grad = back * weight
        gate_lows.append(
            (hidden_grad * up_pre * sigmoid * (1.0 + gate_pre * (1.0 - sigmoid))).astype(BF16)
        )
        up_lows.append((hidden_grad * silu).astype(BF16))
    rows_back = sum(
        dot_out(gate_lows[s], w_gate[s]) + dot_out(up_lows[s], w_up[s]) for s in range(columns)
    )
    expert_part = scatter_tokens(rows_back.astype(BF16))
    made = sum(dot(mixed[s], w_down[s]) for s in range(columns))
    layer_out = (mid + scatter_tokens(made.astype(BF16))).astype(BF16)

    gate_grad = jnp.stack(gate_grads, axis=0).reshape(columns, 2, LINES, rows)
    gate_grad = gate_grad[:, 0] + mv.core(gate_grad[:, 1])
    gate_grad = jnp.stack(
        [gate_grad[:, 0]] + [mv.line[k](gate_grad[:, k]) for k in range(1, LINES)]
    )
    gate_grad = xor_order(xor_order(gate_grad, 0, tz), 1, gc).reshape(experts, rows).T
    pick_grad = gates_own * (gate_grad - jnp.sum(gates_own * gate_grad, axis=-1, keepdims=True))
    logit_low = pick_grad.astype(BF16)
    router_part = dot_rows(logit_low, low_mid)
    normed_mid_grad = expert_part + dot(logit_low, router_t)
    mid_back, mid_gain_part = norm_back(normed_mid_grad, mid, scale_mid, gain_mid)
    mid_grad = mid_back + grad_out

    branch = gather_tokens(mid_grad.astype(BF16))
    out_w_part = dot_rows(attended, branch)
    att_grad = dot_out(branch, w_out).astype(BF16)
    key_grad = jnp.zeros((total, head), F32)
    value_grad = jnp.zeros((total, head), F32)
    query_lows = []
    query_gain_part = jnp.zeros((head,), F32)
    for i in range(local_heads):
        grad_i = att_grad[:, i * head : (i + 1) * head]
        scores = dot_out(query_rot[i], key_rot) * scale
        probs = jnp.where(visible, jnp.exp(scores - log_totals[i]), 0.0)
        prob_grad = dot_out(grad_i, value_low)
        score_low = (
            probs * (prob_grad - jnp.sum(probs * prob_grad, axis=-1, keepdims=True))
        ).astype(BF16)
        query_grad = dot(score_low, key_rot) * scale
        key_grad = key_grad + dot_rows(score_low, query_rot[i]) * scale
        value_grad = value_grad + dot_rows(probs_low[i], grad_i)
        query_back, gain_part = norm_back(
            rotate(query_grad, cosine, -sine), query_pre[i], query_scale[i], gain_q
        )
        query_lows.append(query_back.astype(BF16))
        query_gain_part = query_gain_part + jnp.sum(gain_part, axis=0)
    key_back, key_gain_part = norm_back(rotate(key_grad, cosine, -sine), key_pre, key_scale, gain_k)
    qkv_low = jnp.concatenate(
        query_lows + [key_back.astype(BF16), value_grad.astype(BF16)], axis=1
    )
    normed_grad = swap_columns(scatter_tokens(dot_out(qkv_low, w_qkv).astype(BF16)))
    in_back, in_gain_part = norm_back(normed_grad, inputs, scale_in, gain_in)
    input_grad = mid_grad + in_back

    def whole(values, axis):
        other = mv.core(values)
        return jnp.where(
            core == 0,
            jnp.concatenate([values, other], axis=axis),
            jnp.concatenate([other, values], axis=axis),
        ).astype(F32)

    gate_total = whole(scatter_plane([dot_rows(a2, v) for v in gate_lows], 1).astype(BF16), 1)
    up_total = whole(scatter_plane([dot_rows(a2, v) for v in up_lows], 2).astype(BF16), 1)
    down_total = whole(scatter_plane([dot_rows(v, dy) for v in mixed], 1).astype(BF16), 0)

    out_parts = out_w_part.reshape(local_heads, head, width)
    if out_heads == 2:
        out_parts = xor_order(out_parts, 0, gc)
        out_total = whole(scatter_plane([out_parts[s] for s in range(columns)], 2), 0)
    else:
        zeros = jnp.zeros_like(out_parts)
        spread = jnp.where(
            core == 0, jnp.stack([out_parts, zeros], 1), jnp.stack([zeros, out_parts], 1)
        )
        spread = xor_order(spread.reshape(columns, head, width), 0, gc)
        out_total = scatter_plane([spread[s] for s in range(columns)], 2)
        out_total = out_total + mv.core(out_total)

    w_part = dot_rows(a1, qkv_low).reshape(LINES, columns, piece, -1)
    w_part = scatter_plane([w_part[:, s] for s in range(columns)], 2)
    rel = xor_order(w_part, 0, tz)
    rel_low = rel.astype(BF16)
    rel = jnp.stack([rel[0]] + [mv.line[k](rel_low[k]).astype(F32) for k in range(1, LINES)])
    mine = xor_order(rel, 0, tz)
    other = mv.core(mine)
    low, high = jnp.where(core == 0, mine, other), jnp.where(core == 0, other, mine)
    query_total = jnp.stack(
        [v[..., :q_width].reshape(kv_heads, piece, local_heads, head) for v in (low, high)], axis=3
    )
    query_total = query_total.transpose(1, 0, 2, 3, 4).reshape(piece, heads * head)
    both = low + high
    key_total = both[..., q_width : q_width + head].transpose(1, 0, 2).reshape(piece, -1)
    value_total = both[..., q_width + head :].transpose(1, 0, 2).reshape(piece, -1)

    small_part = jnp.concatenate(
        [
            jnp.sum(in_gain_part, axis=0)[None],
            jnp.sum(mid_gain_part, axis=0)[None],
            router_part,
        ]
    )
    small_part = small_part.reshape(experts + 2, groups, piece).transpose(1, 0, 2)
    gain_parts = jnp.stack(
        [query_gain_part.reshape(groups, part), jnp.sum(key_gain_part, axis=0).reshape(groups, part)],
        axis=1,
    ).reshape(groups, 2 * part)
    gain_parts = jnp.pad(gain_parts, ((0, 0), (0, piece - 2 * part)))[:, None]
    small_part = jnp.concatenate([small_part, gain_parts], axis=1)
    small_part = small_part.reshape(LINES, columns, experts + 3, piece)
    small_part = small_part + mv.core(small_part)
    small_part = xor_order(xor_order(small_part, 0, tz), 1, gc)
    small_part = small_part[0] + sum(mv.line[k](small_part[k]) for k in range(1, LINES))
    small_part = small_part[0] + sum(mv.plane[s](small_part[s]) for s in range(1, columns))
    small_part = small_part + sum(move(small_part) for move in mv.replicas)

    return (
        take_back(layer_out)[None],
        take_back(input_grad)[None],
        small_part[0],
        query_total,
        key_total,
        value_total,
        small_part[experts + 2, :part],
        small_part[experts + 2, part : 2 * part],
        out_total,
        small_part[1],
        small_part[2 : experts + 2].T,
        gate_total[None],
        up_total[None],
        down_total[None],
    )


def solution(mesh):
    tokens = P("rep", None, "grp", None)
    rows = P("grp", None)
    vector = P("grp")
    stacked = P("grp", None, None)
    return jax.shard_map(
        per_device,
        mesh=mesh,
        in_specs=(
            tokens,
            tokens,
            tokens,
            vector,
            rows,
            rows,
            rows,
            vector,
            vector,
            rows,
            vector,
            rows,
            stacked,
            stacked,
            stacked,
        ),
        out_specs=(
            tokens,
            tokens,
            vector,
            rows,
            rows,
            rows,
            vector,
            vector,
            rows,
            vector,
            rows,
            stacked,
            stacked,
            stacked,
        ),
        check_vma=False,
    )
```

time: 3470 us -> 1120 us (0.32)
  waiting for transfers between devices: 2510 us -> 503 us
  blocking collectives: 279 us -> 0 us
  matrix products: 339 us -> 237 us
  starting transfers between devices: 82.1 us -> 184 us
  local copies, waits for them, and re-layouts: 169 us -> 68.8 us
  other arithmetic: 70.1 us -> 111 us
    reduce_scatter x7 -> x0, waiting for transfers between devices: 1560 us -> none  [the longest x1 691 us: per_device(): lax.psum_scatter(full_total[6], 'grp', scatter_dimension=0, tiled=True)]
    ppermute x0 -> x119, waiting for transfers between devices: none -> 503 us  [the longest x42 297 us: line(): return lambda v: lax.ppermute(v, AXES, table)]
    all_gather x8 -> x0, waiting for transfers between devices: 492 us -> none  [the longest x1 191 us: per_device(): lax.all_gather(query_weight, 'grp', axis=0, tiled=True)]
    all_to_all x8 -> x0, waiting for transfers between devices: 263 us -> none  [the longest x2 93.2 us: per_device(): lax.all_to_all(back_rows.astype(jnp.bfloat16).reshape(groups, local_count...]
    ppermute x0 -> x119, starting transfers between devices: none -> 184 us  [the longest x42 113 us: line(): return lambda v: lax.ppermute(v, AXES, table)]
    all_gather x3 -> x0, blocking collectives: 158 us -> none  [the longest x1 77.3 us: per_device(): lax.all_gather(router, 'grp', axis=0, tiled=True)]
    unnamed x20 -> x0, waiting for transfers between devices: 146 us -> none
    unnamed x2 -> x0, blocking collectives: 116 us -> none
  transfers between devices with their start and end apart: 26 -> 119, of which waited for: 21 -> 42; matrix products, arithmetic and copies ran while one was open for 11% -> 34% of each run, Pallas kernels for 0% -> 0%
where the time goes in v1:
time: 1120 us; the launch traced here: 1110 us
  waiting for transfers between devices  503 us (45%)
  matrix products  237 us (21%)
  starting transfers between devices  184 us (16%)
  other arithmetic  111 us (10%)
  local copies, waits for them, and re-layouts  68.8 us (6%)
    ppermute x42, waiting for transfers between devices, line(): return lambda v: lax.ppermute(v, AXES, table)  297 us
    ppermute x36, waiting for transfers between devices, plane(): return lambda v: lax.ppermute(v, AXES, table)  148 us
    ppermute x42, starting transfers between devices, line(): return lambda v: lax.ppermute(v, AXES, table)  113 us
    dot_general x24, matrix products, dot_out(): lax.dot_general(left, right, (((1,), (1,)), ((), ())), preferred_element_...  108 us
    dot_general x23, matrix products, dot(): lax.dot_general(left, right, (((1,), (0,)), ((), ())), preferred_element_...  77.2 us
    dot_general x23, matrix products, dot_rows(): lax.dot_general(left, right, (((0,), (0,)), ((), ())), preferred_element_...  51.5 us
    ppermute x36, starting transfers between devices, plane(): return lambda v: lax.ppermute(v, AXES, table)  50.1 us
    ppermute x4, waiting for transfers between devices, home(): lax.ppermute(v, AXES, back)  46.8 us
  transfers between devices with their start and end apart: 119, of which 42 were waited for; matrix products, arithmetic and copies ran while one was open for 34% of the time, Pallas kernels for 0%

profile of v1, /device:TPU:0, one launch (start us, length us, event | category | flops | bytes accessed | tf_op | source)
XLA Modules:
  0.0 1108.1 jit_solution(13700111535083651830)
XLA Ops:
  51.7 12.2 %collective-permute-done.17 = bf16[128,768]{1,0:T(8,128)(2,1)S(1)} collective-permute-done((bf16[128,768]{1,0:T(8,128)(2,1)S(1)}, bf16[128,768]{1,0:T(8,128)(2,1)S(1)}, u32[]{:S(2)}, u32[]{:S(2)}) %collective-permute-start.17) | collective-permute-done | bytes 196640 | tf_op jit(solution)/shard_map/ppermute | solution.py:79
  86.9 17.3 %collective-permute-done.8 = bf16[128,2048]{1,0:T(8,128)(2,1)S(1)} collective-permute-done((bf16[128,2048]{1,0:T(8,128)(2,1)S(1)}, bf16[128,2048]{1,0:T(8,128)(2,1)S(1)}, u32[]{:S(2)}, u32[]{:S(2)}) %collective-permute-start.8) | collective-permute-done | bytes 524320 | tf_op jit(solution)/shard_map/ppermute | solution.py:79
  106.6 8.1 collective-permute-done.10
  114.8 14.0 %collective-permute-start.62 = (bf16[128,2048]{1,0:T(8,128)(2,1)S(1)}, bf16[128,2048]{1,0:T(8,128)(2,1)S(1)}, u32[]{:S(2)}, u32[]{:S(2)}) collective-permute-start(bf16[128,2048]{1,0:T(8,128)(2,1)S(1)} %bitcast.418), channel_id=1, source_target_pairs={{0,16},{1,17},{2,18},{3,19},{4,20},{5,21},{6,22},{7,23},{8,24},{9,... | collective-permute-start | bytes 1572872 | tf_op jit(solution)/shard_map/ppermute | solution.py:79
  133.3 29.7 %collective-permute-done.62 = bf16[128,2048]{1,0:T(8,128)(2,1)S(1)} collective-permute-done((bf16[128,2048]{1,0:T(8,128)(2,1)S(1)}, bf16[128,2048]{1,0:T(8,128)(2,1)S(1)}, u32[]{:S(2)}, u32[]{:S(2)}) %collective-permute-start.62) | collective-permute-done | bytes 524320 | tf_op jit(solution)/shard_map/ppermute | solution.py:79
  167.2 12.1 %collective-permute-done.22 = bf16[128,2048]{1,0:T(8,128)(2,1)S(1)} collective-permute-done((bf16[128,2048]{1,0:T(8,128)(2,1)}, bf16[128,2048]{1,0:T(8,128)(2,1)S(1)}, u32[]{:S(2)}, u32[]{:S(2)}) %collective-permute-start.22) | collective-permute-done | bytes 524320 | tf_op jit(solution)/shard_map/ppermute | solution.py:83
  196.1 16.8 %collective-permute-done.20 = bf16[4,128,768]{2,1,0:T(8,128)(2,1)S(1)} collective-permute-done((bf16[4,128,768]{2,1,0:T(8,128)(2,1)S(1)}, bf16[4,128,768]{2,1,0:T(8,128)(2,1)S(1)}, u32[]{:S(2)}, u32[]{:S(2)}) %collective-permute-start.20) | collective-permute-done | bytes 786464 | tf_op jit(solution)/shard_map/ppermute | solution.py:83
  272.7 10.5 collective-permute-done.27
  285.3 27.5 %collective-permute-done.26 = bf16[128,2048]{1,0:T(8,128)(2,1)S(1)} collective-permute-done((bf16[128,2048]{1,0:T(8,128)(2,1)S(1)}, bf16[128,2048]{1,0:T(8,128)(2,1)S(1)}, u32[]{:S(2)}, u32[]{:S(2)}) %collective-permute-start.26) | collective-permute-done | bytes 524320 | tf_op jit(solution)/shard_map/ppermute | solution.py:79
  322.7 11.7 %collective-permute-done.28 = bf16[128,2048]{1,0:T(8,128)(2,1)S(1)} collective-permute-done((bf16[128,2048]{1,0:T(8,128)(2,1)S(1)}, bf16[128,2048]{1,0:T(8,128)(2,1)S(1)}, u32[]{:S(2)}, u32[]{:S(2)}) %collective-permute-start.28) | collective-permute-done | bytes 524320 | tf_op jit(solution)/shard_map/ppermute | solution.py:79
  334.5 21.3 %collective-permute-done.29 = bf16[128,2048]{1,0:T(8,128)(2,1)S(1)} collective-permute-done((bf16[128,2048]{1,0:T(8,128)(2,1)S(1)}, bf16[128,2048]{1,0:T(8,128)(2,1)S(1)}, u32[]{:S(2)}, u32[]{:S(2)}) %collective-permute-start.29) | collective-permute-done | bytes 524320 | tf_op jit(solution)/shard_map/ppermute | solution.py:79
  373.6 54.5 %collective-permute-done.51 = bf16[2048,384]{1,0:T(8,128)(2,1)} collective-permute-done((bf16[2048,384]{1,0:T(8,128)(2,1)}, bf16[2048,384]{1,0:T(8,128)(2,1)}, u32[]{:S(2)}, u32[]{:S(2)}) %collective-permute-start.51) | collective-permute-done | bytes 1572896 | tf_op jit(solution)/shard_map/ppermute | solution.py:83
  488.0 7.4 fusion.265
  509.6 15.8 %add_convert_fusion = bf16[1024,2048]{1,0:T(8,128)(2,1)S(1)} fusion(f32[1024,2048]{1,0:T(8,128)} %fusion.270, f32[1024,2048]{1,0:T(8,128)} %fusion.267, f32[1024,2048]{1,0:T(8,128)} %fusion.268, f32[1024,2048]{1,0:T(8,128)} %fusion.264, f32[1024,2048]{1,0:T(8,128)} %fusion.265, f32[1024,2048]{1,0:T(8,128)S(1)} %fusion.261, f32[1024,2048]{1,0:T(8,128)S(1)} %fusion.262, ...), kind=kOutput, calls=%fused_computation.8 | convolution fusion | flops 1627389952 | bytes 65273856 | tf_op jit(solution)/shard_map/dot_general | solution.py:40
  551.7 9.2 collective-permute-start.75
  562.6 12.3 %add_convert_fusion.1 = bf16[1024,2048]{1,0:T(8,128)(2,1)} fusion(f32[1024,2048]{1,0:T(8,128)} %fusion.258, f32[1024,2048]{1,0:T(8,128)S(1)} %fusion.254, f32[1024,2048]{1,0:T(8,128)} %fusion.256, bf16[1024,384]{0,1:T(8,128)(2,1)} %get-tuple-element.144, bf16[384,2048]{1,0:T(8,128)(2,1)} %copy-done.51), kind=kOutput, calls=%fused_computation.9 | convolution fusion | flops 1619001344 | bytes 31719424 | tf_op jit(solution)/shard_map/dot_general | solution.py:36
  581.2 33.2 %collective-permute-done.108 = bf16[2048,384]{0,1:T(8,128)(2,1)S(1)} collective-permute-done((bf16[2048,384]{0,1:T(8,128)(2,1)}, bf16[2048,384]{0,1:T(8,128)(2,1)S(1)}, u32[]{:S(2)}, u32[]{:S(2)}) %collective-permute-start.108) | collective-permute-done | bytes 1572896 | tf_op jit(solution)/shard_map/ppermute | solution.py:83
  627.6 11.1 %collective-permute-done.71 = bf16[128,2048]{1,0:T(8,128)(2,1)S(1)} collective-permute-done((bf16[128,2048]{1,0:T(8,128)(2,1)S(1)}, bf16[128,2048]{1,0:T(8,128)(2,1)S(1)}, u32[]{:S(2)}, u32[]{:S(2)}) %collective-permute-start.71) | collective-permute-done | bytes 524320 | tf_op jit(solution)/shard_map/ppermute | solution.py:79
  641.2 40.5 %collective-permute-done.70 = bf16[128,2048]{1,0:T(8,128)(2,1)S(1)} collective-permute-done((bf16[128,2048]{1,0:T(8,128)(2,1)S(1)}, bf16[128,2048]{1,0:T(8,128)(2,1)S(1)}, u32[]{:S(2)}, u32[]{:S(2)}) %collective-permute-start.70) | collective-permute-done | bytes 524320 | tf_op jit(solution)/shard_map/ppermute | solution.py:79
  686.1 28.7 %collective-permute-done.55 = bf16[128,2048]{1,0:T(8,128)(2,1)S(1)} collective-permute-done((bf16[128,2048]{1,0:T(8,128)(2,1)S(1)}, bf16[128,2048]{1,0:T(8,128)(2,1)S(1)}, u32[]{:S(2)}, u32[]{:S(2)}) %collective-permute-start.55) | collective-permute-done | bytes 524320 | tf_op jit(solution)/shard_map/ppermute | solution.py:79
  721.9 37.6 %collective-permute-done.58 = bf16[64,2048]{1,0:T(8,128)(2,1)S(1)} collective-permute-done((bf16[64,2048]{1,0:T(8,128)(2,1)S(1)}, bf16[64,2048]{1,0:T(8,128)(2,1)S(1)}, u32[]{:S(2)}, u32[]{:S(2)}) %collective-permute-start.58) | collective-permute-done | bytes 262176 | tf_op jit(solution)/shard_map/ppermute | solution.py:100
  760.5 7.2 collective-permute-start.115
  769.8 19.8 %collective-permute-start.76 = (bf16[128,2048]{1,0:T(8,128)(2,1)S(1)}, bf16[128,2048]{1,0:T(8,128)(2,1)S(1)}, u32[]{:S(2)}, u32[]{:S(2)}) collective-permute-start(bf16[128,2048]{1,0:T(8,128)(2,1)S(1)} %get-tuple-element.113), channel_id=1, source_target_pairs={{0,8},{1,9},{2,10},{3,11},{4,12},{5,13},{6,14},{7,15},{8,0},{9,1},... | collective-permute-start | bytes 1572872 | tf_op jit(solution)/shard_map/ppermute | solution.py:79
  808.0 24.5 %collective-permute-done.77 = bf16[128,2048]{1,0:T(8,128)(2,1)S(1)} collective-permute-done((bf16[128,2048]{1,0:T(8,128)(2,1)S(1)}, bf16[128,2048]{1,0:T(8,128)(2,1)S(1)}, u32[]{:S(2)}, u32[]{:S(2)}) %collective-permute-start.77) | collective-permute-done | bytes 524320 | tf_op jit(solution)/shard_map/ppermute | solution.py:79
  849.8 9.9 multiply_reduce_fusion
  859.7 13.4 %multiply_convert_fusion = (bf16[1024,1024]{0,1:T(8,128)(2,1)S(1)}, bf16[1024,1024]{0,1:T(8,128)(2,1)}, bf16[1024,1024]{0,1:T(8,128)(2,1)}, bf16[1024,1024]{0,1:T(8,128)(2,1)}) fusion(f32[1024,1024]{0,1:T(8,128)} %get-tuple-element.356, f32[1024,1024]{0,1:T(8,128)} %copy-done.7, f32[1024]{0:T(1024)S(1)} %get-tuple-element.93, f32[1024]{0:T(1024)S(1)} %copy-done.131, ...), kind=kLoop, calls=%fused_computation.13 | loop fusion | flops 26214400 | bytes 41979904 | tf_op jit(solution)/shard_map/convert_element_type | solution.py:371
  915.6 8.0 collective-permute-done.104
  925.9 13.7 %collective-permute-done.97 = bf16[4,128,768]{2,1,0:T(8,128)(2,1)S(1)} collective-permute-done((bf16[4,128,768]{2,1,0:T(8,128)(2,1)}, bf16[4,128,768]{2,1,0:T(8,128)(2,1)S(1)}, u32[]{:S(2)}, u32[]{:S(2)}) %collective-permute-start.97) | collective-permute-done | bytes 786464 | tf_op jit(solution)/shard_map/ppermute | solution.py:83
  979.5 11.4 %collective-permute-start.101 = (bf16[128,768]{1,0:T(8,128)(2,1)S(1)}, bf16[128,768]{1,0:T(8,128)(2,1)S(1)}, u32[]{:S(2)}, u32[]{:S(2)}) collective-permute-start(bf16[128,768]{1,0:T(8,128)(2,1)S(1)} %get-tuple-element.203), channel_id=1, source_target_pairs={{0,16},{1,17},{2,18},{3,19},{4,20},{5,21},{6,22},{7,23},{8,24},{9,... | collective-permute-start | bytes 589832 | tf_op jit(solution)/shard_map/ppermute | solution.py:79
  1015.7 9.2 collective-permute-done.86
  1024.9 30.1 %collective-permute-done.85 = bf16[128,2048]{1,0:T(8,128)(2,1)S(1)} collective-permute-done((bf16[128,2048]{1,0:T(8,128)(2,1)S(1)}, bf16[128,2048]{1,0:T(8,128)(2,1)S(1)}, u32[]{:S(2)}, u32[]{:S(2)}) %collective-permute-start.85) | collective-permute-done | bytes 524320 | tf_op jit(solution)/shard_map/ppermute | solution.py:79
  1082.9 9.2 collective-permute-done.88
  (869 shorter events, 515.1 us)
Async XLA Ops:
  2.9 163.8 %collective-permute-start.23 = (bf16[128,2048]{1,0:T(8,128)(2,1)}, bf16[128,2048]{1,0:T(8,128)(2,1)}, u32[]{:S(2)}, u32[]{:S(2)}) collective-permute-start(bf16[128,2048]{1,0:T(8,128)(2,1)} %slice_select_fusion.2), channel_id=1, source_target_pairs={{0,4},{1,5},{2,6},{3,7},{4,0},{5,1},{6,2},{7,3},{8,12},{9,13},{10,... | collective-permute-start | bytes 1572872 | tf_op jit(solution)/shard_map/ppermute | solution.py:83
  5.8 126.9 %collective-permute-start.21 = (bf16[128,2048]{1,0:T(8,128)(2,1)}, bf16[128,2048]{1,0:T(8,128)(2,1)}, u32[]{:S(2)}, u32[]{:S(2)}) collective-permute-start(bf16[128,2048]{1,0:T(8,128)(2,1)} %slice_select_fusion.2), channel_id=1, source_target_pairs={{0,2},{1,3},{2,0},{3,1},{4,6},{5,7},{6,4},{7,5},{8,10},{9,11},{10,... | collective-permute-start | bytes 1572872 | tf_op jit(solution)/shard_map/ppermute | solution.py:83
  114.8 48.2 %collective-permute-start.62 = (bf16[128,2048]{1,0:T(8,128)(2,1)S(1)}, bf16[128,2048]{1,0:T(8,128)(2,1)S(1)}, u32[]{:S(2)}, u32[]{:S(2)}) collective-permute-start(bf16[128,2048]{1,0:T(8,128)(2,1)S(1)} %bitcast.418), channel_id=1, source_target_pairs={{0,16},{1,17},{2,18},{3,19},{4,20},{5,21},{6,22},{7,23},{8,24},{9,... | collective-permute-start | bytes 1572872 | tf_op jit(solution)/shard_map/ppermute | solution.py:79
  132.7 52.1 %collective-permute-start.18 = (bf16[4,128,768]{2,1,0:T(8,128)(2,1)S(1)}, bf16[4,128,768]{2,1,0:T(8,128)(2,1)S(1)}, u32[]{:S(2)}, u32[]{:S(2)}) collective-permute-start(bf16[4,128,768]{2,1,0:T(8,128)(2,1)S(1)} %copy-done.64), channel_id=1, source_target_pairs={{0,2},{1,3},{2,0},{3,1},{4,6},{5,7},{6,4},{7,5},{8,10},{9,11},{10,... | collective-permute-start | bytes 2359304 | tf_op jit(solution)/shard_map/ppermute | solution.py:83
  187.5 66.5 %collective-permute-start.49 = (bf16[384,2048]{1,0:T(8,128)(2,1)}, bf16[384,2048]{1,0:T(8,128)(2,1)}, u32[]{:S(2)}, u32[]{:S(2)}) collective-permute-start(bf16[384,2048]{1,0:T(8,128)(2,1)} %select_bitcast_fusion), channel_id=1, source_target_pairs={{0,4},{1,5},{2,6},{3,7},{4,0},{5,1},{6,2},{7,3},{8,12},{9,13},{10,... | collective-permute-start | bytes 4718600 | tf_op jit(solution)/shard_map/ppermute | solution.py:83
  187.7 72.4 %collective-permute-start.46 = (bf16[384,2048]{1,0:T(8,128)(2,1)}, bf16[384,2048]{1,0:T(8,128)(2,1)}, u32[]{:S(2)}, u32[]{:S(2)}) collective-permute-start(bf16[384,2048]{1,0:T(8,128)(2,1)} %select_bitcast_fusion), channel_id=1, source_target_pairs={{0,2},{1,3},{2,0},{3,1},{4,6},{5,7},{6,4},{7,5},{8,10},{9,11},{10,... | collective-permute-start | bytes 4718600 | tf_op jit(solution)/shard_map/ppermute | solution.py:83
  189.3 168.5 %collective-permute-start.45 = (bf16[2048,384]{1,0:T(8,128)(2,1)}, bf16[2048,384]{1,0:T(8,128)(2,1)}, u32[]{:S(2)}, u32[]{:S(2)}) collective-permute-start(bf16[2048,384]{1,0:T(8,128)(2,1)} %slice_select_fusion), channel_id=1, source_target_pairs={{0,2},{1,3},{2,0},{3,1},{4,6},{5,7},{6,4},{7,5},{8,10},{9,11},{10,... | collective-permute-start | bytes 4718600 | tf_op jit(solution)/shard_map/ppermute | solution.py:83
  196.1 48.0 %collective-permute-start.66 = (bf16[128,2048]{1,0:T(8,128)(2,1)S(1)}, bf16[128,2048]{1,0:T(8,128)(2,1)}, u32[]{:S(2)}, u32[]{:S(2)}) collective-permute-start(bf16[128,2048]{1,0:T(8,128)(2,1)S(1)} %collective-permute-done.62), channel_id=1, source_target_pairs={{0,1},{1,0},{2,3},{3,2},{4,5},{5,4},{6,7},{7,6},{8,9},{9,8},{10,11... | collective-permute-start | bytes 1572872 | tf_op jit(solution)/shard_map/ppermute | solution.py:87
  254.0 60.2 %collective-permute-start.52 = (bf16[384,2048]{1,0:T(8,128)(2,1)}, bf16[384,2048]{1,0:T(8,128)(2,1)S(1)}, u32[]{:S(2)}, u32[]{:S(2)}) collective-permute-start(bf16[384,2048]{1,0:T(8,128)(2,1)} %collective-permute-done.49), channel_id=1, source_target_pairs={{0,2},{1,3},{2,0},{3,1},{4,6},{5,7},{6,4},{7,5},{8,10},{9,11},{10,... | collective-permute-start | bytes 4718600 | tf_op jit(solution)/shard_map/ppermute | solution.py:83
  283.2 76.0 %collective-permute-start.47 = (bf16[2048,384]{1,0:T(8,128)(2,1)S(1)}, bf16[2048,384]{1,0:T(8,128)(2,1)}, u32[]{:S(2)}, u32[]{:S(2)}) collective-permute-start(bf16[2048,384]{1,0:T(8,128)(2,1)S(1)} %copy-done.34), channel_id=1, source_target_pairs={{0,4},{1,5},{2,6},{3,7},{4,0},{5,1},{6,2},{7,3},{8,12},{9,13},{10,... | collective-permute-start | bytes 4718600 | tf_op jit(solution)/shard_map/ppermute | solution.py:83
  357.7 73.8 %collective-permute-start.48 = (bf16[2048,384]{1,0:T(8,128)(2,1)}, bf16[2048,384]{1,0:T(8,128)(2,1)}, u32[]{:S(2)}, u32[]{:S(2)}) collective-permute-start(bf16[2048,384]{1,0:T(8,128)(2,1)} %slice_select_fusion), channel_id=1, source_target_pairs={{0,4},{1,5},{2,6},{3,7},{4,0},{5,1},{6,2},{7,3},{8,12},{9,13},{10,... | collective-permute-start | bytes 4718600 | tf_op jit(solution)/shard_map/ppermute | solution.py:83
  357.9 92.1 %collective-permute-start.44 = (bf16[2048,384]{1,0:T(8,128)(2,1)S(1)}, bf16[2048,384]{1,0:T(8,128)(2,1)}, u32[]{:S(2)}, u32[]{:S(2)}) collective-permute-start(bf16[2048,384]{1,0:T(8,128)(2,1)S(1)} %copy-done.34), channel_id=1, source_target_pairs={{0,2},{1,3},{2,0},{3,1},{4,6},{5,7},{6,4},{7,5},{8,10},{9,11},{10,... | collective-permute-start | bytes 4718600 | tf_op jit(solution)/shard_map/ppermute | solution.py:83
  359.2 68.9 %collective-permute-start.51 = (bf16[2048,384]{1,0:T(8,128)(2,1)}, bf16[2048,384]{1,0:T(8,128)(2,1)}, u32[]{:S(2)}, u32[]{:S(2)}) collective-permute-start(bf16[2048,384]{1,0:T(8,128)(2,1)} %collective-permute-done.45), channel_id=1, source_target_pairs={{0,4},{1,5},{2,6},{3,7},{4,0},{5,1},{6,2},{7,3},{8,12},{9,13},{10,... | collective-permute-start | bytes 4718600 | tf_op jit(solution)/shard_map/ppermute | solution.py:83
  360.5 84.1 %collective-permute-start.50 = (bf16[2048,384]{1,0:T(8,128)(2,1)}, bf16[2048,384]{1,0:T(8,128)(2,1)}, u32[]{:S(2)}, u32[]{:S(2)}) collective-permute-start(bf16[2048,384]{1,0:T(8,128)(2,1)} %collective-permute-done.47), channel_id=1, source_target_pairs={{0,2},{1,3},{2,0},{3,1},{4,6},{5,7},{6,4},{7,5},{8,10},{9,11},{10,... | collective-permute-start | bytes 4718600 | tf_op jit(solution)/shard_map/ppermute | solution.py:83
  455.4 96.3 %collective-permute-start.72 = (f32[4,4,128]{2,0,1:T(4,128)S(1)}, f32[4,4,128]{2,0,1:T(4,128)S(1)}, u32[]{:S(2)}, u32[]{:S(2)}) collective-permute-start(f32[4,4,128]{2,0,1:T(4,128)S(1)} %slice_bitcast_fusion.37), channel_id=1, source_target_pairs={{0,1},{1,0},{2,3},{3,2},{4,5},{5,4},{6,7},{7,6},{8,9},{9,8},{10,11... | collective-permute-start | bytes 24584 | tf_op jit(solution)/shard_map/ppermute | solution.py:87
  527.0 93.8 %collective-permute-start.68 = (bf16[512,2048]{1,0:T(8,128)(2,1)}, bf16[512,2048]{1,0:T(8,128)(2,1)S(1)}, u32[]{:S(2)}, u32[]{:S(2)}) collective-permute-start(bf16[512,2048]{1,0:T(8,128)(2,1)} %slice.904), channel_id=1, source_target_pairs={{0,1},{1,0},{2,3},{3,2},{4,5},{5,4},{6,7},{7,6},{8,9},{9,8},{10,11... | collective-permute-start | bytes 6291464 | tf_op jit(solution)/shard_map/ppermute | solution.py:87
  576.9 48.6 %collective-permute-start.53 = (bf16[512,2048]{1,0:T(8,128)(2,1)S(1)}, bf16[512,2048]{1,0:T(8,128)(2,1)S(1)}, u32[]{:S(2)}, u32[]{:S(2)}) collective-permute-start(bf16[512,2048]{1,0:T(8,128)(2,1)S(1)} %slice.894), channel_id=1, source_target_pairs={{0,1},{1,0},{2,3},{3,2},{4,5},{5,4},{6,7},{7,6},{8,9},{9,8},{10,11... | collective-permute-start | bytes 6291464 | tf_op jit(solution)/shard_map/ppermute | solution.py:87
  577.4 190.3 %collective-permute-start.107 = (bf16[2048,384]{0,1:T(8,128)(2,1)}, bf16[2048,384]{0,1:T(8,128)(2,1)}, u32[]{:S(2)}, u32[]{:S(2)}) collective-permute-start(bf16[2048,384]{0,1:T(8,128)(2,1)} %convolution_convert_fusion.5), channel_id=1, source_target_pairs={{0,4},{1,5},{2,6},{3,7},{4,0},{5,1},{6,2},{7,3},{8,12},{9,13},{10,... | collective-permute-start | bytes 4718600 | tf_op jit(solution)/shard_map/ppermute | solution.py:83
  614.4 103.8 %collective-permute-start.116 = (bf16[384,2048]{1,0:T(8,128)(2,1)}, bf16[384,2048]{1,0:T(8,128)(2,1)S(1)}, u32[]{:S(2)}, u32[]{:S(2)}) collective-permute-start(bf16[384,2048]{1,0:T(8,128)(2,1)} %convolution_convert_fusion.6), channel_id=1, source_target_pairs={{0,4},{1,5},{2,6},{3,7},{4,0},{5,1},{6,2},{7,3},{8,12},{9,13},{10,... | collective-permute-start | bytes 4718600 | tf_op jit(solution)/shard_map/ppermute | solution.py:83
  624.4 57.2 %collective-permute-start.70 = (bf16[128,2048]{1,0:T(8,128)(2,1)S(1)}, bf16[128,2048]{1,0:T(8,128)(2,1)S(1)}, u32[]{:S(2)}, u32[]{:S(2)}) collective-permute-start(bf16[128,2048]{1,0:T(8,128)(2,1)S(1)} %get-tuple-element.169), channel_id=1, source_target_pairs={{0,16},{1,17},{2,18},{3,19},{4,20},{5,21},{6,22},{7,23},{8,24},{9,... | collective-permute-start | bytes 1572872 | tf_op jit(solution)/shard_map/ppermute | solution.py:79
  625.5 56.2 %collective-permute-start.69 = (bf16[128,2048]{1,0:T(8,128)(2,1)S(1)}, bf16[128,2048]{1,0:T(8,128)(2,1)S(1)}, u32[]{:S(2)}, u32[]{:S(2)}) collective-permute-start(bf16[128,2048]{1,0:T(8,128)(2,1)S(1)} %get-tuple-element.167), channel_id=1, source_target_pairs={{0,8},{1,9},{2,10},{3,11},{4,12},{5,13},{6,14},{7,15},{8,0},{9,1},... | collective-permute-start | bytes 1572872 | tf_op jit(solution)/shard_map/ppermute | solution.py:79
  638.8 46.5 %collective-permute-start.56 = (bf16[128,2048]{1,0:T(8,128)(2,1)S(1)}, bf16[128,2048]{1,0:T(8,128)(2,1)S(1)}, u32[]{:S(2)}, u32[]{:S(2)}) collective-permute-start(bf16[128,2048]{1,0:T(8,128)(2,1)S(1)} %get-tuple-element.171), channel_id=1, source_target_pairs={{0,24},{1,25},{2,26},{3,27},{4,28},{5,29},{6,30},{7,31},{8,16},{9,... | collective-permute-start | bytes 1572872 | tf_op jit(solution)/shard_map/ppermute | solution.py:79
  685.3 109.0 %collective-permute-start.111 = (bf16[2048,384]{0,1:T(8,128)(2,1)S(1)}, bf16[2048,384]{0,1:T(8,128)(2,1)S(1)}, u32[]{:S(2)}, u32[]{:S(2)}) collective-permute-start(bf16[2048,384]{0,1:T(8,128)(2,1)S(1)} %copy-done.156), channel_id=1, source_target_pairs={{0,2},{1,3},{2,0},{3,1},{4,6},{5,7},{6,4},{7,5},{8,10},{9,11},{10,... | collective-permute-start | bytes 4718600 | tf_op jit(solution)/shard_map/ppermute | solution.py:83
  714.8 55.0 %collective-permute-start.109 = (bf16[2048,384]{0,1:T(8,128)(2,1)}, bf16[2048,384]{0,1:T(8,128)(2,1)S(1)}, u32[]{:S(2)}, u32[]{:S(2)}) collective-permute-start(bf16[2048,384]{0,1:T(8,128)(2,1)} %add_convert_fusion.7), channel_id=1, source_target_pairs={{0,2},{1,3},{2,0},{3,1},{4,6},{5,7},{6,4},{7,5},{8,10},{9,11},{10,... | collective-permute-start | bytes 4718600 | tf_op jit(solution)/shard_map/ppermute | solution.py:83
  716.4 79.0 %collective-permute-start.113 = (bf16[2048,384]{0,1:T(8,128)(2,1)}, bf16[2048,384]{0,1:T(8,128)(2,1)S(1)}, u32[]{:S(2)}, u32[]{:S(2)}) collective-permute-start(bf16[2048,384]{0,1:T(8,128)(2,1)} %add_convert_fusion.5), channel_id=1, source_target_pairs={{0,4},{1,5},{2,6},{3,7},{4,0},{5,1},{6,2},{7,3},{8,12},{9,13},{10,... | collective-permute-start | bytes 4718600 | tf_op jit(solution)/shard_map/ppermute | solution.py:83
  804.3 140.1 %collective-permute-start.110 = (bf16[2048,384]{0,1:T(8,128)(2,1)}, bf16[2048,384]{0,1:T(8,128)(2,1)}, u32[]{:S(2)}, u32[]{:S(2)}) collective-permute-start(bf16[2048,384]{0,1:T(8,128)(2,1)} %add_convert_fusion.6), channel_id=1, source_target_pairs={{0,1},{1,0},{2,3},{3,2},{4,5},{5,4},{6,7},{7,6},{8,9},{9,8},{10,11... | collective-permute-start | bytes 4718600 | tf_op jit(solution)/shard_map/ppermute | solution.py:87
  808.0 148.4 %collective-permute-start.114 = (bf16[2048,384]{0,1:T(8,128)(2,1)}, bf16[2048,384]{0,1:T(8,128)(2,1)}, u32[]{:S(2)}, u32[]{:S(2)}) collective-permute-start(bf16[2048,384]{0,1:T(8,128)(2,1)} %add_convert_fusion.4), channel_id=1, source_target_pairs={{0,1},{1,0},{2,3},{3,2},{4,5},{5,4},{6,7},{7,6},{8,9},{9,8},{10,11... | collective-permute-start | bytes 4718600 | tf_op jit(solution)/shard_map/ppermute | solution.py:87
  834.4 134.8 %collective-permute-start.118 = (bf16[384,2048]{1,0:T(8,128)(2,1)}, bf16[384,2048]{1,0:T(8,128)(2,1)}, u32[]{:S(2)}, u32[]{:S(2)}) collective-permute-start(bf16[384,2048]{1,0:T(8,128)(2,1)} %add_convert_fusion.2), channel_id=1, source_target_pairs={{0,1},{1,0},{2,3},{3,2},{4,5},{5,4},{6,7},{7,6},{8,9},{9,8},{10,11... | collective-permute-start | bytes 4718600 | tf_op jit(solution)/shard_map/ppermute | solution.py:87
  923.6 83.4 %collective-permute-start.83 = (bf16[512,2048]{1,0:T(8,128)(2,1)}, bf16[512,2048]{1,0:T(8,128)(2,1)S(1)}, u32[]{:S(2)}, u32[]{:S(2)}) collective-permute-start(bf16[512,2048]{1,0:T(8,128)(2,1)} %slice.938), channel_id=1, source_target_pairs={{0,1},{1,0},{2,3},{3,2},{4,5},{5,4},{6,7},{7,6},{8,9},{9,8},{10,11... | collective-permute-start | bytes 6291464 | tf_op jit(solution)/shard_map/ppermute | solution.py:87
  1009.6 45.4 %collective-permute-start.85 = (bf16[128,2048]{1,0:T(8,128)(2,1)S(1)}, bf16[128,2048]{1,0:T(8,128)(2,1)S(1)}, u32[]{:S(2)}, u32[]{:S(2)}) collective-permute-start(bf16[128,2048]{1,0:T(8,128)(2,1)S(1)} %get-tuple-element.166), channel_id=1, source_target_pairs={{0,16},{1,17},{2,18},{3,19},{4,20},{5,21},{6,22},{7,23},{8,24},{9,... | collective-permute-start | bytes 1572872 | tf_op jit(solution)/shard_map/ppermute | solution.py:79
  1010.3 44.7 %collective-permute-start.84 = (bf16[128,2048]{1,0:T(8,128)(2,1)S(1)}, bf16[128,2048]{1,0:T(8,128)(2,1)S(1)}, u32[]{:S(2)}, u32[]{:S(2)}) collective-permute-start(bf16[128,2048]{1,0:T(8,128)(2,1)S(1)} %get-tuple-element.164), channel_id=1, source_target_pairs={{0,8},{1,9},{2,10},{3,11},{4,12},{5,13},{6,14},{7,15},{8,0},{9,1},... | collective-permute-start | bytes 1572872 | tf_op jit(solution)/shard_map/ppermute | solution.py:79
  1014.1 79.2 %collective-permute-start.102 = (f32[4,128,768]{2,1,0:T(8,128)}, f32[4,128,768]{2,1,0:T(8,128)}, u32[]{:S(2)}, u32[]{:S(2)}) collective-permute-start(f32[4,128,768]{2,1,0:T(8,128)} %maximum_select_fusion.11), channel_id=1, source_target_pairs={{0,1},{1,0},{2,3},{3,2},{4,5},{5,4},{6,7},{7,6},{8,9},{9,8},{10,11... | collective-permute-start | bytes 4718600 | tf_op jit(solution)/shard_map/ppermute | solution.py:87
  (249 other events, 5093.5 us)

commit v2 on v1

v2 whole, which is shorter than its diff:
```python
import math

import jax
import jax.numpy as jnp
from jax import lax
from jax.sharding import PartitionSpec as P

BLOCK = 256
SEQ = 1024
EPS = 1e-06
THETA = 1000000.0
NEGATIVE = -1e30
AXES = ("grp", "rep")
LINES = 4
LANES = 64
F32 = jnp.float32
BF16 = jnp.bfloat16


def row_scale(values):
    return lax.rsqrt(jnp.mean(values * values, axis=-1, keepdims=True) + EPS)


def norm_back(grad, values, factor, gain):
    inner = grad * gain
    back = factor * inner - values * factor**3 * jnp.mean(inner * values, axis=-1, keepdims=True)
    return (back, grad * values * factor)


def rotate(values, cosine, sine):
    half = values.shape[-1] // 2
    first, second = values[..., :half], values[..., half:]
    return jnp.concatenate([first * cosine - second * sine, second * cosine + first * sine], axis=-1)


def dot(left, right):
    return lax.dot_general(left, right, (((1,), (0,)), ((), ())), preferred_element_type=F32)


def dot_out(left, right):
    return lax.dot_general(left, right, (((1,), (1,)), ((), ())), preferred_element_type=F32)


def dot_rows(left, right):
    return lax.dot_general(left, right, (((0,), (0,)), ((), ())), preferred_element_type=F32)


def flip_bit(values, axis, bit):
    count = values.shape[axis]
    pieces = [lax.slice_in_dim(values, i, i + bit, axis=axis) for i in range(0, count, bit)]
    order = [i ^ 1 for i in range(len(pieces))]
    return jnp.concatenate([pieces[i] for i in order], axis=axis)


def xor_order(values, axis, mine):
    bit = 1
    while bit < values.shape[axis]:
        values = jnp.where((mine & bit) != 0, flip_bit(values, axis, bit), values)
        bit *= 2
    return values


def build(groups, reps):
    columns = groups // LINES

    def mover(target):
        table = [
            (g * reps + r, target(g, r)[0] * reps + target(g, r)[1])
            for g in range(groups)
            for r in range(reps)
        ]
        back = [(b, a) for a, b in table]
        return (
            lambda v: lax.ppermute(v, AXES, table),
            lambda v: lax.ppermute(v, AXES, back),
        )

    def home(k):
        def target(g, r):
            sequence, block = g // 16, g % 16
            column = (sequence * 2 + r % 2) * 2 + (k ^ (g & 1))
            return ((block // 4) * columns + column, (r // 2) * 2 + (block // 2) % 2)

        return mover(target)

    def line(k):
        return mover(lambda g, r: (((g // columns) ^ k) * columns + g % columns, r))[0]

    return dict(
        columns=columns,
        line=[None] + [line(k) for k in range(1, LINES)],
        plane=[None] + [mover(lambda g, r, k=k: (g ^ k, r))[0] for k in range(1, columns)],
        core=mover(lambda g, r: (g, r ^ 1))[0],
        replicas=[mover(lambda g, r, k=k: (g, r ^ (2 * k)))[0] for k in range(1, reps // 2)],
        home=[home(0), home(1)],
    )


def split_tail(values):
    high = lax.reduce_precision(values, 8, 7)
    return jnp.concatenate([high, values - high], axis=1).astype(BF16)


def per_device(
    layer_input,
    out_grad,
    routes,
    norm_in,
    query_weight,
    key_weight,
    value_weight,
    query_gain,
    key_gain,
    out_weight,
    norm_mid,
    router,
    expert_gate,
    expert_up,
    expert_down,
):
    groups, reps = lax.axis_size("grp"), lax.axis_size("rep")
    mv = build(groups, reps)
    columns, line, plane, to_core = mv["columns"], mv["line"], mv["plane"], mv["core"]
    sharing = columns // 2
    g, r = lax.axis_index("grp"), lax.axis_index("rep")
    tz, gc, core = g // columns, g % columns, r % 2
    odd = (g & 1) != 0
    batches, tokens, width = layer_input.shape[1:]
    experts = groups
    piece = width // groups
    head = query_gain.shape[0] * groups
    heads = query_weight.shape[1] // head
    kv_heads = key_weight.shape[1] // head
    local_heads = heads // (2 * kv_heads)
    q_width = local_heads * head
    scale = 1.0 / math.sqrt(head)
    hidden = expert_gate.shape[2] // 2
    rows = batches * tokens
    total = 2 * LINES * rows

    def bring(values):
        values = jnp.where(odd, values[::-1], values)
        got = jnp.stack([mv["home"][k][0](values[k]) for k in range(2)])
        return jnp.where(odd, got[::-1], got).reshape((rows,) + values.shape[2:])

    def take_back(values):
        values = values.reshape((2, tokens) + values.shape[1:])
        values = jnp.where(odd, values[::-1], values)
        got = jnp.stack([mv["home"][k][1](values[k]) for k in range(2)])
        return jnp.where(odd, got[::-1], got)

    def line_parts(values):
        first, second = line[1](values), line[2](values)
        return [values, first, second, line[1](second)]

    def gather_tokens(values):
        half = jnp.concatenate(line_parts(values))
        return jnp.concatenate([half, to_core(half)])

    def gather_shared(values):
        parts = []
        for part in line_parts(values):
            parts += [part] + [plane[2 * u](part) for u in range(1, sharing)]
        half = jnp.concatenate(parts)
        return jnp.concatenate([half, to_core(half)])

    def scatter_line(blocks):
        third = line[1](blocks[3].astype(BF16)).astype(F32)
        second = line[2]((blocks[2] + third).astype(BF16)).astype(F32)
        return blocks[0] + line[1](blocks[1].astype(BF16)).astype(F32) + second

    def scatter_tokens(partial):
        half = total // 2
        both = partial[:half].astype(F32) + to_core(partial[half:]).astype(F32)
        return scatter_line([both[k * rows : (k + 1) * rows] for k in range(LINES)])

    def scatter_shared(partial, tail=False):
        half = partial.shape[0] // 2
        both = partial[:half].astype(F32) + to_core(partial[half:]).astype(F32)
        if tail:
            body, extra = both[:, :width], both[:, width:]
            extra = extra[:, :LANES] + extra[:, LANES:]
            low = jnp.concatenate([body.astype(BF16), split_tail(extra)], axis=1)
        else:
            low = both.astype(BF16)
        blocks = []
        for k in range(LINES):
            at = [low[(k * sharing + u) * rows :][:rows] for u in range(sharing)]
            block = at[0].astype(F32)
            for u in range(1, sharing):
                block = block + plane[2 * u](at[u]).astype(F32)
            blocks.append(block)
        return scatter_line(blocks)

    named = (routes[0][..., None] == jnp.arange(experts, dtype=jnp.int32)).any(axis=2)
    named = jnp.pad(named.astype(BF16), ((0, 0), (0, 0), (0, 2 * LANES - experts)))
    brought = bring(jnp.concatenate([layer_input[0], out_grad[0], named], axis=2))
    inputs = brought[:, :width].astype(F32)
    grad_out = brought[:, width : 2 * width].astype(F32)
    named = brought[:, 2 * width :]

    def to_slots(values):
        pieces = [values[:, i * piece : (i + 1) * piece] for i in range(groups)]
        by_slot = [pieces[t * columns + s] for s in range(columns) for t in range(LINES)]
        whole = jnp.stack(by_slot).reshape(columns, LINES, values.shape[0], piece)
        whole = xor_order(whole, 0, gc)
        return jnp.concatenate([whole[s, t] for s in range(columns) for t in range(LINES)], axis=1)

    def from_slots(values):
        count = LINES * piece
        whole = jnp.stack([values[:, s * count : (s + 1) * count] for s in range(columns)])
        whole = xor_order(whole, 0, gc)
        return jnp.concatenate(
            [
                whole[s, :, t * piece : (t + 1) * piece]
                for t in range(LINES)
                for s in range(columns)
            ],
            axis=1,
        )

    gathered = gather_tokens(to_slots(brought[:, :width]))

    per_q = query_weight.reshape(piece, kv_heads, local_heads, 2, head)
    own_q = jnp.where(core == 0, per_q[:, :, :, 0], per_q[:, :, :, 1]).reshape(
        piece, kv_heads, q_width
    )
    qkv = jnp.concatenate(
        [
            own_q,
            key_weight.reshape(piece, kv_heads, head),
            value_weight.reshape(piece, kv_heads, head),
        ],
        axis=2,
    ).transpose(1, 0, 2)
    rel = xor_order(qkv, 0, tz)
    rel = jnp.stack([rel[0]] + [line[k](rel[k]) for k in range(1, LINES)])
    qkv = xor_order(rel, 0, tz).reshape(LINES * piece, -1)
    w_qkv = jnp.concatenate([qkv] + [plane[s](qkv) for s in range(1, columns)])

    gains = jnp.concatenate([query_gain, key_gain])
    packed = jnp.concatenate(
        [
            norm_in[None],
            norm_mid[None],
            router.T,
            jnp.pad(gains, (0, piece - gains.shape[0]))[None],
        ]
    )[None]
    for bit in (b for b in (1, 2, 4, 8) if b < columns):
        packed = jnp.concatenate([packed, plane[bit](packed)])
    packed = packed[None]
    for bit in (1, 2):
        packed = jnp.concatenate([packed, line[bit](packed)])
    packed = xor_order(xor_order(packed, 0, tz), 1, gc).reshape(groups, experts + 3, piece)
    small = packed[:, : experts + 2].transpose(1, 0, 2).reshape(experts + 2, width)
    gain_in, gain_mid = small[:1].astype(F32), small[1:2].astype(F32)
    router_t = small[2:]
    part = head // groups
    gain_q = packed[:, experts + 2, :part].reshape(head).astype(F32)
    gain_k = packed[:, experts + 2, part : 2 * part].reshape(head).astype(F32)

    out_heads = out_weight.shape[0] // head
    own_out = out_weight
    if out_heads == 2:
        own_out = jnp.where(core == 0, out_weight[:head], out_weight[head:])
    w_out = jnp.stack([own_out] + [plane[s](own_out) for s in range(1, columns)])
    w_out = xor_order(w_out, 0, gc)
    if out_heads == 1:
        w_out = w_out.reshape(local_heads, 2, head, width)
        w_out = jnp.where(core == 0, w_out[:, 0], w_out[:, 1])
    w_out = w_out.reshape(q_width, width)

    def half_of(values, axis):
        low = lax.slice_in_dim(values, 0, hidden, axis=axis)
        high = lax.slice_in_dim(values, hidden, 2 * hidden, axis=axis)
        return jnp.where(core == 0, low, high)

    w_own = jnp.concatenate(
        [half_of(expert_gate[0], 1), half_of(expert_up[0], 1), half_of(expert_down[0], 0).T],
        axis=1,
    )
    w_experts = [w_own, plane[1](w_own)]
    expert_ids = [tz * columns + gc, tz * columns + (gc ^ 1)]

    which = jnp.arange(total, dtype=jnp.int32)
    side, block, inner = which // (LINES * rows), which // rows % LINES, which % rows
    position = ((block ^ tz) * 2 + (side ^ core)) * rows + inner
    block = position // BLOCK
    visible = block[None, :] <= block[:, None]
    inverse = THETA ** (-(jnp.arange(head // 2, dtype=F32) * 2.0 / head))
    angle = position.astype(F32)[:, None] * inverse[None, :]
    cosine, sine = jnp.cos(angle), jnp.sin(angle)

    gathered_f = gathered.astype(F32)
    a1 = (gathered_f * row_scale(gathered_f) * to_slots(gain_in)).astype(BF16)
    pre = dot(a1, w_qkv)
    query_pre = [pre[:, i * head : (i + 1) * head] for i in range(local_heads)]
    key_pre = pre[:, q_width : q_width + head]
    value_low = pre[:, q_width + head :].astype(BF16)
    query_scale = [row_scale(v) for v in query_pre]
    key_scale = row_scale(key_pre)
    query_rot = [
        rotate(v * s * gain_q, cosine, sine).astype(BF16) for v, s in zip(query_pre, query_scale)
    ]
    key_rot = rotate(key_pre * key_scale * gain_k, cosine, sine).astype(BF16)
    attended, probs_low, log_totals = [], [], []
    for i in range(local_heads):
        scores = jnp.where(visible, dot_out(query_rot[i], key_rot) * scale, NEGATIVE)
        peak = jnp.max(scores, axis=-1, keepdims=True)
        expo = jnp.exp(scores - peak)
        mass = jnp.sum(expo, axis=-1, keepdims=True)
        log_totals.append(peak + jnp.log(mass))
        low = (expo / mass).astype(BF16)
        probs_low.append(low)
        attended.append(dot(low, value_low).astype(BF16))
    attended = jnp.concatenate(attended, axis=1)
    mid = inputs + scatter_tokens(dot(attended, w_out).astype(BF16))
    scale_mid = row_scale(mid)
    low_mid = (mid * scale_mid * gain_mid).astype(BF16)

    dyx = gather_shared(brought[:, width:])
    dy, named_all = dyx[:, :width], dyx[:, width : width + experts]
    a2 = gather_shared(low_mid)

    def gates_of(rows_low, mask):
        logits = jnp.where(mask > 0, dot_out(rows_low, router_t), NEGATIVE)
        return jax.nn.softmax(logits, axis=-1)

    gates_own = gates_of(low_mid, named[:, :experts])
    gates_all = gates_of(a2, named_all)
    lanes = jnp.arange(experts, dtype=jnp.int32)[None, :]
    spread = jnp.zeros((a2.shape[0], LANES), F32)
    mixed, pair_lows = [], []
    for w, expert in zip(w_experts, expert_ids):
        weight = jnp.sum(jnp.where(lanes == expert, gates_all, 0.0), axis=1, keepdims=True)
        both = dot(a2, w[:, : 2 * hidden])
        gate_pre, up_pre = both[:, :hidden], both[:, hidden:]
        back = dot(dy, w[:, 2 * hidden :])
        sigmoid = jax.nn.sigmoid(gate_pre)
        silu = gate_pre * sigmoid
        made = silu * up_pre
        gate_grad = jnp.sum(made * back, axis=1, keepdims=True)
        spread = jnp.where(jnp.arange(LANES)[None, :] == expert, gate_grad, spread)
        mixed.append((made * weight).astype(BF16))
        made_grad = back * weight
        pair_lows.append(
            jnp.concatenate(
                [
                    made_grad * up_pre * sigmoid * (1.0 + gate_pre * (1.0 - sigmoid)),
                    made_grad * silu,
                ],
                axis=1,
            ).astype(BF16)
        )
    rows_back = sum(dot_out(p, w[:, : 2 * hidden]) for p, w in zip(pair_lows, w_experts))
    rows_back = jnp.concatenate([rows_back.astype(BF16), split_tail(spread)], axis=1)
    came_back = scatter_shared(rows_back, tail=True)
    rows_out = sum(dot_out(m, w[:, 2 * hidden :]) for m, w in zip(mixed, w_experts))
    layer_out = (mid + scatter_shared(rows_out.astype(BF16))).astype(BF16)

    expert_part = came_back[:, :width]
    gate_grad = came_back[:, width : width + experts] + came_back[:, width + LANES :][:, :experts]
    pick_grad = gates_own * (gate_grad - jnp.sum(gates_own * gate_grad, axis=-1, keepdims=True))
    logit_low = pick_grad.astype(BF16)
    router_part = dot_rows(logit_low, low_mid)
    normed_mid_grad = expert_part + dot(logit_low, router_t)
    mid_back, mid_gain_part = norm_back(normed_mid_grad, mid, scale_mid, gain_mid)
    mid_grad = mid_back + grad_out

    branch = gather_tokens(mid_grad.astype(BF16))
    att_grad = dot_out(branch, w_out).astype(BF16)
    key_grad = jnp.zeros((total, head), F32)
    value_grad = jnp.zeros((total, head), F32)
    query_lows = []
    query_gain_part = jnp.zeros((head,), F32)
    for i in range(local_heads):
        grad_i = att_grad[:, i * head : (i + 1) * head]
        scores = dot_out(query_rot[i], key_rot) * scale
        probs = jnp.where(visible, jnp.exp(scores - log_totals[i]), 0.0)
        prob_grad = dot_out(grad_i, value_low)
        score_low = (
            probs * (prob_grad - jnp.sum(probs * prob_grad, axis=-1, keepdims=True))
        ).astype(BF16)
        query_grad = dot(score_low, key_rot) * scale
        key_grad = key_grad + dot_rows(score_low, query_rot[i]) * scale
        value_grad = value_grad + dot_rows(probs_low[i], grad_i)
        query_back, gain_part = norm_back(
            rotate(query_grad, cosine, -sine), query_pre[i], query_scale[i], gain_q
        )
        query_lows.append(query_back.astype(BF16))
        query_gain_part = query_gain_part + jnp.sum(gain_part, axis=0)
    key_back, key_gain_part = norm_back(rotate(key_grad, cosine, -sine), key_pre, key_scale, gain_k)
    qkv_low = jnp.concatenate(
        query_lows + [key_back.astype(BF16), value_grad.astype(BF16)], axis=1
    )
    normed_grad = from_slots(scatter_tokens(dot_out(qkv_low, w_qkv).astype(BF16)))
    in_back, in_gain_part = norm_back(normed_grad, inputs, row_scale(inputs), gain_in)
    input_grad = mid_grad + in_back

    def over_replicas(values):
        low = values.astype(BF16)
        return values + sum(move(low).astype(F32) for move in mv["replicas"])

    def whole(values, axis):
        other = to_core(values)
        return jnp.where(
            core == 0,
            jnp.concatenate([values, other], axis=axis),
            jnp.concatenate([other, values], axis=axis),
        ).astype(F32)

    def scatter_plane(stacked):
        for bit in [b for b in (8, 4, 2, 1) if b < columns]:
            got = plane[bit](stacked[bit : 2 * bit].astype(BF16))
            stacked = stacked[:bit].astype(F32) + got.astype(F32)
        return over_replicas(stacked[0])

    expert_grads = [
        jnp.concatenate([dot_rows(a2, p), dot_rows(dy, m)], axis=1)
        for p, m in zip(pair_lows, mixed)
    ]
    expert_sum = expert_grads[0] + plane[1](expert_grads[1].astype(BF16)).astype(F32)
    expert_sum = over_replicas(expert_sum).astype(BF16)
    gate_total = whole(expert_sum[:, :hidden], 1)
    up_total = whole(expert_sum[:, hidden : 2 * hidden], 1)
    down_total = whole(expert_sum[:, 2 * hidden :].T, 0)

    out_parts = dot_rows(attended, branch).reshape(local_heads, head, width)
    if out_heads == 2:
        out_total = whole(scatter_plane(xor_order(out_parts, 0, gc)), 0)
    else:
        zeros = jnp.zeros_like(out_parts)
        spaced = jnp.where(
            core == 0, jnp.stack([out_parts, zeros], 1), jnp.stack([zeros, out_parts], 1)
        )
        out_total = scatter_plane(xor_order(spaced.reshape(columns, head, width), 0, gc))
        out_total = out_total + to_core(out_total)

    w_part = scatter_plane(dot_rows(a1, qkv_low).reshape(columns, LINES * piece, -1))
    rel = xor_order(w_part.reshape(LINES, piece, -1), 0, tz)
    rel_low = rel.astype(BF16)
    rel = jnp.stack([rel[0]] + [line[k](rel_low[k]).astype(F32) for k in range(1, LINES)])
    mine = xor_order(rel, 0, tz)
    other = to_core(mine)
    low, high = jnp.where(core == 0, mine, other), jnp.where(core == 0, other, mine)
    query_total = jnp.stack(
        [v[..., :q_width].reshape(kv_heads, piece, local_heads, head) for v in (low, high)], axis=3
    )
    query_total = query_total.transpose(1, 0, 2, 3, 4).reshape(piece, heads * head)
    summed = low + high
    key_total = summed[..., q_width : q_width + head].transpose(1, 0, 2).reshape(piece, -1)
    value_total = summed[..., q_width + head :].transpose(1, 0, 2).reshape(piece, -1)

    small_part = jnp.concatenate(
        [
            jnp.sum(in_gain_part, axis=0)[None],
            jnp.sum(mid_gain_part, axis=0)[None],
            router_part,
        ]
    )
    small_part = small_part.reshape(experts + 2, groups, piece).transpose(1, 0, 2)
    gain_parts = jnp.stack(
        [query_gain_part.reshape(groups, part), jnp.sum(key_gain_part, axis=0).reshape(groups, part)],
        axis=1,
    ).reshape(groups, 2 * part)
    gain_parts = jnp.pad(gain_parts, ((0, 0), (0, piece - 2 * part)))[:, None]
    small_part = jnp.concatenate([small_part, gain_parts], axis=1)
    small_part = small_part.reshape(LINES, columns, experts + 3, piece)
    small_part = xor_order(xor_order(small_part, 0, tz), 1, gc)
    small_part = small_part + to_core(small_part)
    for bit in (2, 1):
        small_part = small_part[:bit] + line[bit](small_part[bit : 2 * bit])
    small_part = small_part[0]
    for bit in [b for b in (8, 4, 2, 1) if b < columns]:
        small_part = small_part[:bit] + plane[bit](small_part[bit : 2 * bit])
    small_part = small_part[0]
    small_part = small_part + sum(move(small_part) for move in mv["replicas"])

    return (
        take_back(layer_out)[None],
        take_back(input_grad)[None],
        small_part[0],
        query_total,
        key_total,
        value_total,
        small_part[experts + 2, :part],
        small_part[experts + 2, part : 2 * part],
        out_total,
        small_part[1],
        small_part[2 : experts + 2].T,
        gate_total[None],
        up_total[None],
        down_total[None],
    )


def solution(mesh):
    tokens = P("rep", None, "grp", None)
    rows = P("grp", None)
    vector = P("grp")
    stacked = P("grp", None, None)
    return jax.shard_map(
        per_device,
        mesh=mesh,
        in_specs=(
            tokens,
            tokens,
            tokens,
            vector,
            rows,
            rows,
            rows,
            vector,
            vector,
            rows,
            vector,
            rows,
            stacked,
            stacked,
            stacked,
        ),
        out_specs=(
            tokens,
            tokens,
            vector,
            rows,
            rows,
            rows,
            vector,
            vector,
            rows,
            vector,
            rows,
            stacked,
            stacked,
            stacked,
        ),
        check_vma=False,
    )
```

time: 1120 us -> 1040 us (0.929)
  starting transfers between devices: 184 us -> 87.6 us
  local copies, waits for them, and re-layouts: 68.8 us -> 144 us
  matrix products: 237 us -> 180 us
  other arithmetic: 111 us -> 146 us
  waiting for transfers between devices: 503 us -> 470 us
    ppermute x119 -> x86, starting transfers between devices: 184 us -> 87.6 us  [the longest x82 80.8 us: mover(): lax.ppermute(v, AXES, table)]
    concatenate x11 -> x13, local copies, waits for them, and re-layouts: 6.22 us -> 42.2 us  [the longest x1 13.8 us: per_device(): jnp.concatenate([rows_back.astype(BF16), split_tail(spread)], axis=1)]
    ppermute x119 -> x86, waiting for transfers between devices: 503 us -> 470 us  [the longest x82 461 us: mover(): lax.ppermute(v, AXES, table)]
    dot_general x24 -> x16, matrix products: 108 us -> 80.4 us  [dot_out(): lax.dot_general(left, right, (((1,), (1,)), ((), ())), preferred_element_...]
    unnamed x365 -> x424, local copies, waits for them, and re-layouts: 33.7 us -> 61.4 us
    dot_general x23 -> x15, matrix products: 77.2 us -> 51.9 us  [dot(): lax.dot_general(left, right, (((1,), (0,)), ((), ())), preferred_element_...]
    convert_element_type x9 -> x10, other arithmetic: 7.44 us -> 23.8 us  [the longest x1 8.29 us: per_device(): expert_sum = over_replicas(expert_sum).astype(BF16)]
    slice x10 -> x19, local copies, waits for them, and re-layouts: 8.89 us -> 21.2 us  [the longest x2 7.36 us: scatter_shared(): both = partial[:half].astype(F32) + to_core(partial[half:]).astype(F32)]
  transfers between devices with their start and end apart: 119 -> 86, of which waited for: 42 -> 42; matrix products, arithmetic and copies ran while one was open for 34% -> 28% of each run, Pallas kernels for 0% -> 0%
where the time goes in v2:
time: 1040 us; the launch traced here: 1030 us
  waiting for transfers between devices  470 us (45%)
  matrix products  180 us (17%)
  other arithmetic  146 us (14%)
  local copies, waits for them, and re-layouts  144 us (14%)
  starting transfers between devices  87.6 us (8%)
    ppermute x82, waiting for transfers between devices, mover(): lax.ppermute(v, AXES, table)  461 us
    ppermute x82, starting transfers between devices, mover(): lax.ppermute(v, AXES, table)  80.8 us
    dot_general x16, matrix products, dot_out(): lax.dot_general(left, right, (((1,), (1,)), ((), ())), preferred_element_...  80.4 us
    unnamed x424, local copies, waits for them, and re-layouts  61.4 us
    dot_general x15, matrix products, dot(): lax.dot_general(left, right, (((1,), (0,)), ((), ())), preferred_element_...  51.9 us
    dot_general x15, matrix products, dot_rows(): lax.dot_general(left, right, (((0,), (0,)), ((), ())), preferred_element_...  47.9 us
  transfers between devices with their start and end apart: 86, of which 42 were waited for; matrix products, arithmetic and copies ran while one was open for 28% of the time, Pallas kernels for 0%

profile of v2, /device:TPU:0, one launch (start us, length us, event | category | flops | bytes accessed | tf_op | source)
XLA Modules:
  0.0 1032.4 jit_solution(17764515051165231515)
XLA Ops:
  63.9 18.5 %collective-permute-done.3 = bf16[128,2048]{1,0:T(8,128)(2,1)S(1)} collective-permute-done((bf16[128,2048]{1,0:T(8,128)(2,1)}, bf16[128,2048]{1,0:T(8,128)(2,1)S(1)}, u32[]{:S(2)}, u32[]{:S(2)}) %collective-permute-start.3) | collective-permute-done | bytes 524320 | tf_op jit(solution)/shard_map/ppermute | solution.py:74
  110.6 11.9 %collective-permute-done.14 = bf16[512,768]{1,0:T(8,128)(2,1)S(1)} collective-permute-done((bf16[512,768]{1,0:T(8,128)(2,1)S(1)}, bf16[512,768]{1,0:T(8,128)(2,1)S(1)}, u32[]{:S(2)}, u32[]{:S(2)}) %collective-permute-start.14) | collective-permute-done | bytes 786464 | tf_op jit(solution)/shard_map/ppermute | solution.py:74
  163.6 23.3 %collective-permute-done.34 = bf16[128,2176]{1,0:T(8,128)(2,1)S(1)} collective-permute-done((bf16[128,2176]{1,0:T(8,128)(2,1)S(1)}, bf16[128,2176]{1,0:T(8,128)(2,1)S(1)}, u32[]{:S(2)}, u32[]{:S(2)}) %collective-permute-start.34) | collective-permute-done | bytes 557088 | tf_op jit(solution)/shard_map/ppermute | solution.py:74
  194.0 10.2 collective-permute-done.36
  204.5 9.9 collective-permute-done.33
  220.4 17.1 %collective-permute-done.20 = bf16[128,2048]{1,0:T(8,128)(2,1)S(1)} collective-permute-done((bf16[128,2048]{1,0:T(8,128)(2,1)S(1)}, bf16[128,2048]{1,0:T(8,128)(2,1)S(1)}, u32[]{:S(2)}, u32[]{:S(2)}) %collective-permute-start.20) | collective-permute-done | bytes 524320 | tf_op jit(solution)/shard_map/ppermute | solution.py:74
  247.7 15.1 %collective-permute-done.24 = bf16[128,2048]{1,0:T(8,128)(2,1)S(1)} collective-permute-done((bf16[128,2048]{1,0:T(8,128)(2,1)S(1)}, bf16[128,2048]{1,0:T(8,128)(2,1)S(1)}, u32[]{:S(2)}, u32[]{:S(2)}) %collective-permute-start.24) | collective-permute-done | bytes 524320 | tf_op jit(solution)/shard_map/ppermute | solution.py:74
  268.3 8.8 collective-permute-done.28
  279.4 9.5 collective-permute-done.27
  333.5 10.9 %fusion.33 = f32[2048,768]{0,1:T(8,128)} fusion(bf16[2048,2048]{1,0:T(8,128)(2,1)} %constant_dynamic-update-slice_fusion.92, bf16[2048,384]{0,1:T(8,128)(2,1)S(1)} %get-tuple-element.420, bf16[2048,384]{0,1:T(8,128)(2,1)S(1)} %copy-done.39), kind=kOutput, calls=%fused_computation.107 | convolution fusion | flops 6448742400 | bytes 17825792 | tf_op jit(solution)/shard_map/dot_general | solution.py:37
  357.3 12.2 %fusion.32 = f32[2048,2048]{1,0:T(8,128)} fusion(bf16[2048,384]{0,1:T(8,128)(2,1)} %get-tuple-element.135, bf16[2048,384]{0,1:T(8,128)(2,1)S(1)} %get-tuple-element.134, bf16[2048,384]{0,1:T(8,128)(2,1)S(1)} %copy-done.37, bf16[2048,384]{0,1:T(8,128)(2,1)S(1)} %copy-done.39), kind=kOutput, calls=%fused_computation.106 | convolution fusion | flops 6455033856 | bytes 23068672 | tf_op jit(solution)/shard_map/dot_general | solution.py:41
  369.5 54.8 %collective-permute-done.39 = bf16[2048,1152]{0,1:T(8,128)(2,1)} collective-permute-done((bf16[2048,1152]{0,1:T(8,128)(2,1)}, bf16[2048,1152]{0,1:T(8,128)(2,1)}, u32[]{:S(2)}, u32[]{:S(2)}) %collective-permute-start.39) | collective-permute-done | bytes 4718624 | tf_op jit(solution)/shard_map/ppermute | solution.py:74
  424.3 10.0 fusion.25
  444.5 13.7 %add_convert_fusion = bf16[2048,2048]{1,0:T(8,128)(2,1)} fusion(f32[2048,2048]{1,0:T(8,128)} %fusion.32, bf16[2048,1152]{0,1:T(8,128)(2,1)} %collective-permute-done.39, bf16[2048,384]{0,1:T(8,128)(2,1)S(1)} %get-tuple-element.133, bf16[2048,384]{0,1:T(8,128)(2,1)S(1)} %get-tuple-element.132), kind=kOutput, calls=%fused_computation | convolution fusion | flops 6457131008 | bytes 31457280 | tf_op jit(solution)/shard_map/dot_general | solution.py:41
  458.2 13.8 %concatenate.397 = bf16[2048,2176]{1,0:T(8,128)(2,1)} concatenate(bf16[2048,2048]{1,0:T(8,128)(2,1)} %add_convert_fusion, bf16[2048,64]{1,0:T(8,128)(2,1)} %get-tuple-element.355, bf16[2048,64]{1,0:T(8,128)(2,1)} %get-tuple-element.354), dimensions={1} | concatenate | bytes 17825792 | tf_op jit(solution)/shard_map/concatenate | solution.py:357
  485.0 11.3 %add_convert_fusion.1 = bf16[2048,2048]{1,0:T(8,128)(2,1)S(1)} fusion(f32[2048,2048]{1,0:T(8,128)} %fusion.35, bf16[2048,384]{0,1:T(8,128)(2,1)} %get-tuple-element.141, bf16[2048,1152]{0,1:T(8,128)(2,1)} %collective-permute-done.39), kind=kOutput, calls=%fused_computation.1 | convolution fusion | flops 3229614080 | bytes 28311552 | tf_op jit(solution)/shard_map/dot_general | solution.py:41
  499.4 9.5 convolution_convert_fusion.2
  516.0 11.8 %fusion.31 = f32[2048,768]{0,1:T(8,128)} fusion(bf16[2048,2048]{1,0:T(8,128)(2,1)} %constant_dynamic-update-slice_fusion.92, bf16[2048,384]{0,1:T(8,128)(2,1)} %get-tuple-element.135, bf16[2048,384]{0,1:T(8,128)(2,1)S(1)} %copy-done.147), kind=kOutput, calls=%fused_computation.105 | convolution fusion | flops 6448742400 | bytes 17825792 | tf_op jit(solution)/shard_map/dot_general | solution.py:45
  576.8 10.2 collective-permute-done.55
  589.5 30.0 %collective-permute-done.82 = bf16[2048,1152]{0,1:T(8,128)(2,1)} collective-permute-done((bf16[2048,1152]{0,1:T(8,128)(2,1)}, bf16[2048,1152]{0,1:T(8,128)(2,1)}, u32[]{:S(2)}, u32[]{:S(2)}) %collective-permute-start.82) | collective-permute-done | bytes 4718624 | tf_op jit(solution)/shard_map/ppermute | solution.py:74
  619.5 8.3 fusion
  666.3 10.4 %collective-permute-done.43 = bf16[128,2048]{1,0:T(8,128)(2,1)S(1)} collective-permute-done((bf16[128,2048]{1,0:T(8,128)(2,1)S(1)}, bf16[128,2048]{1,0:T(8,128)(2,1)S(1)}, u32[]{:S(2)}, u32[]{:S(2)}) %collective-permute-start.43) | collective-permute-done | bytes 524320 | tf_op jit(solution)/shard_map/ppermute | solution.py:74
  691.2 18.8 %collective-permute-done.59 = bf16[128,2048]{1,0:T(8,128)(2,1)S(1)} collective-permute-done((bf16[128,2048]{1,0:T(8,128)(2,1)S(1)}, bf16[128,2048]{1,0:T(8,128)(2,1)S(1)}, u32[]{:S(2)}, u32[]{:S(2)}) %collective-permute-start.59) | collective-permute-done | bytes 524320 | tf_op jit(solution)/shard_map/ppermute | solution.py:74
  715.5 10.1 collective-permute-done.60
  774.0 9.5 multiply_reduce_fusion
  783.5 13.5 %multiply_convert_fusion = (bf16[1024,1024]{0,1:T(8,128)(2,1)S(1)}, bf16[1024,1024]{0,1:T(8,128)(2,1)}, bf16[1024,1024]{0,1:T(8,128)(2,1)}, bf16[1024,1024]{0,1:T(8,128)(2,1)}) fusion(f32[1024,1024]{0,1:T(8,128)} %get-tuple-element.419, f32[1024,1024]{0,1:T(8,128)} %copy-done.9, f32[1024]{0:T(1024)S(1)} %get-tuple-element.109, f32[1024]{0:T(1024)S(1)} %copy-done.112, ...), kind=kLoop, calls=%fused_computation.33 | loop fusion | flops 26214400 | bytes 41979904 | tf_op jit(solution)/shard_map/convert_element_type | solution.py:384
  842.7 41.2 %collective-permute-done.79 = bf16[2,128,2048]{2,1,0:T(8,128)(2,1)} collective-permute-done((bf16[2,128,2048]{2,1,0:T(8,128)(2,1)}, bf16[2,128,2048]{2,1,0:T(8,128)(2,1)}, u32[]{:S(2)}, u32[]{:S(2)}) %collective-permute-start.79) | collective-permute-done | bytes 1048608 | tf_op jit(solution)/shard_map/ppermute | solution.py:74
  892.3 11.0 %collective-permute-done.80 = bf16[1,128,2048]{2,1,0:T(8,128)(2,1)} collective-permute-done((bf16[1,128,2048]{2,1,0:T(8,128)(2,1)}, bf16[1,128,2048]{2,1,0:T(8,128)(2,1)}, u32[]{:S(2)}, u32[]{:S(2)}) %collective-permute-start.80) | collective-permute-done | bytes 524320 | tf_op jit(solution)/shard_map/ppermute | solution.py:74
  907.1 11.4 %collective-permute-done.74 = bf16[1,512,768]{2,1,0:T(8,128)(2,1)S(1)} collective-permute-done((bf16[1,512,768]{2,1,0:T(8,128)(2,1)S(1)}, bf16[1,512,768]{2,1,0:T(8,128)(2,1)S(1)}, u32[]{:S(2)}, u32[]{:S(2)}) %collective-permute-start.74) | collective-permute-done | bytes 786464 | tf_op jit(solution)/shard_map/ppermute | solution.py:74
  930.2 24.0 %collective-permute-done.76 = bf16[128,768]{1,0:T(8,128)(2,1)S(1)} collective-permute-done((bf16[128,768]{1,0:T(8,128)(2,1)S(1)}, bf16[128,768]{1,0:T(8,128)(2,1)S(1)}, u32[]{:S(2)}, u32[]{:S(2)}) %collective-permute-start.76) | collective-permute-done | bytes 196640 | tf_op jit(solution)/shard_map/ppermute | solution.py:74
  957.6 22.6 %collective-permute-done.65 = bf16[128,2048]{1,0:T(8,128)(2,1)S(1)} collective-permute-done((bf16[128,2048]{1,0:T(8,128)(2,1)S(1)}, bf16[128,2048]{1,0:T(8,128)(2,1)S(1)}, u32[]{:S(2)}, u32[]{:S(2)}) %collective-permute-start.65) | collective-permute-done | bytes 524320 | tf_op jit(solution)/shard_map/ppermute | solution.py:74
  1005.4 9.1 collective-permute-done.67
  (850 shorter events, 525.0 us)
Async XLA Ops:
  7.3 93.0 %collective-permute-start.18 = (bf16[128,2048]{1,0:T(8,128)(2,1)}, bf16[128,2048]{1,0:T(8,128)(2,1)S(1)}, u32[]{:S(2)}, u32[]{:S(2)}) collective-permute-start(bf16[128,2048]{1,0:T(8,128)(2,1)} %slice_select_fusion.3), channel_id=1, source_target_pairs={{0,4},{1,5},{2,6},{3,7},{4,0},{5,1},{6,2},{7,3},{8,12},{9,13},{10,... | collective-permute-start | bytes 1572872 | tf_op jit(solution)/shard_map/ppermute | solution.py:74
  12.2 35.5 %collective-permute-start.1 = (bf16[64,4224]{1,0:T(8,128)(2,1)}, bf16[64,4224]{1,0:T(8,128)(2,1)}, u32[]{:S(2)}, u32[]{:S(2)}) collective-permute-start(bf16[64,4224]{1,0:T(8,128)(2,1)} %get-tuple-element.216), channel_id=1, source_target_pairs={{0,2},{1,6},{2,0},{3,4},{4,3},{5,7},{6,1},{7,5},{8,10},{9,14},{10,... | collective-permute-start | bytes 1622024 | tf_op jit(solution)/shard_map/ppermute | solution.py:74
  12.7 35.0 %collective-permute-start = (bf16[64,4224]{1,0:T(8,128)(2,1)}, bf16[64,4224]{1,0:T(8,128)(2,1)}, u32[]{:S(2)}, u32[]{:S(2)}) collective-permute-start(bf16[64,4224]{1,0:T(8,128)(2,1)} %get-tuple-element.215), channel_id=1, source_target_pairs={{0,0},{1,4},{2,2},{3,6},{4,1},{5,5},{6,3},{7,7},{8,8},{9,12},{10,1... | collective-permute-start | bytes 1622024 | tf_op jit(solution)/shard_map/ppermute | solution.py:74
  24.7 36.2 %collective-permute-start.12 = (bf16[128,768]{1,0:T(8,128)(2,1)}, bf16[128,768]{1,0:T(8,128)(2,1)S(1)}, u32[]{:S(2)}, u32[]{:S(2)}) collective-permute-start(bf16[128,768]{1,0:T(8,128)(2,1)} %get-tuple-element.232), channel_id=1, source_target_pairs={{0,16},{1,17},{2,18},{3,19},{4,20},{5,21},{6,22},{7,23},{8,24},{9,... | collective-permute-start | bytes 589832 | tf_op jit(solution)/shard_map/ppermute | solution.py:74
  60.9 39.8 %collective-permute-start.17 = (bf16[128,2048]{1,0:T(8,128)(2,1)}, bf16[128,2048]{1,0:T(8,128)(2,1)S(1)}, u32[]{:S(2)}, u32[]{:S(2)}) collective-permute-start(bf16[128,2048]{1,0:T(8,128)(2,1)} %slice_select_fusion.3), channel_id=1, source_target_pairs={{0,6},{1,7},{2,4},{3,5},{4,2},{5,3},{6,0},{7,1},{8,14},{9,15},{10,... | collective-permute-start | bytes 1572872 | tf_op jit(solution)/shard_map/ppermute | solution.py:74
  61.5 39.2 %collective-permute-start.16 = (bf16[128,2048]{1,0:T(8,128)(2,1)}, bf16[128,2048]{1,0:T(8,128)(2,1)S(1)}, u32[]{:S(2)}, u32[]{:S(2)}) collective-permute-start(bf16[128,2048]{1,0:T(8,128)(2,1)} %slice_select_fusion.3), channel_id=1, source_target_pairs={{0,2},{1,3},{2,0},{3,1},{4,6},{5,7},{6,4},{7,5},{8,10},{9,11},{10,... | collective-permute-start | bytes 1572872 | tf_op jit(solution)/shard_map/ppermute | solution.py:74
  157.9 32.0 %collective-permute-start.19 = (bf16[512,2048]{1,0:T(8,128)(2,1)S(1)}, bf16[512,2048]{1,0:T(8,128)(2,1)S(1)}, u32[]{:S(2)}, u32[]{:S(2)}) collective-permute-start(bf16[512,2048]{1,0:T(8,128)(2,1)S(1)} %slice.1376), channel_id=1, source_target_pairs={{0,1},{1,0},{2,3},{3,2},{4,5},{5,4},{6,7},{7,6},{8,9},{9,8},{10,11... | collective-permute-start | bytes 6291464 | tf_op jit(solution)/shard_map/ppermute | solution.py:74
  186.9 32.6 %collective-permute-start.35 = (bf16[128,2176]{1,0:T(8,128)(2,1)S(1)}, bf16[128,2176]{1,0:T(8,128)(2,1)S(1)}, u32[]{:S(2)}, u32[]{:S(2)}) collective-permute-start(bf16[128,2176]{1,0:T(8,128)(2,1)S(1)} %collective-permute-done.34), channel_id=1, source_target_pairs={{0,4},{1,5},{2,6},{3,7},{4,0},{5,1},{6,2},{7,3},{8,12},{9,13},{10,... | collective-permute-start | bytes 1671176 | tf_op jit(solution)/shard_map/ppermute | solution.py:74
  204.2 42.6 %collective-permute-start.37 = (bf16[128,2176]{1,0:T(8,128)(2,1)S(1)}, bf16[128,2176]{1,0:T(8,128)(2,1)S(1)}, u32[]{:S(2)}, u32[]{:S(2)}) collective-permute-start(bf16[128,2176]{1,0:T(8,128)(2,1)S(1)} %collective-permute-done.36), channel_id=1, source_target_pairs={{0,4},{1,5},{2,6},{3,7},{4,0},{5,1},{6,2},{7,3},{8,12},{9,13},{10,... | collective-permute-start | bytes 1671176 | tf_op jit(solution)/shard_map/ppermute | solution.py:74
  247.7 75.0 %collective-permute-start.38 = (bf16[1024,2176]{1,0:T(8,128)(2,1)}, bf16[1024,2176]{1,0:T(8,128)(2,1)}, u32[]{:S(2)}, u32[]{:S(2)}) collective-permute-start(bf16[1024,2176]{1,0:T(8,128)(2,1)} %get-tuple-element.241), channel_id=1, source_target_pairs={{0,1},{1,0},{2,3},{3,2},{4,5},{5,4},{6,7},{7,6},{8,9},{9,8},{10,11... | collective-permute-start | bytes 13369352 | tf_op jit(solution)/shard_map/ppermute | solution.py:74
  319.8 104.5 %collective-permute-start.39 = (bf16[2048,1152]{0,1:T(8,128)(2,1)}, bf16[2048,1152]{0,1:T(8,128)(2,1)}, u32[]{:S(2)}, u32[]{:S(2)}) collective-permute-start(bf16[2048,1152]{0,1:T(8,128)(2,1)} %pad_maximum_fusion), channel_id=1, source_target_pairs={{0,2},{1,3},{2,0},{3,1},{4,6},{5,7},{6,4},{7,5},{8,10},{9,11},{10,... | collective-permute-start | bytes 14155784 | tf_op jit(solution)/shard_map/ppermute | solution.py:74
  476.8 62.0 %collective-permute-start.50 = (bf16[1024,2176]{1,0:T(8,128)(2,1)}, bf16[1024,2176]{1,0:T(8,128)(2,1)}, u32[]{:S(2)}, u32[]{:S(2)}) collective-permute-start(bf16[1024,2176]{1,0:T(8,128)(2,1)} %slice.1409), channel_id=1, source_target_pairs={{0,1},{1,0},{2,3},{3,2},{4,5},{5,4},{6,7},{7,6},{8,9},{9,8},{10,11... | collective-permute-start | bytes 13369352 | tf_op jit(solution)/shard_map/ppermute | solution.py:74
  515.4 104.1 %collective-permute-start.82 = (bf16[2048,1152]{0,1:T(8,128)(2,1)}, bf16[2048,1152]{0,1:T(8,128)(2,1)}, u32[]{:S(2)}, u32[]{:S(2)}) collective-permute-start(bf16[2048,1152]{0,1:T(8,128)(2,1)} %pad_maximum_fusion.1), channel_id=1, source_target_pairs={{0,2},{1,3},{2,0},{3,1},{4,6},{5,7},{6,4},{7,5},{8,10},{9,11},{10,... | collective-permute-start | bytes 14155784 | tf_op jit(solution)/shard_map/ppermute | solution.py:74
  557.3 29.7 %collective-permute-start.55 = (bf16[128,2176]{1,0:T(8,128)(2,1)S(1)}, bf16[128,2176]{1,0:T(8,128)(2,1)S(1)}, u32[]{:S(2)}, u32[]{:S(2)}) collective-permute-start(bf16[128,2176]{1,0:T(8,128)(2,1)S(1)} %get-tuple-element.153), channel_id=1, source_target_pairs={{0,4},{1,5},{2,6},{3,7},{4,0},{5,1},{6,2},{7,3},{8,12},{9,13},{10,... | collective-permute-start | bytes 1671176 | tf_op jit(solution)/shard_map/ppermute | solution.py:74
  563.6 79.5 %collective-permute-start.44 = (bf16[128,2048]{1,0:T(8,128)(2,1)}, bf16[128,2048]{1,0:T(8,128)(2,1)}, u32[]{:S(2)}, u32[]{:S(2)}) collective-permute-start(bf16[128,2048]{1,0:T(8,128)(2,1)} %get-tuple-element.166), channel_id=1, source_target_pairs={{0,4},{1,5},{2,6},{3,7},{4,0},{5,1},{6,2},{7,3},{8,12},{9,13},{10,... | collective-permute-start | bytes 1572872 | tf_op jit(solution)/shard_map/ppermute | solution.py:74
  565.4 62.4 %collective-permute-start.54 = (bf16[128,2176]{1,0:T(8,128)(2,1)}, bf16[128,2176]{1,0:T(8,128)(2,1)}, u32[]{:S(2)}, u32[]{:S(2)}) collective-permute-start(bf16[128,2176]{1,0:T(8,128)(2,1)} %get-tuple-element.154), channel_id=1, source_target_pairs={{0,4},{1,5},{2,6},{3,7},{4,0},{5,1},{6,2},{7,3},{8,12},{9,13},{10,... | collective-permute-start | bytes 1671176 | tf_op jit(solution)/shard_map/ppermute | solution.py:74
  575.0 73.5 %collective-permute-start.51 = (bf16[128,2176]{1,0:T(8,128)(2,1)}, bf16[128,2176]{1,0:T(8,128)(2,1)}, u32[]{:S(2)}, u32[]{:S(2)}) collective-permute-start(bf16[128,2176]{1,0:T(8,128)(2,1)} %get-tuple-element.152), channel_id=1, source_target_pairs={{0,4},{1,5},{2,6},{3,7},{4,0},{5,1},{6,2},{7,3},{8,12},{9,13},{10,... | collective-permute-start | bytes 1671176 | tf_op jit(solution)/shard_map/ppermute | solution.py:74
  587.0 57.9 %collective-permute-start.46 = (bf16[128,2048]{1,0:T(8,128)(2,1)}, bf16[128,2048]{1,0:T(8,128)(2,1)}, u32[]{:S(2)}, u32[]{:S(2)}) collective-permute-start(bf16[128,2048]{1,0:T(8,128)(2,1)} %get-tuple-element.169), channel_id=1, source_target_pairs={{0,8},{1,9},{2,10},{3,11},{4,12},{5,13},{6,14},{7,15},{8,0},{9,1},... | collective-permute-start | bytes 1572872 | tf_op jit(solution)/shard_map/ppermute | solution.py:74
  644.9 31.8 %collective-permute-start.43 = (bf16[128,2048]{1,0:T(8,128)(2,1)S(1)}, bf16[128,2048]{1,0:T(8,128)(2,1)S(1)}, u32[]{:S(2)}, u32[]{:S(2)}) collective-permute-start(bf16[128,2048]{1,0:T(8,128)(2,1)S(1)} %copy-done.72), channel_id=1, source_target_pairs={{0,8},{1,9},{2,10},{3,11},{4,12},{5,13},{6,14},{7,15},{8,0},{9,1},... | collective-permute-start | bytes 1572872 | tf_op jit(solution)/shard_map/ppermute | solution.py:74
  648.6 82.3 %collective-permute-start.83 = (bf16[2048,384]{0,1:T(8,128)(2,1)S(1)}, bf16[2048,384]{0,1:T(8,128)(2,1)S(1)}, u32[]{:S(2)}, u32[]{:S(2)}) collective-permute-start(bf16[2048,384]{0,1:T(8,128)(2,1)S(1)} %get-tuple-element.151), channel_id=1, source_target_pairs={{0,1},{1,0},{2,3},{3,2},{4,5},{5,4},{6,7},{7,6},{8,9},{9,8},{10,11... | collective-permute-start | bytes 4718600 | tf_op jit(solution)/shard_map/ppermute | solution.py:74
  687.8 53.7 %collective-permute-start.84 = (bf16[2048,384]{0,1:T(8,128)(2,1)}, bf16[2048,384]{0,1:T(8,128)(2,1)}, u32[]{:S(2)}, u32[]{:S(2)}) collective-permute-start(bf16[2048,384]{0,1:T(8,128)(2,1)} %get-tuple-element.150), channel_id=1, source_target_pairs={{0,1},{1,0},{2,3},{3,2},{4,5},{5,4},{6,7},{7,6},{8,9},{9,8},{10,11... | collective-permute-start | bytes 4718600 | tf_op jit(solution)/shard_map/ppermute | solution.py:74
  687.9 65.0 %collective-permute-start.85 = (bf16[384,2048]{1,0:T(8,128)(2,1)}, bf16[384,2048]{1,0:T(8,128)(2,1)}, u32[]{:S(2)}, u32[]{:S(2)}) collective-permute-start(bf16[384,2048]{1,0:T(8,128)(2,1)} %get-tuple-element.149), channel_id=1, source_target_pairs={{0,1},{1,0},{2,3},{3,2},{4,5},{5,4},{6,7},{7,6},{8,9},{9,8},{10,11... | collective-permute-start | bytes 4718600 | tf_op jit(solution)/shard_map/ppermute | solution.py:74
  715.0 43.0 %collective-permute-start.49 = (bf16[64,2048]{1,0:T(8,128)(2,1)}, bf16[64,2048]{1,0:T(8,128)(2,1)}, u32[]{:S(2)}, u32[]{:S(2)}) collective-permute-start(bf16[64,2048]{1,0:T(8,128)(2,1)} %get-tuple-element.276), channel_id=1, source_target_pairs={{2,0},{6,1},{0,2},{4,3},{3,4},{7,5},{1,6},{5,7},{10,8},{14,9},{8,1... | collective-permute-start | bytes 786440 | tf_op jit(solution)/shard_map/ppermute | solution.py:75
  725.6 32.3 %collective-permute-start.48 = (bf16[64,2048]{1,0:T(8,128)(2,1)}, bf16[64,2048]{1,0:T(8,128)(2,1)}, u32[]{:S(2)}, u32[]{:S(2)}) collective-permute-start(bf16[64,2048]{1,0:T(8,128)(2,1)} %get-tuple-element.275), channel_id=1, source_target_pairs={{0,0},{4,1},{2,2},{6,3},{1,4},{5,5},{3,6},{7,7},{8,8},{12,9},{10,1... | collective-permute-start | bytes 786440 | tf_op jit(solution)/shard_map/ppermute | solution.py:75
  824.4 64.3 %collective-permute-start.73 = (bf16[2,512,768]{2,1,0:T(8,128)(2,1)}, bf16[2,512,768]{2,1,0:T(8,128)(2,1)}, u32[]{:S(2)}, u32[]{:S(2)}) collective-permute-start(bf16[2,512,768]{2,1,0:T(8,128)(2,1)} %bitcast.172), channel_id=1, source_target_pairs={{0,4},{1,5},{2,6},{3,7},{4,0},{5,1},{6,2},{7,3},{8,12},{9,13},{10,... | collective-permute-start | bytes 4718600 | tf_op jit(solution)/shard_map/ppermute | solution.py:74
  831.9 52.0 %collective-permute-start.79 = (bf16[2,128,2048]{2,1,0:T(8,128)(2,1)}, bf16[2,128,2048]{2,1,0:T(8,128)(2,1)}, u32[]{:S(2)}, u32[]{:S(2)}) collective-permute-start(bf16[2,128,2048]{2,1,0:T(8,128)(2,1)} %slice.2085), channel_id=1, source_target_pairs={{0,4},{1,5},{2,6},{3,7},{4,0},{5,1},{6,2},{7,3},{8,12},{9,13},{10,... | collective-permute-start | bytes 3145736 | tf_op jit(solution)/shard_map/ppermute | solution.py:74
  841.1 63.5 %collective-permute-start.62 = (bf16[512,2048]{1,0:T(8,128)(2,1)}, bf16[512,2048]{1,0:T(8,128)(2,1)}, u32[]{:S(2)}, u32[]{:S(2)}) collective-permute-start(bf16[512,2048]{1,0:T(8,128)(2,1)} %slice.1441), channel_id=1, source_target_pairs={{0,1},{1,0},{2,3},{3,2},{4,5},{5,4},{6,7},{7,6},{8,9},{9,8},{10,11... | collective-permute-start | bytes 6291464 | tf_op jit(solution)/shard_map/ppermute | solution.py:74
  904.5 78.1 %collective-permute-start.81 = (f32[128,2048]{1,0:T(8,128)S(1)}, f32[128,2048]{1,0:T(8,128)S(1)}, u32[]{:S(2)}, u32[]{:S(2)}) collective-permute-start(f32[128,2048]{1,0:T(8,128)S(1)} %fusion.56), channel_id=1, source_target_pairs={{0,1},{1,0},{2,3},{3,2},{4,5},{5,4},{6,7},{7,6},{8,9},{9,8},{10,11... | collective-permute-start | bytes 3145736 | tf_op jit(solution)/shard_map/ppermute | solution.py:74
  919.9 36.7 %collective-permute-start.64 = (bf16[128,2048]{1,0:T(8,128)(2,1)S(1)}, bf16[128,2048]{1,0:T(8,128)(2,1)S(1)}, u32[]{:S(2)}, u32[]{:S(2)}) collective-permute-start(bf16[128,2048]{1,0:T(8,128)(2,1)S(1)} %get-tuple-element.180), channel_id=1, source_target_pairs={{0,8},{1,9},{2,10},{3,11},{4,12},{5,13},{6,14},{7,15},{8,0},{9,1},... | collective-permute-start | bytes 1572872 | tf_op jit(solution)/shard_map/ppermute | solution.py:74
  922.2 35.4 %collective-permute-start.63 = (bf16[128,2048]{1,0:T(8,128)(2,1)S(1)}, bf16[128,2048]{1,0:T(8,128)(2,1)S(1)}, u32[]{:S(2)}, u32[]{:S(2)}) collective-permute-start(bf16[128,2048]{1,0:T(8,128)(2,1)S(1)} %get-tuple-element.179), channel_id=1, source_target_pairs={{0,8},{1,9},{2,10},{3,11},{4,12},{5,13},{6,14},{7,15},{8,0},{9,1},... | collective-permute-start | bytes 1572872 | tf_op jit(solution)/shard_map/ppermute | solution.py:74
  922.3 31.9 %collective-permute-start.76 = (bf16[128,768]{1,0:T(8,128)(2,1)S(1)}, bf16[128,768]{1,0:T(8,128)(2,1)S(1)}, u32[]{:S(2)}, u32[]{:S(2)}) collective-permute-start(bf16[128,768]{1,0:T(8,128)(2,1)S(1)} %get-tuple-element.228), channel_id=1, source_target_pairs={{0,24},{1,25},{2,26},{3,27},{4,28},{5,29},{6,30},{7,31},{8,16},{9,... | collective-permute-start | bytes 589832 | tf_op jit(solution)/shard_map/ppermute | solution.py:74
  957.5 58.1 %collective-permute-start.78 = (f32[4,128,768]{2,1,0:T(8,128)S(1)}, f32[4,128,768]{2,1,0:T(8,128)S(1)}, u32[]{:S(2)}, u32[]{:S(2)}) collective-permute-start(f32[4,128,768]{2,1,0:T(8,128)S(1)} %maximum_select_fusion.11), channel_id=1, source_target_pairs={{0,1},{1,0},{2,3},{3,2},{4,5},{5,4},{6,7},{7,6},{8,9},{9,8},{10,11... | collective-permute-start | bytes 4718600 | tf_op jit(solution)/shard_map/ppermute | solution.py:74
  (216 other events, 3532.5 us)

commit v3 on v2

v3 whole, which is shorter than its diff:
```python
import math

import jax
import jax.numpy as jnp
from jax import lax
from jax.sharding import PartitionSpec as P

EPS = 1e-06
THETA = 1000000.0
NEGATIVE = -1e30
AXES = ("grp", "rep")
LINES = 4
TAIL = 128
ROWS = 16
F32 = jnp.float32
BF16 = jnp.bfloat16


def row_scale(values):
    return lax.rsqrt(jnp.mean(values * values, axis=-1, keepdims=True) + EPS)


def norm_back(grad, values, factor, gain):
    inner = grad * gain
    back = factor * inner - values * factor**3 * jnp.mean(inner * values, axis=-1, keepdims=True)
    return (back, grad * values * factor)


def dot(left, right):
    return lax.dot_general(left, right, (((1,), (0,)), ((), ())), preferred_element_type=F32)


def dot_out(left, right):
    return lax.dot_general(left, right, (((1,), (1,)), ((), ())), preferred_element_type=F32)


def dot_rows(left, right):
    return lax.dot_general(left, right, (((0,), (0,)), ((), ())), preferred_element_type=F32)


def flip_bit(values, axis, bit):
    count = values.shape[axis]
    pieces = [lax.slice_in_dim(values, i, i + bit, axis=axis) for i in range(0, count, bit)]
    order = [i ^ 1 for i in range(len(pieces))]
    return jnp.concatenate([pieces[i] for i in order], axis=axis)


def xor_order(values, axis, mine):
    bit = 1
    while bit < values.shape[axis]:
        values = jnp.where((mine & bit) != 0, flip_bit(values, axis, bit), values)
        bit *= 2
    return values


def tie(*values):
    return lax.optimization_barrier(values)


def rows_together(parts):
    near, far, other_near, other_far = parts
    count = far.shape[0]
    own = jnp.concatenate([near, far]).reshape(LINES, 1, count, -1)
    other = jnp.concatenate([other_near, other_far]).reshape(LINES, 1, count, -1)
    return jnp.concatenate([own, other], axis=1).reshape(2 * LINES * count, -1)


def two_sides(values):
    sides = values.reshape(LINES, 2, -1, values.shape[1])
    return [sides[:, i].reshape(-1, values.shape[1]) for i in range(2)]


def slots_of(values, slots, piece, shift):
    pieces = values.reshape(values.shape[0], LINES, slots, piece)
    return xor_order(pieces, 2, shift).transpose(0, 2, 1, 3).reshape(values.shape)


def from_slots_of(values, slots, piece, shift):
    pieces = values.reshape(values.shape[0], slots, LINES, piece).transpose(0, 2, 1, 3)
    return xor_order(pieces, 2, shift).reshape(values.shape)


def turn(values, cosine, sine):
    half = values.shape[-1] // 2
    return values * cosine + jnp.concatenate([values[:, half:], values[:, :half]], axis=1) * sine


def block_mask(total, tz):
    block = jnp.arange(total, dtype=jnp.int32) // (total // LINES) ^ tz
    return block[None, :] <= block[:, None]


def attention_forward(scalars, rows, w_slots, w_out, gain_in, gain_q, gain_k, cosine, sine):
    tz, place, shift = scalars[0], scalars[1], scalars[2]
    slots, width = len(w_slots), rows[1].shape[1]
    depth = width // slots
    head = gain_q.shape[1]
    q_width = w_out.shape[0]
    local_heads = q_width // head
    x = rows_together(rows)
    if (depth // LINES) % 128 == 0:
        x = slots_of(x, slots, depth // LINES, shift)
        gain_in = slots_of(gain_in, slots, depth // LINES, shift)
    x = x.astype(F32)
    a1 = (x * row_scale(x) * gain_in).astype(BF16)
    pre = dot(a1, jnp.concatenate([w[:depth] for w in w_slots]))
    scale = 1.0 / math.sqrt(head)
    visible = block_mask(x.shape[0], tz)
    q = jnp.stack(
        [
            turn(u * row_scale(u) * gain_q, cosine, sine).astype(BF16)
            for u in (pre[:, i * head : (i + 1) * head] for i in range(local_heads))
        ]
    )
    q = xor_order(q, 0, place)
    u = pre[:, q_width : q_width + head]
    k = turn(u * row_scale(u) * gain_k, cosine, sine).astype(BF16)
    v = pre[:, q_width + head :].astype(BF16)
    made, inverse = [], []
    for i in range(local_heads):
        expo = jnp.where(visible, jnp.exp(dot_out(q[i], k) * scale), 0.0)
        factor = 1.0 / jnp.sum(expo, axis=1, keepdims=True)
        inverse.append(factor)
        made.append((dot(expo.astype(BF16), v) * factor).astype(BF16))
    o = jnp.concatenate(made, axis=1)
    mine, theirs = two_sides(dot(o, w_out).astype(BF16))
    return a1, pre, q, k, v, o, jnp.stack(inverse), mine, theirs


def attention_backward(
    scalars, grads, w_slots, w_out, gain_q, gain_k, cosine, sine, pre, q, k, v, o, inverse, rows
):
    tz, place, shift = scalars[0], scalars[1], scalars[2]
    slots, width = len(w_slots), rows[1].shape[1]
    depth = width // slots
    head = gain_q.shape[1]
    q_width = w_out.shape[0]
    local_heads = q_width // head
    scale = 1.0 / math.sqrt(head)
    db = rows_together(grads)
    grad = dot_out(db, w_out).astype(BF16)
    visible = block_mask(db.shape[0], tz)
    dk = jnp.zeros(k.shape, F32)
    dv = jnp.zeros(k.shape, F32)
    dqs = []
    for i in range(local_heads):
        at = slice(i * head, (i + 1) * head)
        g = grad[:, at]
        row = jnp.sum(g.astype(F32) * o[:, at].astype(F32), axis=1, keepdims=True)
        probs = jnp.where(visible, jnp.exp(dot_out(q[i], k) * scale), 0.0) * inverse[i]
        low = (probs * (dot_out(g, v) - row)).astype(BF16)
        dqs.append(dot(low, k) * scale)
        dk = dk + dot_rows(low, q[i])
        dv = dv + dot_rows(probs.astype(BF16), g)
    dqs = xor_order(jnp.stack(dqs), 0, place)
    lows, q_gain = [], 0.0
    for i in range(local_heads):
        values = pre[:, i * head : (i + 1) * head]
        back, part = norm_back(turn(dqs[i], cosine, -sine), values, row_scale(values), gain_q)
        lows.append(back.astype(BF16))
        q_gain = q_gain + jnp.sum(part, axis=0)
    values = pre[:, q_width : q_width + head]
    back, part = norm_back(turn(dk * scale, cosine, -sine), values, row_scale(values), gain_k)
    low = jnp.concatenate(lows + [back.astype(BF16), dv.astype(BF16)], axis=1)
    gains = jnp.stack([q_gain, jnp.sum(part, axis=0)])
    da = dot_out(low, jnp.concatenate([w[:depth] for w in w_slots]))
    x = rows_together(rows).astype(F32)
    if (depth // LINES) % 128 == 0:
        da = from_slots_of(da, slots, depth // LINES, shift)
    norm = jnp.sum(da * x * row_scale(x), axis=0)[None]
    mine, theirs = two_sides(da.astype(BF16))
    return db, low, gains, norm, mine, theirs


def expert_rows(ids, a2, dyx, w_experts, router_t):
    width = a2.shape[1]
    mask, dy = dyx[:, width:], dyx[:, :width]
    logits = jnp.where(mask > 0, dot_out(a2, router_t), NEGATIVE)
    gates = jax.nn.softmax(logits, axis=-1)
    lane = jnp.arange(TAIL, dtype=jnp.int32)[None, :]
    hidden = w_experts[0][0].shape[1] // 3
    spread = jnp.zeros(mask.shape, F32)
    pairs, mixes, rows_back = [], [], 0.0
    for e, pieces in enumerate(w_experts):
        w = jnp.concatenate(pieces)
        weight = jnp.sum(jnp.where(lane == ids[e], gates, 0.0), axis=1, keepdims=True)
        both = dot(a2, w[:, : 2 * hidden])
        gate_pre, up_pre = both[:, :hidden], both[:, hidden:]
        back = dot(dy, w[:, 2 * hidden :])
        sigmoid = jax.nn.sigmoid(gate_pre)
        silu = gate_pre * sigmoid
        made = silu * up_pre
        grad = jnp.sum(made * back, axis=1, keepdims=True)
        high = lax.reduce_precision(grad, 8, 7)
        place = ids[len(w_experts)] + ids[e]
        spread = jnp.where(lane == place, high, spread)
        spread = jnp.where(lane == place + TAIL // 4, grad - high, spread)
        mixes.append((made * weight).astype(BF16))
        made_grad = back * weight
        pair = jnp.concatenate(
            [
                made_grad * up_pre * sigmoid * (1.0 + gate_pre * (1.0 - sigmoid)),
                made_grad * silu,
            ],
            axis=1,
        ).astype(BF16)
        pairs.append(pair)
        rows_back = rows_back + dot_out(pair, w[:, : 2 * hidden])
    rows_back = jnp.concatenate([rows_back.astype(BF16), spread.astype(BF16)], axis=1)
    return jnp.concatenate(pairs, axis=1), jnp.concatenate(mixes, axis=1), rows_back


def expert_outputs(mixed, w_experts):
    hidden = w_experts[0][0].shape[1] // 3
    return [
        sum(
            dot_out(m[:, hidden * e : hidden * (e + 1)], jnp.concatenate(w)[:, 2 * hidden :])
            for e, w in enumerate(w_experts)
        ).astype(BF16)
        for m in mixed
    ]


def expert_weight_grads(pairs, mixes, a2, dyx):
    width = a2[0].shape[1]
    units = pairs[0].shape[1] // 2
    hidden = units // 2
    pair = dot_rows(pairs[0], a2[0]) + dot_rows(pairs[1], a2[1])
    down = dot_rows(mixes[0], dyx[0][:, :width]) + dot_rows(mixes[1], dyx[1][:, :width])
    own = jnp.concatenate([pair[:units], down[:hidden]])
    return own, jnp.concatenate([pair[units:], down[hidden:]]).astype(BF16)


def join_expert_grads(core, own, other):
    hidden = own.shape[0] // 3
    first = core[0] == 0
    low, high = jnp.where(first, own, other), jnp.where(first, other, own)
    low, high = low.astype(F32), high.astype(F32)
    return (
        jnp.concatenate([low[:hidden].T, high[:hidden].T], axis=1),
        jnp.concatenate([low[hidden : 2 * hidden].T, high[hidden : 2 * hidden].T], axis=1),
        jnp.concatenate([low[2 * hidden :], high[2 * hidden :]]),
    )


def join_column_grads(core, own, other, head):
    kv_heads, piece, columns = own.shape
    local_heads = columns // head - 2
    q_width = local_heads * head
    first = core[0] == 0
    low, high = jnp.where(first, own, other), jnp.where(first, other, own)
    q = jnp.stack(
        [v[..., :q_width].reshape(kv_heads, piece, local_heads, head) for v in (low, high)], axis=3
    )
    q = q.transpose(1, 0, 2, 3, 4).reshape(piece, -1)
    both = low + high
    k = both[..., q_width : q_width + head].transpose(1, 0, 2).reshape(piece, -1)
    v = both[..., q_width + head :].transpose(1, 0, 2).reshape(piece, -1)
    return q, k, v


def build(groups, reps):
    columns = groups // LINES

    def mover(target):
        table = [
            (g * reps + r, target(g, r)[0] * reps + target(g, r)[1])
            for g in range(groups)
            for r in range(reps)
        ]
        back = [(b, a) for a, b in table]
        return (
            lambda v: lax.ppermute(v, AXES, table),
            lambda v: lax.ppermute(v, AXES, back),
        )

    def home(k):
        def target(g, r):
            sequence, block = g // 16, g % 16
            column = (sequence * 2 + r % 2) * 2 + (k ^ (g & 1))
            return ((block // 4) * columns + column, (r // 2) * 2 + (block // 2) % 2)

        return mover(target)

    def line(k):
        return mover(lambda g, r: (((g // columns) ^ k) * columns + g % columns, r))[0]

    return dict(
        columns=columns,
        line=[None] + [line(k) for k in range(1, LINES)],
        plane=[None] + [mover(lambda g, r, k=k: (g ^ k, r))[0] for k in range(1, columns)],
        core=mover(lambda g, r: (g, r ^ 1))[0],
        replicas=[mover(lambda g, r, k=k: (g, r ^ (2 * k)))[0] for k in range(1, reps // 2)],
        home=[home(0), home(1)],
    )


def per_device(
    layer_input,
    out_grad,
    routes,
    norm_in,
    query_weight,
    key_weight,
    value_weight,
    query_gain,
    key_gain,
    out_weight,
    norm_mid,
    router,
    expert_gate,
    expert_up,
    expert_down,
):
    groups, reps = lax.axis_size("grp"), lax.axis_size("rep")
    mv = build(groups, reps)
    columns, line, plane, to_core = mv["columns"], mv["line"], mv["plane"], mv["core"]
    sharing = columns // 2
    axes = [b for b in (1, 2, 4, 8) if b < columns]
    g, r = lax.axis_index("grp"), lax.axis_index("rep")
    tz, gc, core = g // columns, g % columns, r % 2
    odd = (g & 1) != 0
    batches, tokens, width = layer_input.shape[1:]
    experts = groups
    piece = width // groups
    head = query_gain.shape[0] * groups
    heads = query_weight.shape[1] // head
    kv_heads = key_weight.shape[1] // head
    local_heads = heads // (2 * kv_heads)
    q_width = local_heads * head
    hidden = expert_gate.shape[2] // 2
    rows = batches * tokens
    total = 2 * LINES * rows
    part = head // groups
    wide = width + TAIL

    def at_line(values, i):
        return values[i * rows : (i + 1) * rows]

    def send_home(values):
        values = values.reshape((2, tokens) + values.shape[1:])
        values = jnp.where(odd, values[::-1], values)
        return [mv["home"][k][1](values[k]) for k in range(2)]

    def at_home(got):
        got = jnp.stack(got)
        return jnp.where(odd, got[::-1], got)[None]

    def to_slots(values):
        if piece % 128 == 0:
            return values
        pieces = [values[:, i * piece : (i + 1) * piece] for i in range(groups)]
        by_slot = [pieces[t * columns + s] for s in range(columns) for t in range(LINES)]
        whole = jnp.stack(by_slot).reshape(columns, LINES, values.shape[0], piece)
        whole = xor_order(whole, 0, gc)
        return jnp.concatenate([whole[s, t] for s in range(columns) for t in range(LINES)], axis=1)

    def from_slots(values):
        if piece % 128 == 0:
            return values
        count = LINES * piece
        whole = jnp.stack([values[:, s * count : (s + 1) * count] for s in range(columns)])
        whole = xor_order(whole, 0, gc)
        return jnp.concatenate(
            [
                whole[s, :, t * piece : (t + 1) * piece]
                for t in range(LINES)
                for s in range(columns)
            ],
            axis=1,
        )

    def over_replicas(values):
        low = values.astype(BF16)
        return values + sum(move(low).astype(F32) for move in mv["replicas"])

    def whole(values, other, axis):
        return jnp.where(
            core == 0,
            jnp.concatenate([values, other], axis=axis),
            jnp.concatenate([other, values], axis=axis),
        ).astype(F32)

    def half_of(values, axis):
        low = lax.slice_in_dim(values, 0, hidden, axis=axis)
        high = lax.slice_in_dim(values, hidden, 2 * hidden, axis=axis)
        return jnp.where(core == 0, low, high)

    named = (routes[0][..., None] == jnp.arange(experts, dtype=jnp.int32)).any(axis=2)
    named = jnp.pad(named.astype(F32), ((0, 0), (0, 0), (0, TAIL - experts)))
    named = tie(named)[0].astype(BF16)
    leaving = jnp.concatenate([layer_input[0], out_grad[0], named], axis=2)
    leaving = jnp.where(odd, leaving[::-1], leaving)
    got = [mv["home"][k][0](leaving[k]) for k in range(2)]
    rel = []
    for h in range(kv_heads):
        sides = [
            jnp.concatenate(
                [
                    query_weight[:, ((h * local_heads + i) * 2 + n) * head :][:, :head]
                    for i in range(local_heads)
                ],
                axis=1,
            )
            for n in range(2)
        ]
        at = slice(h * head, (h + 1) * head)
        rel.append(
            jnp.concatenate(
                [jnp.where(core == 0, *sides), key_weight[:, at], value_weight[:, at]], axis=1
            )
        )
    qkv = jnp.stack(rel)
    rel = xor_order(qkv, 0, tz)
    gains = jnp.concatenate([query_gain, key_gain]).astype(F32)
    packed = jnp.concatenate(
        [
            norm_in.astype(F32)[None],
            norm_mid.astype(F32)[None],
            router.astype(F32).T,
            jnp.pad(gains, (0, piece - gains.shape[0]))[None],
        ]
    )
    strips = -(-packed.shape[0] // ROWS)
    packed = jnp.pad(packed, ((0, strips * ROWS - packed.shape[0]), (0, 0)))
    packed = jnp.concatenate([packed[i * ROWS : (i + 1) * ROWS] for i in range(strips)], axis=1)
    packed = jnp.pad(packed, ((0, 0), (0, qkv.shape[2] - packed.shape[1])))
    packed = tie(packed)[0].astype(BF16)
    rel = [jnp.concatenate([rel[k], packed]) for k in range(LINES)]
    rel_got = [line[k](rel[k]) for k in range(1, LINES)]
    out_heads = out_weight.shape[0] // head
    own_out = out_weight
    if out_heads == 2:
        own_out = jnp.where(core == 0, out_weight[:head], out_weight[head:])
    rel_own, own_out, *moved = tie(rel[0], own_out, *got, *rel_got)
    got, rel_got = moved[:2], moved[2:]

    got = jnp.stack(got)
    brought = jnp.where(odd, got[::-1], got).reshape(rows, -1)
    slotted = to_slots(brought[:, :width])
    first, second = line[1](slotted), line[2](slotted)
    qkv = xor_order(jnp.stack([rel_own] + rel_got), 0, tz)
    qkv = jnp.concatenate(
        [qkv[:, :piece].reshape(LINES * piece, -1), qkv[:, piece:].reshape(LINES * ROWS, -1)]
    )
    w_held = {0: qkv}
    for bit in axes[::-1]:
        w_held[bit] = plane[bit](qkv)
    out_held = jnp.stack([own_out, plane[1](own_out)])
    slotted, first, second, out_held, *moved = tie(
        slotted, first, second, out_held, *[w_held[b] for b in [0] + axes]
    )
    for bit, value in zip([0] + axes, moved):
        w_held[bit] = value

    third = line[1](second)
    near_rows = jnp.concatenate([slotted, first, second])
    others = to_core(near_rows)
    for s in range(1, columns):
        if s not in w_held:
            top = max(b for b in axes if s & b)
            w_held[s] = plane[s ^ top](w_held[top])
    for bit in axes[1:]:
        out_held = jnp.concatenate([out_held, plane[bit](out_held)])
    third, others, near_rows, out_held, *w_slots = tie(
        third, others, near_rows, out_held, *[w_held[s] for s in range(columns)]
    )
    w_out = [out_held[s] for s in range(columns)]

    other_third = to_core(third)
    place = gc
    if out_heads == 1:
        place = gc // 2
        swapped = ((gc & 1) ^ core) != 0
        w_out = [jnp.where(swapped, w_out[i + 1], w_out[i]) for i in range(0, columns, 2)]
    w_out = jnp.concatenate(w_out)
    scalars = jnp.stack([tz, place, gc]).astype(jnp.int32)
    which = jnp.arange(total, dtype=jnp.int32)
    block, side, inner = which // (2 * rows), which // rows % 2, which % rows
    position = ((block ^ tz) * 2 + (side ^ core)) * rows + inner
    inverse = THETA ** (-(jnp.arange(head // 2, dtype=F32) * 2.0 / head))
    angle = position.astype(F32)[:, None] * inverse[None, :]
    cosine, sine = jnp.cos(angle), jnp.sin(angle)
    cosine = jnp.concatenate([cosine, cosine], axis=1)
    sine = jnp.concatenate([-sine, sine], axis=1)
    w_own = jnp.concatenate(
        [half_of(expert_gate[0], 1), half_of(expert_up[0], 1), half_of(expert_down[0], 0).T],
        axis=1,
    )
    packed = tie(*[w[LINES * piece :, : strips * piece].astype(F32) for w in w_slots])
    packed = jnp.stack([w.reshape(LINES, ROWS, -1) for w in packed], axis=1)
    packed = xor_order(packed, 1, gc).reshape(groups, ROWS, strips, piece)
    packed = packed.transpose(0, 2, 1, 3).reshape(groups, strips * ROWS, piece)
    other_third, packed, w_out, cosine, sine, w_own, brought = tie(
        other_third, packed, w_out, cosine, sine, w_own, brought
    )
    row_parts = (near_rows, third, others, other_third)
    small = packed[:, : experts + 2].transpose(1, 0, 2).reshape(experts + 2, width)
    gain_in, gain_mid, router_f = tie(small[:1], small[1:2], small[2:])
    router_t = router_f.astype(BF16)
    gain_q = packed[:, experts + 2, :part].reshape(1, head)
    gain_k = packed[:, experts + 2, part : 2 * part].reshape(1, head)

    cuts = [0] + [width * n // 16 for n in (6, 9, 12, 16)]
    w_near = []

    def next_weights():
        n = len(w_near)
        return plane[1](w_own[cuts[n] : cuts[n + 1]])

    grad_rows = brought[:, width:]
    grad_got = [line[n](grad_rows) for n in range(1, LINES)]
    w_got = next_weights()
    a1, pre, q, k, v, attended, inverse, mine, theirs = attention_forward(
        scalars, row_parts, w_slots, w_out, to_slots(gain_in), gain_q, gain_k, cosine, sine
    )
    mine, theirs, w_got, w_own, *grad_got = tie(mine, theirs, w_got, w_own, *grad_got)
    w_near.append(w_got)

    theirs = to_core(theirs)
    grad_own = jnp.concatenate([grad_rows] + grad_got)
    grad_low, grad_high = grad_own[: 2 * rows], grad_own[2 * rows :]
    mine, theirs, grad_low, grad_high = tie(mine, theirs, grad_low, grad_high)
    both = mine.astype(F32) + theirs.astype(F32)

    first = line[1](at_line(both, 1).astype(BF16))
    third = line[1](at_line(both, 3).astype(BF16))
    grads = [[grad_low], [grad_high]]
    got = [plane[2 * u](grad_low) for u in range(1, sharing)]
    w_got = next_weights()
    both, first, third, w_got, w_own, grad_high, *got = tie(
        both, first, third, w_got, w_own, grad_high, *got
    )
    w_near.append(w_got)
    grads[0] += got

    second = line[2]((at_line(both, 2) + third.astype(F32)).astype(BF16))
    got = [plane[2 * u](grad_high) for u in range(1, sharing)]
    w_got = next_weights()
    both, first, second, w_got, w_own, *got = tie(both, first, second, w_got, w_own, *got)
    w_near.append(w_got)
    grads[1] += got
    inputs = brought[:, :width].astype(F32)
    grad_out = brought[:, width : 2 * width].astype(F32)
    mid = inputs + at_line(both, 0) + first.astype(F32) + second.astype(F32)
    scale_mid = row_scale(mid)
    low_mid = (mid * scale_mid * gain_mid).astype(BF16)

    def across(rows_in):
        return [rows_in] + [plane[2 * u](rows_in) for u in range(1, sharing)]

    def join(blocks):
        return jnp.concatenate(blocks)

    first, second = line[1](low_mid), line[2](low_mid)
    a_own = [across(low_mid)]
    grad_half = join(
        [
            at_line(grads[i // 2][u], i % 2)
            for i in range(LINES)
            for u in range(sharing)
        ]
    )
    w_got = next_weights()
    grad_other = to_core(grad_half)
    low_mid, first, second, w_got, grad_half, grad_other, *got = tie(
        low_mid, first, second, w_got, grad_half, grad_other, *a_own[0][1:]
    )
    w_near.append(w_got)
    a_own = [[low_mid] + got]

    third = line[1](second)
    a_own += [across(first), across(second)]
    a_near = join([v for block in a_own[:1] for v in block])
    other_near = to_core(a_near)
    a_near, other_near, third, *got = tie(
        a_near, other_near, third, *a_own[1], *a_own[2]
    )
    far = across(third)
    a_middle = join(got)
    other_middle = to_core(a_middle)
    a_near, other_near, a_middle, other_middle, *far = tie(
        a_near, other_near, a_middle, other_middle, *far
    )
    a_far = join(far)
    other_far = to_core(a_far)
    a_half = join([a_near, a_middle, a_far])
    a_half, other_far = tie(a_half, other_far)
    a_other = join([other_near, other_middle, other_far])

    ids = jnp.stack(
        [tz * columns + gc, tz * columns + (gc ^ 1), core * (TAIL // 2)]
    ).astype(jnp.int32)
    router_pad = jnp.pad(router_t, ((0, TAIL - experts), (0, 0)))
    w_experts = [[w_own], w_near]
    their_pair, their_mixed, their_back = expert_rows(
        ids, a_other, grad_other, w_experts, router_pad
    )
    their_back, a_half = tie(their_back, a_half)
    their_back = to_core(their_back)
    pair, mixed, back = expert_rows(ids, a_half, grad_half, w_experts, router_pad)
    back, their_back, pair, mixed, their_pair, their_mixed = tie(
        back, their_back, pair, mixed, their_pair, their_mixed
    )
    count = sharing * rows

    def summed(mine, theirs, i, u):
        at = i * count + u * rows
        return mine[at : at + rows].astype(F32) + theirs[at : at + rows].astype(F32)

    def to_share(mine, theirs, i):
        return [plane[2 * u](summed(mine, theirs, i, u).astype(BF16)) for u in range(1, sharing)]

    def shared(mine, theirs, i, got):
        return summed(mine, theirs, i, 0) + sum(v.astype(F32) for v in got)

    got = [to_share(back, their_back, i) for i in (3, 2)]
    own, near = expert_weight_grads(
        (pair, their_pair), (mixed, their_mixed), (a_half, a_other), (grad_half, grad_other)
    )
    back, their_back, own, near, mixed, their_mixed, *moved = tie(
        back, their_back, own, near, mixed, their_mixed, *got[0], *got[1]
    )
    line_blocks = {
        3: shared(back, their_back, 3, moved[: sharing - 1]),
        2: shared(back, their_back, 2, moved[sharing - 1 :]),
    }

    ends = [0] + [hidden * n // 8 for n in (6, 17, 24)]
    near = [near[a:b] for a, b in zip(ends[:-1], ends[1:])]
    third = line[1](line_blocks[3].astype(BF16))
    got = to_share(back, their_back, 1)
    near_got = [plane[1](near[0])]
    made, their_made = expert_outputs((mixed, their_mixed), w_experts)
    near_got[0], near[1], third, their_made, made, back, their_back, *moved = tie(
        near_got[0], near[1], third, their_made, made, back, their_back, *got
    )
    line_blocks[1] = shared(back, their_back, 1, moved)

    second = line[2]((line_blocks[2] + third.astype(F32)).astype(BF16))
    first = line[1](line_blocks[1].astype(BF16))
    their_made = to_core(their_made)
    got = to_share(back, their_back, 0)
    first, second, made, their_made, near[1], back, their_back, *got = tie(
        first, second, made, their_made, near[1], back, their_back, *got
    )
    line_blocks[0] = shared(back, their_back, 0, got)
    came_back = line_blocks[0] + first.astype(F32) + second.astype(F32)

    named = brought[:, 2 * width :]
    logits = jnp.where(named[:, :experts] > 0, dot_out(low_mid, router_t), NEGATIVE)
    gates_own = jax.nn.softmax(logits, axis=-1)
    expert_part = came_back[:, :width]
    gate_grad = sum(came_back[:, width + i * (TAIL // 4) :][:, :experts] for i in range(4))
    pick_grad = gates_own * (gate_grad - jnp.sum(gates_own * gate_grad, axis=-1, keepdims=True))
    logit_low = pick_grad.astype(BF16)
    router_part = dot_rows(logit_low, low_mid)
    normed_mid_grad = expert_part + dot(logit_low, router_t)
    mid_back, mid_gain_part = norm_back(normed_mid_grad, mid, scale_mid, gain_mid)
    mid_grad = mid_back + grad_out

    low_grad = mid_grad.astype(BF16)
    first, second = line[1](low_grad), line[2](low_grad)
    got = [to_share(made, their_made, i) for i in (2, 3)]
    near_got.append(plane[1](near[1]))
    low_grad, first, second, made, their_made, *moved = tie(
        low_grad, first, second, made, their_made, *got[0], *got[1]
    )
    out_blocks = {
        2: shared(made, their_made, 2, moved[: sharing - 1]),
        3: shared(made, their_made, 3, moved[sharing - 1 :]),
    }

    third = line[1](second)
    got = to_share(made, their_made, 1)
    near_rows = jnp.concatenate([low_grad, first, second])
    others = to_core(near_rows)
    third, near_rows, others, near_got[1], near[2], *moved = tie(
        third, near_rows, others, near_got[1], near[2], *got
    )
    out_blocks[1] = shared(made, their_made, 1, moved)

    other_third = to_core(third)
    out_low = [out_blocks[i].astype(BF16) for i in range(1, LINES)]
    third, other_third, made, their_made, *out_low = tie(
        third, other_third, made, their_made, *out_low
    )

    out_got = [line[i](out_low[i - 1]) for i in range(1, LINES)]
    out_last = to_share(made, their_made, 0)
    near_got.append(plane[1](near[2]))
    branch, qkv_low, gain_parts, in_gain_part, mine, theirs = attention_backward(
        scalars,
        (near_rows, third, others, other_third),
        w_slots,
        w_out,
        gain_q,
        gain_k,
        cosine,
        sine,
        pre,
        q,
        k,
        v,
        attended,
        inverse,
        row_parts,
    )
    branch, qkv_low, gain_parts, in_gain_part, mine, theirs, near_got[2], made, *out_got = tie(
        branch, qkv_low, gain_parts, in_gain_part, mine, theirs, near_got[2], made, *out_got, *out_last
    )
    out_got, out_last = out_got[: LINES - 1], out_got[LINES - 1 :]

    theirs = to_core(theirs)
    small_part = jnp.concatenate(
        [from_slots(in_gain_part[:1]), jnp.sum(mid_gain_part, axis=0)[None], router_part]
    )
    small_part = small_part.reshape(experts + 2, groups, piece).transpose(1, 0, 2)
    gain_parts = jnp.concatenate(
        [gain_parts[0].reshape(groups, part), gain_parts[1].reshape(groups, part)], axis=1
    )
    gain_parts = jnp.pad(gain_parts, ((0, 0), (0, piece - 2 * part)))[:, None]
    small_part = jnp.concatenate([small_part, gain_parts], axis=1)
    small_part = small_part.reshape(LINES, columns, experts + 3, piece)
    small_part = xor_order(xor_order(small_part, 0, tz), 1, gc)
    small_part = small_part + to_core(small_part)
    w_part = dot_rows(a1, qkv_low).astype(BF16).reshape(columns, LINES * piece, -1)
    near_got = jnp.concatenate(near_got)
    mine, theirs, w_part, small_part, near_got, attended, branch = tie(
        mine, theirs, w_part, small_part, near_got, attended, branch
    )

    def both(i):
        return at_line(mine, i).astype(F32) + at_line(theirs, i).astype(F32)

    def start_scatter(held, bit):
        leaving = sorted(s for s in held if s & bit)
        return plane[bit](jnp.stack([held[s].astype(BF16) for s in leaving]))

    def end_scatter(held, bit, got):
        leaving = sorted(s for s in held if s & bit)
        return {
            s: v.astype(F32) + got[leaving.index(s ^ bit)].astype(F32)
            for s, v in held.items()
            if not s & bit
        }

    def two_ways(blocks):
        middle = blocks.shape[2] // 2
        halves = blocks[..., :middle], blocks[..., middle:]
        return [(dict(enumerate(half)), bits) for half, bits in zip(halves, (axes[::-1], axes))]

    def start_ways(ways, n):
        return [start_scatter(held, bits[n]) for held, bits in ways]

    def end_ways(ways, n, got):
        return [(end_scatter(held, bits[n], v), bits) for (held, bits), v in zip(ways, got)]

    def rest_of_ways(ways):
        for n in range(1, len(axes)):
            ways = end_ways(ways, n, start_ways(ways, n))
        return [held[0] for held, _ in ways]

    first = line[1](both(1).astype(BF16))
    third = line[1](both(3).astype(BF16))
    w_ways = two_ways(w_part)
    w_got = start_ways(w_ways, 0)
    small_got = line[2](small_part[2:])
    out_parts = dot_rows(attended, branch).reshape(local_heads, head, width)
    expert_sum = over_replicas(own + near_got.astype(F32)).astype(BF16)
    mine, theirs, first, third, out_parts, expert_sum, small_got, small_part, *w_got = tie(
        mine, theirs, first, third, out_parts, expert_sum, small_got, small_part, *w_got
    )
    small_part = small_part[:2] + small_got
    w_ways = end_ways(w_ways, 0, w_got)

    second = line[2]((both(2) + third.astype(F32)).astype(BF16))
    w_parts = rest_of_ways(w_ways)
    expert_other = to_core(expert_sum)
    small_got = line[1](small_part[1])
    layer_out = mid + shared(made, their_made, 0, out_last) + sum(v.astype(F32) for v in out_got)
    layer_out = layer_out.astype(BF16)
    second, expert_other, expert_sum, layer_out, out_parts, small_part, small_got, *w_parts = tie(
        second, expert_other, expert_sum, layer_out, out_parts, small_part, small_got, *w_parts
    )
    small_part = small_part[0] + small_got

    w_part = over_replicas(jnp.concatenate(w_parts, axis=1))
    rel = xor_order(w_part.reshape(LINES, piece, -1), 0, tz)
    rel_low = rel.astype(BF16)
    rel_got = [line[i](rel_low[i]) for i in range(1, LINES)]
    if out_heads == 1:
        zeros = jnp.zeros_like(out_parts)
        out_parts = jnp.where(
            swapped, jnp.stack([zeros, out_parts], 1), jnp.stack([out_parts, zeros], 1)
        ).reshape(columns, head, width)
    out_ways = two_ways(out_parts)
    out_more = start_ways(out_ways, 0)
    normed_grad = from_slots(both(0) + first.astype(F32) + second.astype(F32))
    in_back, _ = norm_back(normed_grad, inputs, row_scale(inputs), gain_in)
    input_grad = (mid_grad + in_back).astype(BF16)
    leaving = jnp.concatenate([layer_out, input_grad], axis=1)
    rel_own, leaving, small_part, *moved = tie(rel[0], leaving, small_part, *rel_got, *out_more)
    rel_got, out_more = moved[: LINES - 1], moved[LINES - 1 :]
    out_ways = end_ways(out_ways, 0, out_more)

    going = send_home(leaving)
    for bit in axes[::-1]:
        small_part = small_part[:bit] + plane[bit](small_part[bit : 2 * bit])
    small_part = small_part[0]
    small_part = small_part + sum(move(small_part) for move in mv["replicas"])
    out_own = over_replicas(jnp.concatenate(rest_of_ways(out_ways), axis=1))
    own_cols = xor_order(jnp.stack([rel_own] + [v.astype(F32) for v in rel_got]), 0, tz)
    other_cols = to_core(own_cols)
    core_scalar = core.reshape(1).astype(jnp.int32)
    gate_total, up_total, down_total = join_expert_grads(core_scalar, expert_sum, expert_other)
    out_own, own_cols, other_cols, gate_total, up_total, down_total, small_part, *going = tie(
        out_own, own_cols, other_cols, gate_total, up_total, down_total, small_part, *going
    )

    out_other = to_core(out_own)
    out_total = whole(out_own, out_other, 0) if out_heads == 2 else out_own + out_other
    query_total, key_total, value_total = join_column_grads(core_scalar, own_cols, other_cols, head)
    arrived = at_home(going)

    return (
        arrived[..., :width],
        arrived[..., width:].astype(F32),
        small_part[0],
        query_total,
        key_total,
        value_total,
        small_part[experts + 2, :part],
        small_part[experts + 2, part : 2 * part],
        out_total,
        small_part[1],
        small_part[2 : experts + 2].T,
        gate_total[None],
        up_total[None],
        down_total[None],
    )


def solution(mesh):
    tokens = P("rep", None, "grp", None)
    rows = P("grp", None)
    vector = P("grp")
    stacked = P("grp", None, None)
    return jax.shard_map(
        per_device,
        mesh=mesh,
        in_specs=(
            tokens,
            tokens,
            tokens,
            vector,
            rows,
            rows,
            rows,
            vector,
            vector,
            rows,
            vector,
            rows,
            stacked,
            stacked,
            stacked,
        ),
        out_specs=(
            tokens,
            tokens,
            vector,
            rows,
            rows,
            rows,
            vector,
            vector,
            rows,
            vector,
            rows,
            stacked,
            stacked,
            stacked,
        ),
        check_vma=False,
    )
```

time: 1040 us -> 1040 us (level)
  waiting for transfers between devices: 470 us -> 309 us
  other arithmetic: 146 us -> 253 us
  local copies, waits for them, and re-layouts: 144 us -> 215 us
  matrix products: 180 us -> 155 us
    ppermute x82 -> x86, waiting for transfers between devices: 461 us -> 304 us  [mover(): lax.ppermute(v, AXES, table)]
    concatenate x9 -> x36, other arithmetic: 7.22 us -> 54 us  [the longest x1 8.86 us: expert_weight_grads(): own = jnp.concatenate([pair[:units], down[:hidden]])]
    concatenate x13 -> x9, local copies, waits for them, and re-layouts: 42.2 us -> 2.13 us  [the longest x1 0.83 us: per_device(): near_rows = jnp.concatenate([slotted, first, second])]
    slice x19 -> x17, local copies, waits for them, and re-layouts: 1.82 us -> 38.9 us  [flip_bit(): lax.slice_in_dim(values, i, i + bit, axis=axis)]
    slice x22 -> x45, local copies, waits for them, and re-layouts: 21.5 us -> 47.6 us  [the longest x2 8.15 us: expert_weight_grads(): own = jnp.concatenate([pair[:units], down[:hidden]])]
    convert_element_type x16 -> x29, other arithmetic: 56.1 us -> 79.6 us  [the longest x1 15.9 us: attention_forward(): x = x.astype(F32)]
    reduce_sum x3 -> x5, other arithmetic: 4.29 us -> 27.6 us  [row_scale(): return lax.rsqrt(jnp.mean(values * values, axis=-1, keepdims=True) + EPS)]
    dot_general x16 -> x21, matrix products: 80.4 us -> 60.6 us  [dot_out(): lax.dot_general(left, right, (((1,), (1,)), ((), ())), preferred_element_...]
  transfers between devices with their start and end apart: 86 -> 88, of which waited for: 42 -> 31; matrix products, arithmetic and copies ran while one was open for 28% -> 44% of each run, Pallas kernels for 0% -> 0%
where the time goes in v3:
time: 1040 us; the launch traced here: 1030 us
  waiting for transfers between devices  309 us (30%)
  other arithmetic  253 us (24%)
  local copies, waits for them, and re-layouts  215 us (21%)
  matrix products  155 us (15%)
  starting transfers between devices  91.8 us (9%)
    ppermute x86, waiting for transfers between devices, mover(): lax.ppermute(v, AXES, table)  304 us
    ppermute x86, starting transfers between devices, mover(): lax.ppermute(v, AXES, table)  89.9 us
    dot_general x21, matrix products, dot_out(): lax.dot_general(left, right, (((1,), (1,)), ((), ())), preferred_element_...  60.6 us
    unnamed x406, local copies, waits for them, and re-layouts  57.8 us
    dot_general x15, matrix products, dot_rows(): lax.dot_general(left, right, (((0,), (0,)), ((), ())), preferred_element_...  55.1 us
    dot_general x19, matrix products, dot(): lax.dot_general(left, right, (((1,), (0,)), ((), ())), preferred_element_...  39.3 us
    slice x17, local copies, waits for them, and re-layouts, flip_bit(): lax.slice_in_dim(values, i, i + bit, axis=axis)  38.9 us
    reduce_sum x5, other arithmetic, row_scale(): return lax.rsqrt(jnp.mean(values * values, axis=-1, keepdims=True) + EPS)  27.6 us
  transfers between devices with their start and end apart: 88, of which 31 were waited for; matrix products, arithmetic and copies ran while one was open for 44% of the time, Pallas kernels for 0%

profile of v3, /device:TPU:0, one launch (start us, length us, event | category | flops | bytes accessed | tf_op | source)
XLA Modules:
  0.0 1028.3 jit_solution(13724775498858853177)
XLA Ops:
  47.7 23.6 %collective-permute-done.7 = bf16[128,2048]{1,0:T(8,128)(2,1)S(1)} collective-permute-done((bf16[128,2048]{1,0:T(8,128)(2,1)S(1)}, bf16[128,2048]{1,0:T(8,128)(2,1)S(1)}, u32[]{:S(2)}, u32[]{:S(2)}) %collective-permute-start.7) | collective-permute-done | bytes 524320 | tf_op jit(solution)/shard_map/ppermute | solution.py:273
  84.2 16.9 %collective-permute-done.12 = bf16[2,128,2048]{2,1,0:T(8,128)(2,1)} collective-permute-done((bf16[2,128,2048]{2,1,0:T(8,128)(2,1)}, bf16[2,128,2048]{2,1,0:T(8,128)(2,1)}, u32[]{:S(2)}, u32[]{:S(2)}) %collective-permute-start.12) | collective-permute-done | bytes 1048608 | tf_op jit(solution)/shard_map/ppermute | solution.py:273
  139.3 13.3 %fusion.223 = (bf16[1024,4,1,128]{3,2,1,0:T(2,128)(2,1)S(1)}, bf16[1024,4,1,128]{3,2,1,0:T(2,128)(2,1)S(1)}, bf16[1024,4,1,128]{3,2,1,0:T(2,128)(2,1)S(1)}, bf16[1024,4,1,128]{3,2,1,0:T(2,128)(2,1)S(1)}) fusion(bf16[1024,4,4,128]{3,2,1,0:T(4,128)(2,1)} %reshape_reshape.3), kind=kLoop, calls=%fused_computation.617 | loop fusion | bytes 8388608 | tf_op jit(solution)/shard_map/slice | solution.py:43
  152.7 11.1 %maximum_select_fusion.2 = bf16[1024,4,4,128]{3,2,1,0:T(4,128)(2,1)S(1)} fusion(bf16[1024,4,4,128]{3,2,1,0:T(4,128)(2,1)S(1)} %copy-done, bf16[1024,4,1,128]{3,2,1,0:T(2,128)(2,1)S(1)} %get-tuple-element.579, bf16[1024,4,1,128]{3,2,1,0:T(2,128)(2,1)S(1)} %get-tuple-element.580, bf16[1024,4,1,128]{3,2,1,0:T(2,128)(2,1)S(1)} %get-tuple-element.581, ...), kind=kLoop, calls=%fused_computation.34 | loop fusion | flops 18874368 | bytes 12582913 | tf_op jit(solution)/shard_map/jit(_where)/select_n | solution.py:51
  166.8 24.4 %fusion = f32[1024]{0:T(1024)S(1)} fusion(bf16[1024,4,2,128]{3,2,1,0:T(2,128)(2,1)S(1)} %get-tuple-element.577, bf16[1024,4,2,128]{3,2,1,0:T(2,128)(2,1)S(1)} %get-tuple-element.576, pred[]{:T(512)S(6)} %ne.145, bf16[1024,4,4,128]{3,2,1,0:T(4,128)(2,1)S(1)} %copy-done, bf16[1024,4,1,128]{3,2,1,0:T(2,128)(2,1)S(1)} %get-tuple-element.579, ...), kind=kLoop, calls=%fused_computation.5 | loop fusion | flops 35650560 | bytes 12587010 | tf_op jit(solution)/shard_map/reduce_sum | solution.py:20
  191.2 15.9 %convert_bitcast_fusion = f32[1024,4,4,128]{3,1,2,0:T(4,128)} fusion(bf16[1024,4,2,128]{3,2,1,0:T(2,128)(2,1)S(1)} %get-tuple-element.577, bf16[1024,4,2,128]{3,2,1,0:T(2,128)(2,1)S(1)} %get-tuple-element.576, pred[]{:T(512)S(6)} %ne.145, bf16[1024,4,4,128]{3,2,1,0:T(4,128)(2,1)S(1)} %copy-done, bf16[1024,4,1,128]{3,2,1,0:T(2,128)(2,1)S(1)} %get-tuple-element.579, ...), kind=kLoop, calls=%fused_computation.1 | loop fusion | flops 31457280 | bytes 20971522 | tf_op jit(solution)/shard_map/convert_element_type | solution.py:104
  207.4 10.0 copy.176
  246.3 33.2 %collective-permute-done.15 = bf16[768,1152]{0,1:T(8,128)(2,1)S(1)} collective-permute-done((bf16[768,1152]{0,1:T(8,128)(2,1)S(1)}, bf16[768,1152]{0,1:T(8,128)(2,1)S(1)}, u32[]{:S(2)}, u32[]{:S(2)}) %collective-permute-start.15) | collective-permute-done | bytes 1769504 | tf_op jit(solution)/shard_map/ppermute | solution.py:273
  287.8 13.9 %collective-permute-done.22 = bf16[384,1152]{0,1:T(8,128)(2,1)S(1)} collective-permute-done((bf16[384,1152]{0,1:T(8,128)(2,1)S(1)}, bf16[384,1152]{0,1:T(8,128)(2,1)S(1)}, u32[]{:S(2)}, u32[]{:S(2)}) %collective-permute-start.22) | collective-permute-done | bytes 884768 | tf_op jit(solution)/shard_map/ppermute | solution.py:273
  316.2 19.1 %collective-permute-done.24 = bf16[128,2048]{1,0:T(8,128)(2,1)S(1)} collective-permute-done((bf16[128,2048]{1,0:T(8,128)(2,1)S(1)}, bf16[128,2048]{1,0:T(8,128)(2,1)S(1)}, u32[]{:S(2)}, u32[]{:S(2)}) %collective-permute-start.24) | collective-permute-done | bytes 524320 | tf_op jit(solution)/shard_map/ppermute | solution.py:273
  345.1 10.9 %collective-permute-done.31 = bf16[128,2048]{1,0:T(8,128)(2,1)S(1)} collective-permute-done((bf16[128,2048]{1,0:T(8,128)(2,1)S(1)}, bf16[128,2048]{1,0:T(8,128)(2,1)S(1)}, u32[]{:S(2)}, u32[]{:S(2)}) %collective-permute-start.31) | collective-permute-done | bytes 524320 | tf_op jit(solution)/shard_map/ppermute | solution.py:273
  356.0 13.0 %collective-permute-done.28 = bf16[128,2048]{1,0:T(8,128)(2,1)S(1)} collective-permute-done((bf16[128,2048]{1,0:T(8,128)(2,1)S(1)}, bf16[128,2048]{1,0:T(8,128)(2,1)S(1)}, u32[]{:S(2)}, u32[]{:S(2)}) %collective-permute-start.28) | collective-permute-done | bytes 524320 | tf_op jit(solution)/shard_map/ppermute | solution.py:273
  371.4 12.6 %collective-permute-done.34 = bf16[128,2048]{1,0:T(8,128)(2,1)S(1)} collective-permute-done((bf16[128,2048]{1,0:T(8,128)(2,1)S(1)}, bf16[128,2048]{1,0:T(8,128)(2,1)S(1)}, u32[]{:S(2)}, u32[]{:S(2)}) %collective-permute-start.34) | collective-permute-done | bytes 524320 | tf_op jit(solution)/shard_map/ppermute | solution.py:273
  384.1 10.8 %collective-permute-done.35 = bf16[128,2048]{1,0:T(8,128)(2,1)S(1)} collective-permute-done((bf16[128,2048]{1,0:T(8,128)(2,1)S(1)}, bf16[128,2048]{1,0:T(8,128)(2,1)S(1)}, u32[]{:S(2)}, u32[]{:S(2)}) %collective-permute-start.35) | collective-permute-done | bytes 524320 | tf_op jit(solution)/shard_map/ppermute | solution.py:273
  399.4 12.9 %collective-permute-done.37 = bf16[128,2048]{1,0:T(8,128)(2,1)S(1)} collective-permute-done((bf16[128,2048]{1,0:T(8,128)(2,1)S(1)}, bf16[128,2048]{1,0:T(8,128)(2,1)S(1)}, u32[]{:S(2)}, u32[]{:S(2)}) %collective-permute-start.37) | collective-permute-done | bytes 524320 | tf_op jit(solution)/shard_map/ppermute | solution.py:273
  485.9 9.1 fusion.3
  506.6 9.1 fusion.267
  515.7 12.8 %convolution_add_fusion = f32[1536,2048]{1,0:T(8,128)} fusion(f32[1536,2048]{1,0:T(8,128)} %fusion.267, bf16[1024,1536]{0,1:T(8,128)(2,1)S(1)} %pad_maximum_fusion.13, bf16[1024,2048]{1,0:T(8,128)(2,1)S(1)} %copy-done.54), kind=kOutput, calls=%fused_computation.4 | convolution fusion | flops 6445596672 | bytes 32505856 | tf_op jit(solution)/shard_map/dot_general | solution.py:38
  544.2 8.9 pad_maximum_fusion
  558.0 11.0 %collective-permute-done.40 = bf16[128,2176]{1,0:T(8,128)(2,1)} collective-permute-done((bf16[128,2176]{1,0:T(8,128)(2,1)}, bf16[128,2176]{1,0:T(8,128)(2,1)}, u32[]{:S(2)}, u32[]{:S(2)}) %collective-permute-start.40) | collective-permute-done | bytes 557088 | tf_op jit(solution)/shard_map/ppermute | solution.py:273
  592.1 9.2 collective-permute-done.42
  618.4 11.3 %collective-permute-done.45 = bf16[128,2176]{1,0:T(8,128)(2,1)S(1)} collective-permute-done((bf16[128,2176]{1,0:T(8,128)(2,1)S(1)}, bf16[128,2176]{1,0:T(8,128)(2,1)S(1)}, u32[]{:S(2)}, u32[]{:S(2)}) %collective-permute-start.45) | collective-permute-done | bytes 557088 | tf_op jit(solution)/shard_map/ppermute | solution.py:273
  645.4 18.9 %collective-permute-done.50 = bf16[128,2048]{1,0:T(8,128)(2,1)S(1)} collective-permute-done((bf16[128,2048]{1,0:T(8,128)(2,1)S(1)}, bf16[128,2048]{1,0:T(8,128)(2,1)S(1)}, u32[]{:S(2)}, u32[]{:S(2)}) %collective-permute-start.50) | collective-permute-done | bytes 524320 | tf_op jit(solution)/shard_map/ppermute | solution.py:273
  672.0 9.4 collective-permute-done.56
  681.4 10.5 %collective-permute-done.55 = bf16[528,2048]{1,0:T(8,128)(2,1)S(1)} collective-permute-done((bf16[528,2048]{1,0:T(8,128)(2,1)S(1)}, bf16[528,2048]{1,0:T(8,128)(2,1)S(1)}, u32[]{:S(2)}, u32[]{:S(2)}) %collective-permute-start.55) | collective-permute-done | bytes 2162720 | tf_op jit(solution)/shard_map/ppermute | solution.py:273
  735.0 10.8 %reshape.634 = f32[1024,4,4,128]{3,2,1,0:T(4,128)} reshape(f32[1024,2048]{1,0:T(8,128)} %fusion.121) | data formatting | bytes 16777216 | tf_op jit(solution)/shard_map/reshape | solution.py:79
  745.8 8.9 copy.219
  754.6 18.4 %fusion.219 = (f32[1024,4,1,128]{3,2,1,0:T(1,128)S(1)}, f32[1024,4,1,128]{3,2,1,0:T(1,128)S(1)}, f32[1024,4,1,128]{3,2,1,0:T(1,128)S(1)}, f32[1024,4,1,128]{3,2,1,0:T(1,128)S(1)}) fusion(f32[1024,4,4,128]{3,2,1,0:T(4,128)} %bitcast.354), kind=kLoop, calls=%fused_computation.613 | loop fusion | bytes 16777216 | tf_op jit(solution)/shard_map/slice | solution.py:43
  773.1 9.4 maximum_select_fusion
  785.9 14.1 %fusion.152 = bf16[1024,4,4,128]{3,2,1,0:T(4,128)(2,1)} fusion(f32[1024,4,2,128]{3,2,1,0:T(2,128)S(1)} %get-tuple-element.544, f32[1024,4,2,128]{3,2,1,0:T(2,128)S(1)} %get-tuple-element.543, pred[]{:T(512)S(6)} %ne.145, f32[1024,4,4,128]{3,2,1,0:T(4,128)S(1)} %bitcast.343, f32[1024,4,1,128]{3,2,1,0:T(1,128)S(1)} %get-tuple-element.546, ...), kind=kLoop, calls=%fused_computation.405 | loop fusion | flops 18874368 | bytes 29360130 | tf_op jit(solution)/shard_map/convert_element_type | solution.py:171
  800.0 18.2 %multiply_reduce_fusion = f32[4,4,128]{2,1,0:T(4,128)} fusion(bf16[1024,4,4,128]{3,2,1,0:T(4,128)(2,1)S(1)} %copy-done.1, f32[1024]{0:T(1024)S(1)} %bitcast.448, f32[1024,4,2,128]{3,2,1,0:T(2,128)S(1)} %get-tuple-element.544, f32[1024,4,2,128]{3,2,1,0:T(2,128)S(1)} %get-tuple-element.543, pred[]{:T(512)S(6)} %ne.145, f32[1024,4,4,128]{3,2,1,0:T(4,128)S(1)} %bitcast.343, ...), kind=kLoop, calls=%fused_computation.12 | loop fusion | flops 20969472 | bytes 29372418 | tf_op jit(solution)/shard_map/reduce_sum | solution.py:170
  922.2 11.4 %select_convert_fusion.1 = (f32[1152,2048]{1,0:T(8,128)}, f32[1152,2048]{1,0:T(8,128)}) fusion(bf16[1152,2048]{1,0:T(8,128)(2,1)} %add_convert_fusion, bf16[1152,2048]{1,0:T(8,128)(2,1)} %copy-done.47, pred[]{:T(512)S(6)} %eq.112), kind=kLoop, calls=%fused_computation.30 | loop fusion | flops 9437184 | bytes 28311552 | tf_op jit(solution)/shard_map/convert_element_type | solution.py:238
  (909 shorter events, 580.2 us)
Async XLA Ops:
  8.3 26.5 %collective-permute-start.4 = (bf16[144,768]{1,0:T(8,128)(2,1)}, bf16[144,768]{1,0:T(8,128)(2,1)}, u32[]{:S(2)}, u32[]{:S(2)}) collective-permute-start(bf16[144,768]{1,0:T(8,128)(2,1)} %get-tuple-element.721), channel_id=1, source_target_pairs={{0,24},{1,25},{2,26},{3,27},{4,28},{5,29},{6,30},{7,31},{8,16},{9,... | collective-permute-start | bytes 663560 | tf_op jit(solution)/shard_map/ppermute | solution.py:273
  38.4 33.9 %collective-permute-start.9 = (bf16[576,768]{1,0:T(8,128)(2,1)S(1)}, bf16[576,768]{1,0:T(8,128)(2,1)}, u32[]{:S(2)}, u32[]{:S(2)}) collective-permute-start(bf16[576,768]{1,0:T(8,128)(2,1)S(1)} %pad_maximum_fusion.33), channel_id=1, source_target_pairs={{0,4},{1,5},{2,6},{3,7},{4,0},{5,1},{6,2},{7,3},{8,12},{9,13},{10,... | collective-permute-start | bytes 2654216 | tf_op jit(solution)/shard_map/ppermute | solution.py:273
  38.5 33.9 %collective-permute-start.8 = (bf16[576,768]{1,0:T(8,128)(2,1)S(1)}, bf16[576,768]{1,0:T(8,128)(2,1)S(1)}, u32[]{:S(2)}, u32[]{:S(2)}) collective-permute-start(bf16[576,768]{1,0:T(8,128)(2,1)S(1)} %pad_maximum_fusion.33), channel_id=1, source_target_pairs={{0,2},{1,3},{2,0},{3,1},{4,6},{5,7},{6,4},{7,5},{8,10},{9,11},{10,... | collective-permute-start | bytes 2654216 | tf_op jit(solution)/shard_map/ppermute | solution.py:273
  40.8 31.5 %collective-permute-start.6 = (bf16[128,2048]{1,0:T(8,128)(2,1)S(1)}, bf16[128,2048]{1,0:T(8,128)(2,1)S(1)}, u32[]{:S(2)}, u32[]{:S(2)}) collective-permute-start(bf16[128,2048]{1,0:T(8,128)(2,1)S(1)} %slice.1388), channel_id=1, source_target_pairs={{0,16},{1,17},{2,18},{3,19},{4,20},{5,21},{6,22},{7,23},{8,24},{9,... | collective-permute-start | bytes 1572872 | tf_op jit(solution)/shard_map/ppermute | solution.py:273
  43.0 29.3 %collective-permute-start.5 = (bf16[128,2048]{1,0:T(8,128)(2,1)S(1)}, bf16[128,2048]{1,0:T(8,128)(2,1)S(1)}, u32[]{:S(2)}, u32[]{:S(2)}) collective-permute-start(bf16[128,2048]{1,0:T(8,128)(2,1)S(1)} %slice.1388), channel_id=1, source_target_pairs={{0,8},{1,9},{2,10},{3,11},{4,12},{5,13},{6,14},{7,15},{8,0},{9,1},... | collective-permute-start | bytes 1572872 | tf_op jit(solution)/shard_map/ppermute | solution.py:273
  75.2 27.4 %collective-permute-start.11 = (bf16[384,2048]{1,0:T(8,128)(2,1)}, bf16[384,2048]{1,0:T(8,128)(2,1)}, u32[]{:S(2)}, u32[]{:S(2)}) collective-permute-start(bf16[384,2048]{1,0:T(8,128)(2,1)} %constant_dynamic-update-slice_fusion), channel_id=1, source_target_pairs={{0,1},{1,0},{2,3},{3,2},{4,5},{5,4},{6,7},{7,6},{8,9},{9,8},{10,11... | collective-permute-start | bytes 4718600 | tf_op jit(solution)/shard_map/ppermute | solution.py:273
  121.8 124.4 %collective-permute-start.18 = (bf16[128,2176]{0,1:T(8,128)(2,1)}, bf16[128,2176]{0,1:T(8,128)(2,1)}, u32[]{:S(2)}, u32[]{:S(2)}) collective-permute-start(bf16[128,2176]{0,1:T(8,128)(2,1)} %slice.1438), channel_id=1, source_target_pairs={{0,24},{1,25},{2,26},{3,27},{4,28},{5,29},{6,30},{7,31},{8,16},{9,... | collective-permute-start | bytes 1671176 | tf_op jit(solution)/shard_map/ppermute | solution.py:273
  125.4 120.9 %collective-permute-start.17 = (bf16[128,2176]{0,1:T(8,128)(2,1)}, bf16[128,2176]{0,1:T(8,128)(2,1)}, u32[]{:S(2)}, u32[]{:S(2)}) collective-permute-start(bf16[128,2176]{0,1:T(8,128)(2,1)} %slice.1438), channel_id=1, source_target_pairs={{0,16},{1,17},{2,18},{3,19},{4,20},{5,21},{6,22},{7,23},{8,24},{9,... | collective-permute-start | bytes 1671176 | tf_op jit(solution)/shard_map/ppermute | solution.py:273
  125.4 120.9 %collective-permute-start.16 = (bf16[128,2176]{0,1:T(8,128)(2,1)}, bf16[128,2176]{0,1:T(8,128)(2,1)}, u32[]{:S(2)}, u32[]{:S(2)}) collective-permute-start(bf16[128,2176]{0,1:T(8,128)(2,1)} %slice.1438), channel_id=1, source_target_pairs={{0,8},{1,9},{2,10},{3,11},{4,12},{5,13},{6,14},{7,15},{8,0},{9,1},... | collective-permute-start | bytes 1671176 | tf_op jit(solution)/shard_map/ppermute | solution.py:273
  239.2 40.2 %collective-permute-start.15 = (bf16[768,1152]{0,1:T(8,128)(2,1)S(1)}, bf16[768,1152]{0,1:T(8,128)(2,1)S(1)}, u32[]{:S(2)}, u32[]{:S(2)}) collective-permute-start(bf16[768,1152]{0,1:T(8,128)(2,1)S(1)} %slice.1191), channel_id=1, source_target_pairs={{0,2},{1,3},{2,0},{3,1},{4,6},{5,7},{6,4},{7,5},{8,10},{9,11},{10,... | collective-permute-start | bytes 5308424 | tf_op jit(solution)/shard_map/ppermute | solution.py:273
  283.9 26.3 %collective-permute-start.23 = (bf16[256,2176]{0,1:T(8,128)(2,1)S(1)}, bf16[256,2176]{0,1:T(8,128)(2,1)S(1)}, u32[]{:S(2)}, u32[]{:S(2)}) collective-permute-start(bf16[256,2176]{0,1:T(8,128)(2,1)S(1)} %pad_maximum_fusion.23), channel_id=1, source_target_pairs={{0,4},{1,5},{2,6},{3,7},{4,0},{5,1},{6,2},{7,3},{8,12},{9,13},{10,... | collective-permute-start | bytes 3342344 | tf_op jit(solution)/shard_map/ppermute | solution.py:273
  338.8 30.3 %collective-permute-start.30 = (bf16[1024,2176]{0,1:T(8,128)(2,1)S(1)}, bf16[1024,2176]{0,1:T(8,128)(2,1)S(1)}, u32[]{:S(2)}, u32[]{:S(2)}) collective-permute-start(bf16[1024,2176]{0,1:T(8,128)(2,1)S(1)} %slice_dynamic-update-slice_fusion), channel_id=1, source_target_pairs={{0,1},{1,0},{2,3},{3,2},{4,5},{5,4},{6,7},{7,6},{8,9},{9,8},{10,11... | collective-permute-start | bytes 13369352 | tf_op jit(solution)/shard_map/ppermute | solution.py:273
  339.0 30.1 %collective-permute-start.29 = (bf16[512,1152]{0,1:T(8,128)(2,1)S(1)}, bf16[512,1152]{0,1:T(8,128)(2,1)S(1)}, u32[]{:S(2)}, u32[]{:S(2)}) collective-permute-start(bf16[512,1152]{0,1:T(8,128)(2,1)S(1)} %slice.1199), channel_id=1, source_target_pairs={{0,2},{1,3},{2,0},{3,1},{4,6},{5,7},{6,4},{7,5},{8,10},{9,11},{10,... | collective-permute-start | bytes 3538952 | tf_op jit(solution)/shard_map/ppermute | solution.py:273
  574.7 26.6 %collective-permute-start.42 = (bf16[288,2048]{1,0:T(8,128)(2,1)S(1)}, bf16[288,2048]{1,0:T(8,128)(2,1)}, u32[]{:S(2)}, u32[]{:S(2)}) collective-permute-start(bf16[288,2048]{1,0:T(8,128)(2,1)S(1)} %slice.1232), channel_id=1, source_target_pairs={{0,2},{1,3},{2,0},{3,1},{4,6},{5,7},{6,4},{7,5},{8,10},{9,11},{10,... | collective-permute-start | bytes 3538952 | tf_op jit(solution)/shard_map/ppermute | solution.py:273
  601.3 33.8 %collective-permute-start.47 = (bf16[1024,2048]{1,0:T(8,128)(2,1)}, bf16[1024,2048]{1,0:T(8,128)(2,1)S(1)}, u32[]{:S(2)}, u32[]{:S(2)}) collective-permute-start(bf16[1024,2048]{1,0:T(8,128)(2,1)} %add_convert_fusion.2), channel_id=1, source_target_pairs={{0,1},{1,0},{2,3},{3,2},{4,5},{5,4},{6,7},{7,6},{8,9},{9,8},{10,11... | collective-permute-start | bytes 12582920 | tf_op jit(solution)/shard_map/ppermute | solution.py:273
  607.8 27.4 %collective-permute-start.46 = (bf16[128,2176]{1,0:T(8,128)(2,1)S(1)}, bf16[128,2176]{1,0:T(8,128)(2,1)S(1)}, u32[]{:S(2)}, u32[]{:S(2)}) collective-permute-start(bf16[128,2176]{1,0:T(8,128)(2,1)S(1)} %add_convert_fusion.6), channel_id=1, source_target_pairs={{0,16},{1,17},{2,18},{3,19},{4,20},{5,21},{6,22},{7,23},{8,24},{9,... | collective-permute-start | bytes 1671176 | tf_op jit(solution)/shard_map/ppermute | solution.py:273
  645.0 46.9 %collective-permute-start.55 = (bf16[528,2048]{1,0:T(8,128)(2,1)S(1)}, bf16[528,2048]{1,0:T(8,128)(2,1)S(1)}, u32[]{:S(2)}, u32[]{:S(2)}) collective-permute-start(bf16[528,2048]{1,0:T(8,128)(2,1)S(1)} %copy-done.71), channel_id=1, source_target_pairs={{0,2},{1,3},{2,0},{3,1},{4,6},{5,7},{6,4},{7,5},{8,10},{9,11},{10,... | collective-permute-start | bytes 6488072 | tf_op jit(solution)/shard_map/ppermute | solution.py:273
  691.9 139.1 %collective-permute-start.58 = (bf16[336,2048]{1,0:T(8,128)(2,1)S(1)}, bf16[336,2048]{1,0:T(8,128)(2,1)S(1)}, u32[]{:S(2)}, u32[]{:S(2)}) collective-permute-start(bf16[336,2048]{1,0:T(8,128)(2,1)S(1)} %slice.1261), channel_id=1, source_target_pairs={{0,2},{1,3},{2,0},{3,1},{4,6},{5,7},{6,4},{7,5},{8,10},{9,11},{10,... | collective-permute-start | bytes 4128776 | tf_op jit(solution)/shard_map/ppermute | solution.py:273
  710.4 120.6 %collective-permute-start.62 = (bf16[128,2048]{1,0:T(8,128)(2,1)}, bf16[128,2048]{1,0:T(8,128)(2,1)}, u32[]{:S(2)}, u32[]{:S(2)}) collective-permute-start(bf16[128,2048]{1,0:T(8,128)(2,1)} %add_convert_fusion.16), channel_id=1, source_target_pairs={{0,4},{1,5},{2,6},{3,7},{4,0},{5,1},{6,2},{7,3},{8,12},{9,13},{10,... | collective-permute-start | bytes 1572872 | tf_op jit(solution)/shard_map/ppermute | solution.py:273
  711.2 119.7 %collective-permute-start.59 = (bf16[128,2048]{1,0:T(8,128)(2,1)}, bf16[128,2048]{1,0:T(8,128)(2,1)}, u32[]{:S(2)}, u32[]{:S(2)}) collective-permute-start(bf16[128,2048]{1,0:T(8,128)(2,1)} %get-tuple-element.330), channel_id=1, source_target_pairs={{0,8},{1,9},{2,10},{3,11},{4,12},{5,13},{6,14},{7,15},{8,0},{9,1},... | collective-permute-start | bytes 1572872 | tf_op jit(solution)/shard_map/ppermute | solution.py:273
  711.5 119.5 %collective-permute-start.60 = (bf16[128,2048]{1,0:T(8,128)(2,1)}, bf16[128,2048]{1,0:T(8,128)(2,1)}, u32[]{:S(2)}, u32[]{:S(2)}) collective-permute-start(bf16[128,2048]{1,0:T(8,128)(2,1)} %get-tuple-element.331), channel_id=1, source_target_pairs={{0,16},{1,17},{2,18},{3,19},{4,20},{5,21},{6,22},{7,23},{8,24},{9,... | collective-permute-start | bytes 1572872 | tf_op jit(solution)/shard_map/ppermute | solution.py:273
  712.9 118.1 %collective-permute-start.61 = (bf16[128,2048]{1,0:T(8,128)(2,1)}, bf16[128,2048]{1,0:T(8,128)(2,1)}, u32[]{:S(2)}, u32[]{:S(2)}) collective-permute-start(bf16[128,2048]{1,0:T(8,128)(2,1)} %get-tuple-element.332), channel_id=1, source_target_pairs={{0,24},{1,25},{2,26},{3,27},{4,28},{5,29},{6,30},{7,31},{8,16},{9,... | collective-permute-start | bytes 1572872 | tf_op jit(solution)/shard_map/ppermute | solution.py:273
  845.5 28.1 %collective-permute-start.69 = (bf16[2,512,384]{2,1,0:T(8,128)(2,1)}, bf16[2,512,384]{2,1,0:T(8,128)(2,1)}, u32[]{:S(2)}, u32[]{:S(2)}) collective-permute-start(bf16[2,512,384]{2,1,0:T(8,128)(2,1)} %pad_maximum_fusion.34), channel_id=1, source_target_pairs={{0,2},{1,3},{2,0},{3,1},{4,6},{5,7},{6,4},{7,5},{8,10},{9,11},{10,... | collective-permute-start | bytes 2359304 | tf_op jit(solution)/shard_map/ppermute | solution.py:273
  847.1 26.5 %collective-permute-start.68 = (bf16[2,512,384]{2,1,0:T(8,128)(2,1)}, bf16[2,512,384]{2,1,0:T(8,128)(2,1)}, u32[]{:S(2)}, u32[]{:S(2)}) collective-permute-start(bf16[2,512,384]{2,1,0:T(8,128)(2,1)} %stack.173), channel_id=1, source_target_pairs={{0,4},{1,5},{2,6},{3,7},{4,0},{5,1},{6,2},{7,3},{8,12},{9,13},{10,... | collective-permute-start | bytes 2359304 | tf_op jit(solution)/shard_map/ppermute | solution.py:273
  873.6 33.4 %collective-permute-start.71 = (bf16[1152,2048]{1,0:T(8,128)(2,1)S(1)}, bf16[1152,2048]{1,0:T(8,128)(2,1)S(1)}, u32[]{:S(2)}, u32[]{:S(2)}) collective-permute-start(bf16[1152,2048]{1,0:T(8,128)(2,1)S(1)} %copy-done.23), channel_id=1, source_target_pairs={{0,1},{1,0},{2,3},{3,2},{4,5},{5,4},{6,7},{7,6},{8,9},{9,8},{10,11... | collective-permute-start | bytes 14155784 | tf_op jit(solution)/shard_map/ppermute | solution.py:273
  880.2 26.8 %collective-permute-start.70 = (bf16[128,2048]{1,0:T(8,128)(2,1)S(1)}, bf16[128,2048]{1,0:T(8,128)(2,1)S(1)}, u32[]{:S(2)}, u32[]{:S(2)}) collective-permute-start(bf16[128,2048]{1,0:T(8,128)(2,1)S(1)} %add_convert_fusion.13), channel_id=1, source_target_pairs={{0,16},{1,17},{2,18},{3,19},{4,20},{5,21},{6,22},{7,23},{8,24},{9,... | collective-permute-start | bytes 1572872 | tf_op jit(solution)/shard_map/ppermute | solution.py:273
  914.9 45.1 %collective-permute-start.77 = (bf16[128,768]{1,0:T(8,128)(2,1)}, bf16[128,768]{1,0:T(8,128)(2,1)}, u32[]{:S(2)}, u32[]{:S(2)}) collective-permute-start(bf16[128,768]{1,0:T(8,128)(2,1)} %get-tuple-element.666), channel_id=1, source_target_pairs={{0,24},{1,25},{2,26},{3,27},{4,28},{5,29},{6,30},{7,31},{8,16},{9,... | collective-permute-start | bytes 589832 | tf_op jit(solution)/shard_map/ppermute | solution.py:273
  916.8 43.2 %collective-permute-start.76 = (bf16[128,768]{1,0:T(8,128)(2,1)}, bf16[128,768]{1,0:T(8,128)(2,1)}, u32[]{:S(2)}, u32[]{:S(2)}) collective-permute-start(bf16[128,768]{1,0:T(8,128)(2,1)} %get-tuple-element.667), channel_id=1, source_target_pairs={{0,16},{1,17},{2,18},{3,19},{4,20},{5,21},{6,22},{7,23},{8,24},{9,... | collective-permute-start | bytes 589832 | tf_op jit(solution)/shard_map/ppermute | solution.py:273
  916.8 43.2 %collective-permute-start.75 = (bf16[128,768]{1,0:T(8,128)(2,1)}, bf16[128,768]{1,0:T(8,128)(2,1)}, u32[]{:S(2)}, u32[]{:S(2)}) collective-permute-start(bf16[128,768]{1,0:T(8,128)(2,1)} %get-tuple-element.668), channel_id=1, source_target_pairs={{0,8},{1,9},{2,10},{3,11},{4,12},{5,13},{6,14},{7,15},{8,0},{9,1},... | collective-permute-start | bytes 589832 | tf_op jit(solution)/shard_map/ppermute | solution.py:273
  920.2 39.8 %collective-permute-start.79 = (bf16[2,128,1024]{2,1,0:T(8,128)(2,1)}, bf16[2,128,1024]{2,1,0:T(8,128)(2,1)}, u32[]{:S(2)}, u32[]{:S(2)}) collective-permute-start(bf16[2,128,1024]{2,1,0:T(8,128)(2,1)} %pad_maximum_fusion.39), channel_id=1, source_target_pairs={{0,2},{1,3},{2,0},{3,1},{4,6},{5,7},{6,4},{7,5},{8,10},{9,11},{10,... | collective-permute-start | bytes 1572872 | tf_op jit(solution)/shard_map/ppermute | solution.py:273
  921.4 38.7 %collective-permute-start.78 = (bf16[2,128,1024]{2,1,0:T(8,128)(2,1)}, bf16[2,128,1024]{2,1,0:T(8,128)(2,1)}, u32[]{:S(2)}, u32[]{:S(2)}) collective-permute-start(bf16[2,128,1024]{2,1,0:T(8,128)(2,1)} %slice.1513), channel_id=1, source_target_pairs={{0,4},{1,5},{2,6},{3,7},{4,0},{5,1},{6,2},{7,3},{8,12},{9,13},{10,... | collective-permute-start | bytes 1572872 | tf_op jit(solution)/shard_map/ppermute | solution.py:273
  988.6 36.1 %collective-permute-start.87 = (f32[128,2048]{1,0:T(8,128)S(1)}, f32[128,2048]{1,0:T(8,128)}, u32[]{:S(2)}, u32[]{:S(2)}) collective-permute-start(f32[128,2048]{1,0:T(8,128)S(1)} %pad_maximum_fusion.31), channel_id=1, source_target_pairs={{0,1},{1,0},{2,3},{3,2},{4,5},{5,4},{6,7},{7,6},{8,9},{9,8},{10,11... | collective-permute-start | bytes 3145736 | tf_op jit(solution)/shard_map/ppermute | solution.py:273
  (246 other events, 3275.8 us)
